TPU v7x, 256 devices: a whole 4x4x8 slice. The times are simulated.
256 devices in a mesh: replica: 32 (over x, z_hi, y), tensor: 8 (over z_lo, core).
Axes of the slice: x: 4, y: 4, z: 8 (z_hi: 2, z_lo: 4; z = z_hi * 4 + z_lo), core: 2. Of those that a mesh axis runs over, the one named last changes fastest.
Arguments:
- lengths: int32 [512], replicated, may hold values from 1 to 254, as said below
- page_table: int32 [512, 2], P('replica'), may hold values from 0 to 31, as said below
- key_pool: bfloat16 [1024, 128, 1024], P('replica', None, 'tensor'), may hold values from -4 to 4
- value_pool: bfloat16 [1024, 128, 1024], P('replica', None, 'tensor'), may hold values from -5 to 5
- queries: bfloat16 [2, 512, 4096], P(None, 'replica', 'tensor'), may hold values from -80 to 80
- new_keys: bfloat16 [2, 512, 1024], P(None, 'replica', 'tensor'), may hold values from -4 to 4
- new_values: bfloat16 [2, 512, 1024], P(None, 'replica', 'tensor'), may hold values from -5 to 5
- conv_state: float32 [512, 3, 8192], P('replica', None, 'tensor'), may hold values from -5 to 5
- ssm_state: float32 [512, 16, 8192], P('replica', None, 'tensor'), may hold values from -5 to 5
- mamba_x: bfloat16 [2, 512, 8192], P(None, 'replica', 'tensor'), may hold values from -5 to 5
- mamba_z: bfloat16 [2, 512, 8192], P(None, 'replica', 'tensor'), may hold values from -5 to 5
- conv_weight: float32 [4, 8192], P(None, 'tensor'), may hold values from -3 to 3
- conv_bias: float32 [8192], P('tensor'), may hold values from -3 to 3
- dt_down: bfloat16 [8192, 256], P('tensor'), may hold values from -0.0625 to 0.0625
- bc_proj: bfloat16 [8192, 32], P('tensor'), may hold values from -0.0625 to 0.0625
- dt_up: bfloat16 [256, 8192], P(None, 'tensor'), may hold values from -0.375 to 0.375
- dt_bias: float32 [8192], P('tensor'), may hold values from -3 to 0
- a_log: float32 [16, 8192], P(None, 'tensor'), may hold values from 0 to 2.77
- skip_d: float32 [8192], P('tensor'), may hold values from 0.5 to 2
- moves: int32 [256, 2], replicated, may hold values from 0 to 511, as said below
Outputs:
- attention: bfloat16 [2, 512, 4096], P(None, 'replica', 'tensor')
- mamba_out: bfloat16 [2, 512, 8192], P(None, 'replica', 'tensor')
- final_ssm: float32 [512, 16, 8192], P('replica', None, 'tensor')
- final_conv: float32 [512, 3, 8192], P('replica', None, 'tensor')
Inputs may be any that keep to these rules, and one draw needn't show every extreme that they name: `lengths`: each replica has one request of the longest length. `page_table`: the rows of the 16 requests of one replica name each of that replica's 32 pages once. `moves`: rows r * 8 to r * 8 + 7 are the 8 requests that leave replica r, each to another replica, no two to the same one; every replica receives 8 requests, from 8 different replicas, into exactly the slots that its own leaving requests free; the j-th row of every replica goes the same number of replicas further along, counted modulo the number of replicas; one of these numbers is 1 and another is half the number of replicas.
All inputs are finite; a program needn't handle non-finite values.
Results may differ from a plain program's by a relative error of at most 0.013.
Values may be sent and summed in bfloat16 or wider, within the bound.
No kernel may reach another device: no remote copies, remote signals or barrier semaphores. Data moves between devices by JAX's collectives and lax.ppermute only.
A program may use at most 64 MiB of HBM per device.

v0:
```python
import math

import jax
import jax.numpy as jnp
from jax import lax
from jax.sharding import PartitionSpec as P

HD = 128


def attend(query_rows, key_rows, value_rows, last_pos):
    rows_count = query_rows.shape[0]
    key_span = key_rows.shape[1]
    kv_heads = key_rows.shape[2] // HD
    group_size = query_rows.shape[1] // key_rows.shape[2]
    query_heads = query_rows.reshape(rows_count, kv_heads, group_size, HD)
    key_heads = key_rows.reshape(rows_count, key_span, kv_heads, HD)
    value_heads = value_rows.reshape(rows_count, key_span, kv_heads, HD)
    scores = jnp.einsum(
        "skgd,spkd->skgp", query_heads, key_heads, preferred_element_type=jnp.float32
    ) * (1.0 / math.sqrt(HD))
    visible = jnp.arange(key_span)[None, :] <= last_pos[:, None]
    scores = jnp.where(visible[:, None, None, :], scores, -1e30)
    largest = jnp.max(scores, axis=-1, keepdims=True)
    exponent = jnp.exp(scores - largest)
    weights = (exponent / jnp.sum(exponent, axis=-1, keepdims=True)).astype(jnp.bfloat16)
    attended = jnp.einsum(
        "skgp,spkd->skgd", weights, value_heads, preferred_element_type=jnp.float32
    )
    return attended.astype(jnp.bfloat16).reshape(rows_count, query_rows.shape[1])


def mamba_step(conv_prev, state_prev, x_in, z_in, params):
    conv_weight, conv_bias, dt_down, bc_proj, dt_up, dt_bias, a_log, skip_d = params
    window = jnp.concatenate([conv_prev, x_in.astype(jnp.float32)[:, None, :]], axis=1)
    conv_out = jax.nn.silu(jnp.sum(window * conv_weight[None], axis=1) + conv_bias)
    mixed_in = conv_out.astype(jnp.bfloat16)
    low_rank, bc_terms = lax.psum(
        (
            jnp.dot(mixed_in, dt_down, preferred_element_type=jnp.float32),
            jnp.dot(mixed_in, bc_proj, preferred_element_type=jnp.float32),
        ),
        "tensor",
    )
    dt_step = jax.nn.softplus(
        jnp.dot(low_rank.astype(jnp.bfloat16), dt_up, preferred_element_type=jnp.float32) + dt_bias
    )
    state_count = a_log.shape[0]
    b_in = bc_terms[:, :state_count]
    c_out = bc_terms[:, state_count:]
    inputs_wide = mixed_in.astype(jnp.float32)
    decay_rate = jnp.exp(-dt_step[:, None, :] * jnp.exp(a_log)[None])
    state_new = (
        decay_rate * state_prev + dt_step[:, None, :] * b_in[:, :, None] * inputs_wide[:, None, :]
    )
    output = (jnp.sum(c_out[:, :, None] * state_new, axis=1) + skip_d * inputs_wide) * jax.nn.silu(
        z_in.astype(jnp.float32)
    )
    return (output.astype(jnp.bfloat16), window[:, 1:], state_new)


def keep_where(flags, moved, staying):
    return jnp.where(flags.reshape((flags.shape[0],) + (1,) * (staying.ndim - 1)), moved, staying)


def shards(
    lengths,
    page_table,
    key_pool,
    value_pool,
    queries,
    new_keys,
    new_values,
    conv_state,
    ssm_state,
    mamba_x,
    mamba_z,
    conv_weight,
    conv_bias,
    dt_down,
    bc_proj,
    dt_up,
    dt_bias,
    a_log,
    skip_d,
    moves,
):
    params = (conv_weight, conv_bias, dt_down, bc_proj, dt_up, dt_bias, a_log, skip_d)
    replica = lax.axis_index("replica")
    replicas = lax.axis_size("replica")
    slot_count = page_table.shape[0]
    span_total = page_table.shape[1] * key_pool.shape[1]
    leaving_count = moves.shape[0] // replicas
    slot_ids = jnp.arange(slot_count, dtype=jnp.int32)
    own_slots = replica * slot_count + slot_ids
    own_lengths = lax.dynamic_slice_in_dim(lengths, replica * slot_count, slot_count)
    key_cache = (
        key_pool[page_table]
        .reshape(slot_count, span_total, key_pool.shape[2])
        .at[slot_ids, own_lengths]
        .set(new_keys[0])
    )
    value_cache = (
        value_pool[page_table]
        .reshape(slot_count, span_total, value_pool.shape[2])
        .at[slot_ids, own_lengths]
        .set(new_values[0])
    )
    attention_one = attend(queries[0], key_cache, value_cache, own_lengths)
    mamba_one, conv_one, state_one = mamba_step(
        conv_state, ssm_state, mamba_x[0], mamba_z[0], params
    )
    outgoing = lax.dynamic_slice_in_dim(moves, replica * leaving_count, leaving_count, 0)
    leave_slot = outgoing[:, 0] - replica * slot_count
    leave_dest = outgoing[:, 1] // slot_count
    matches = moves[None, :, 1] == own_slots[:, None]
    arrived = jnp.any(matches, axis=1)
    source_slot = jnp.where(
        arrived, jnp.sum(jnp.where(matches, moves[None, :, 0], 0), axis=1), own_slots
    )
    source_rep = source_slot // slot_count
    later_lengths = lengths[source_slot]

    def pack_moving(local_rows):
        empty = jnp.zeros((replicas,) + local_rows.shape[1:], local_rows.dtype)
        return empty.at[leave_dest].set(local_rows[leave_slot])

    def take_arrived(received, local_rows):
        return keep_where(arrived, received[source_rep], local_rows)

    conv_got, state_got = (
        lax.all_to_all(pack_moving(conv_one), "replica", split_axis=0, concat_axis=0, tiled=True),
        lax.all_to_all(pack_moving(state_one), "replica", split_axis=0, concat_axis=0, tiled=True),
    )
    conv_next = take_arrived(conv_got, conv_one)
    state_next = take_arrived(state_got, state_one)
    mamba_two, final_conv, final_ssm = mamba_step(
        conv_next, state_next, mamba_x[1], mamba_z[1], params
    )
    keys_got, values_got = (
        lax.all_to_all(pack_moving(key_cache), "replica", split_axis=0, concat_axis=0, tiled=True),
        lax.all_to_all(
            pack_moving(value_cache), "replica", split_axis=0, concat_axis=0, tiled=True
        ),
    )
    moved_keys_all = take_arrived(keys_got, key_cache)
    moved_values_all = take_arrived(values_got, value_cache)
    later_keys = moved_keys_all.at[slot_ids, later_lengths + 1].set(new_keys[1])
    later_values = moved_values_all.at[slot_ids, later_lengths + 1].set(new_values[1])
    attention_two = attend(queries[1], later_keys, later_values, later_lengths + 1)
    return (
        jnp.stack([attention_one, attention_two]),
        jnp.stack([mamba_one, mamba_two]),
        final_ssm,
        final_conv,
    )


def solution(mesh):
    in_specs = (
        P(),
        P("replica", None),
        P("replica", None, "tensor"),
        P("replica", None, "tensor"),
        P(None, "replica", "tensor"),
        P(None, "replica", "tensor"),
        P(None, "replica", "tensor"),
        P("replica", None, "tensor"),
        P("replica", None, "tensor"),
        P(None, "replica", "tensor"),
        P(None, "replica", "tensor"),
        P(None, "tensor"),
        P("tensor"),
        P("tensor", None),
        P("tensor", None),
        P(None, "tensor"),
        P("tensor"),
        P(None, "tensor"),
        P("tensor"),
        P(),
    )
    out_specs = (
        P(None, "replica", "tensor"),
        P(None, "replica", "tensor"),
        P("replica", None, "tensor"),
        P("replica", None, "tensor"),
    )
    return jax.shard_map(shards, mesh=mesh, in_specs=in_specs, out_specs=out_specs, check_vma=False)
```

profile of v0, /device:TPU:8, one launch (start us, length us, event | category | flops | bytes accessed | tf_op | source)
XLA Modules:
  0.0 247.5 jit_solution(321677015727897227)
XLA Ops:
  0.7 0.8 constant_dynamic-slice_fusion
  1.5 1.4 fusion.45
  3.0 1.1 copy.32
  4.2 0.6 gather_fusion.7
  4.9 0.9 broadcast_in_dim.74
  5.8 2.1 scatter_fusion.6
  7.9 14.2 %all-to-all-start.2 = ((f32[32,3,1024]{2,1,0:T(4,128)}), f32[32,3,1024]{2,1,0:T(4,128)S(1)}, u32[]{:S(2)}, u32[]{:S(2)}) async-start(f32[32,3,1024]{2,1,0:T(4,128)} %scatter_fusion.6), calls=%async_computation.2 | async-start | bytes 1048576 | tf_op jit(solution)/shard_map/all_to_all | solution.py:132
  22.2 0.7 gather_fusion
  23.0 0.6 fusion.41
  24.2 1.3 scatter_fusion
  25.6 0.6 gather_fusion.3
  26.2 1.8 broadcast.412.clone
  28.0 2.5 scatter_fusion.2
  30.5 7.5 %all-to-all-done.2 = f32[32,3,1024]{2,1,0:T(4,128)S(1)} async-done(((f32[32,3,1024]{2,1,0:T(4,128)}), f32[32,3,1024]{2,1,0:T(4,128)S(1)}, u32[]{:S(2)}, u32[]{:S(2)}) %all-to-all-start.2) | async-done | bytes 393248 | tf_op jit(solution)/shard_map/all_to_all | solution.py:132
  38.0 0.8 copy-done.6
  38.8 5.4 %all-to-all-start = ((bf16[32,256,128]{2,1,0:T(8,128)(2,1)}), bf16[32,256,128]{2,1,0:T(8,128)(2,1)}, u32[]{:S(2)}, u32[]{:S(2)}) async-start(bf16[32,256,128]{2,1,0:T(8,128)(2,1)} %scatter_fusion.2), calls=%async_computation | async-start | bytes 4194304 | tf_op jit(solution)/shard_map/all_to_all | solution.py:141
  44.2 2.0 gather_fusion.1
  46.8 1.3 scatter_fusion.1
  48.1 1.4 gather_fusion.5
  49.6 1.8 broadcast.412.clone.1
  51.3 2.7 %scatter_fusion.4 = bf16[32,256,128]{2,1,0:T(8,128)(2,1)} fusion(bf16[32,256,128]{2,1,0:T(8,128)(2,1)} %broadcast.412.clone.1, s32[8]{0:T(128)S(1)} %get-tuple-element.49, bf16[8,256,128]{2,1,0:T(8,128)(2,1)} %gather_fusion.5), kind=kCustom, calls=%fused_computation.15 | custom fusion | bytes 1572896 | tf_op jit(solution)/shard_map/scatter | solution.py:126
  54.1 20.6 %all-to-all-done = bf16[32,256,128]{2,1,0:T(8,128)(2,1)} async-done(((bf16[32,256,128]{2,1,0:T(8,128)(2,1)}), bf16[32,256,128]{2,1,0:T(8,128)(2,1)}, u32[]{:S(2)}, u32[]{:S(2)}) %all-to-all-start) | async-done | bytes 2097184 | tf_op jit(solution)/shard_map/all_to_all | solution.py:141
  74.6 6.0 %all-to-all-start.1 = ((bf16[32,256,128]{2,1,0:T(8,128)(2,1)}), bf16[32,256,128]{2,1,0:T(8,128)(2,1)}, u32[]{:S(2)}, u32[]{:S(2)}) async-start(bf16[32,256,128]{2,1,0:T(8,128)(2,1)} %scatter_fusion.4), calls=%async_computation.1 | async-start | bytes 4194304 | tf_op jit(solution)/shard_map/all_to_all | solution.py:142
  80.7 0.9 exp.70
  81.6 0.8 fusion.49
  84.2 1.4 fusion.24
  85.7 2.5 %gather_fusion.8 = f32[16,3,1024]{2,1,0:T(4,128)} fusion(f32[32,3,1024]{2,1,0:T(4,128)} %copy-done.6, s32[1024]{0:T(1024)} %pad_clamp_fusion), kind=kCustom, calls=%fused_computation.8 | custom fusion | bytes 393280 | tf_op jit(solution)/shard_map/gather | solution.py:129
  88.2 1.2 broadcast_select_fusion.2
  89.4 1.5 fusion.11
  91.5 0.7 fusion.43
  92.2 1.0 fusion.54
  93.7 77.9 %all-reduce = (f32[16,32]{1,0:T(8,128)S(1)}, bf16[16,256]{1,0:T(8,128)(2,1)S(1)}, f32[16,32]{1,0:T(8,128)}, bf16[16,256]{1,0:T(8,128)(2,1)}) all-reduce(f32[16,32]{1,0:T(8,128)S(1)} %fusion.54, f32[16,256]{1,0:T(8,128)S(1)} %fusion.55, f32[16,32]{1,0:T(8,128)S(1)} %fusion.56, ...), channel_id=1, replica_groups=mesh['replica'=32,'tensor'=8] {'tensor'}, use_global_device_ids=true, to_apply=%region_13.14 | all-reduce | flops 9216 | bytes 57344 | tf_op jit(solution)/shard_map/psum | solution.py:38
  171.7 1.2 fusion.52
  172.9 3.5 %multiply_reduce_fusion.1 = (f32[16,1024]{1,0:T(8,128)}, f32[16,16,1024]{2,1,0:T(8,128)}) fusion(f32[16,16]{1,0:T(8,128)S(1)} %get-tuple-element.37, f32[16,1024]{1,0:T(8,128)S(1)} %get-tuple-element.44, f32[16,16]{1,0:T(8,128)S(1)} %get-tuple-element.36, f32[16,1024]{1,0:T(8,128)S(1)} %get-tuple-element.53, f32[16,16,1024]{2,1,0:T(8,128)} %param.28, ...), kind=kLoop, calls=%fused_computation.37 | loop fusion | flops 1818624 | bytes 2426880 | tf_op jit(solution)/shard_map/reduce_sum | solution.py:56
  176.4 2.7 %gather_fusion.9 = f32[8,16,1024]{2,1,0:T(8,128)} fusion(f32[16,16,1024]{2,1,0:T(8,128)} %get-tuple-element.19, s32[1024]{0:T(1024)} %copy-done.27), kind=kCustom, calls=%fused_computation.9 | custom fusion | bytes 1048608 | tf_op jit(solution)/shard_map/gather | solution.py:126
  179.1 1.6 broadcast_in_dim.76
  180.7 2.7 %scatter_fusion.7 = f32[32,16,1024]{2,1,0:T(8,128)} fusion(f32[32,16,1024]{2,1,0:T(8,128)} %broadcast_in_dim.76, s32[8]{0:T(128)S(1)} %get-tuple-element.49, f32[8,16,1024]{2,1,0:T(8,128)} %gather_fusion.9), kind=kCustom, calls=%fused_computation.18 | custom fusion | bytes 1572896 | tf_op jit(solution)/shard_map/scatter | solution.py:126
  183.4 8.1 %all-to-all-start.3 = ((f32[32,16,1024]{2,1,0:T(8,128)}), f32[32,16,1024]{2,1,0:T(8,128)}, u32[]{:S(2)}, u32[]{:S(2)}) async-start(f32[32,16,1024]{2,1,0:T(8,128)} %scatter_fusion.7), calls=%async_computation.3 | async-start | bytes 4194304 | tf_op jit(solution)/shard_map/all_to_all | solution.py:133
  191.6 0.7 gather_fusion.2
  192.3 1.4 fusion.46
  193.7 1.3 reshape.471
  195.0 1.3 reshape.469
  196.3 0.7 iota_compare_fusion.1
  197.0 1.1 fusion.9
  198.1 0.6 copy-done.17
  198.8 0.8 fusion.51
  199.5 1.8 convolution_convert_fusion.1
  201.4 1.3 stack_reshape.6
  202.7 0.7 iota_compare_fusion
  203.5 0.8 copy.34
  204.3 1.4 fusion.48
  205.8 1.9 fusion.53
  207.7 3.4 %gather_fusion.4 = bf16[16,256,128]{2,1,0:T(8,128)(2,1)} fusion(bf16[32,256,128]{2,1,0:T(8,128)(2,1)} %all-to-all-done, s32[1024]{0:T(1024)} %pad_clamp_fusion), kind=kCustom, calls=%fused_computation.4 | custom fusion | bytes 2097216 | tf_op jit(solution)/shard_map/gather | solution.py:129
  211.1 3.4 %gather_fusion.6 = bf16[16,256,128]{2,1,0:T(8,128)(2,1)} fusion(bf16[32,256,128]{2,1,0:T(8,128)(2,1)} %all-to-all-done.1, s32[1024]{0:T(1024)} %pad_clamp_fusion), kind=kCustom, calls=%fused_computation.6 | custom fusion | bytes 2097216 | tf_op jit(solution)/shard_map/gather | solution.py:129
  214.5 3.3 %broadcast_select_fusion.1 = (bf16[16,256,128]{2,1,0:T(8,128)(2,1)}, bf16[16,256,128]{2,1,0:T(8,128)(2,1)}) fusion(bf16[16,256,128]{2,1,0:T(8,128)(2,1)} %gather_fusion.4, bf16[16,256,128]{2,1,0:T(8,128)(2,1)S(1)} %scatter_fusion, pred[16]{0:T(512)(128)(4,1)S(1)} %copy-done.26, bf16[16,256,128]{2,1,0:T(8,128)(2,1)} %gather_fusion.6, ...), kind=kLoop, calls=%fused_computation.40 | loop fusion | flops 1048576 | bytes 6291472 | tf_op jit(solution)/shard_map/jit(_where)/select_n | solution.py:63
  217.8 2.2 scatter_fusion.5
  219.9 2.3 scatter_fusion.3
  222.2 1.7 fusion.7
  224.1 1.5 convolution_convert_fusion
  225.7 0.6 pad_maximum_fusion.3
  226.3 15.5 %all-to-all-done.3 = f32[32,16,1024]{2,1,0:T(8,128)} async-done(((f32[32,16,1024]{2,1,0:T(8,128)}), f32[32,16,1024]{2,1,0:T(8,128)}, u32[]{:S(2)}, u32[]{:S(2)}) %all-to-all-start.3) | async-done | bytes 2097184 | tf_op jit(solution)/shard_map/all_to_all | solution.py:133
  241.8 2.3 gather_fusion.10
  244.2 2.5 %multiply_reduce_fusion = (f32[16,1024]{1,0:T(8,128)S(1)}, f32[16,16,1024]{2,1,0:T(8,128)}) fusion(f32[16,16]{1,0:T(8,128)} %get-tuple-element.39, f32[16,1024]{1,0:T(8,128)S(1)} %copy-done.13, f32[16,16]{1,0:T(8,128)S(1)} %get-tuple-element.38, f32[16,1024]{1,0:T(8,128)} %get-tuple-element.55, f32[16,16,1024]{2,1,0:T(8,128)S(1)} %gather_fusion.10, ...), kind=kLoop, calls=%fused_computation.35 | loop fusion | flops 2080768 | bytes 3475472 | tf_op jit(solution)/shard_map/reduce_sum | solution.py:56
  246.8 0.6 pad_maximum_fusion.2
  (92 shorter events, 5.3 us)
Async XLA Ops:
  0.6 21.6 %copy-start = (bf16[32,128,128]{2,1,0:T(8,128)(2,1)S(1)}, bf16[32,128,128]{2,1,0:T(8,128)(2,1)}, u32[]{:S(2)}) copy-start(bf16[32,128,128]{2,1,0:T(8,128)(2,1)} %param.22) | copy-start | bytes 3145732
  0.6 21.4 %copy-start.32 = (s32[16,2]{0,1:T(2,128)S(1)}, s32[16,2]{0,1:T(2,128)}, u32[]{:S(2)}) copy-start(s32[16,2]{0,1:T(2,128)} %param.21) | copy-start | bytes 388
  1.5 46.6 %copy-start.27 = (s32[1024]{0:T(1024)}, s32[1024]{0:T(1024)S(1)}, u32[]{:S(2)}) copy-start(s32[1024]{0:T(1024)S(1)} %pad_clamp_fusion.1) | copy-start | bytes 12292
  4.8 18.2 %copy-start.1 = (s32[512]{0:T(512)S(1)}, s32[512]{0:T(512)}, u32[]{:S(2)}) copy-start(s32[512]{0:T(512)} %param.20) | copy-start | bytes 6148
  4.9 18.8 %copy-start.28 = (bf16[2,16,128]{2,1,0:T(8,128)(2,1)S(1)}, bf16[2,16,128]{2,1,0:T(8,128)(2,1)}, u32[]{:S(2)}) copy-start(bf16[2,16,128]{2,1,0:T(8,128)(2,1)} %param.25) | copy-start | bytes 24580
  7.9 30.1 %all-to-all-start.2 = ((f32[32,3,1024]{2,1,0:T(4,128)}), f32[32,3,1024]{2,1,0:T(4,128)S(1)}, u32[]{:S(2)}, u32[]{:S(2)}) async-start(f32[32,3,1024]{2,1,0:T(4,128)} %scatter_fusion.6), calls=%async_computation.2 | async-start | bytes 1048576 | tf_op jit(solution)/shard_map/all_to_all | solution.py:132
  38.0 0.8 copy-start.6
  38.8 35.8 %all-to-all-start = ((bf16[32,256,128]{2,1,0:T(8,128)(2,1)}), bf16[32,256,128]{2,1,0:T(8,128)(2,1)}, u32[]{:S(2)}, u32[]{:S(2)}) async-start(bf16[32,256,128]{2,1,0:T(8,128)(2,1)} %scatter_fusion.2), calls=%async_computation | async-start | bytes 4194304 | tf_op jit(solution)/shard_map/all_to_all | solution.py:141
  44.2 2.0 copy-start.29
  74.6 108.8 %all-to-all-start.1 = ((bf16[32,256,128]{2,1,0:T(8,128)(2,1)}), bf16[32,256,128]{2,1,0:T(8,128)(2,1)}, u32[]{:S(2)}, u32[]{:S(2)}) async-start(bf16[32,256,128]{2,1,0:T(8,128)(2,1)} %scatter_fusion.4), calls=%async_computation.1 | async-start | bytes 4194304 | tf_op jit(solution)/shard_map/all_to_all | solution.py:142
  80.7 10.8 %copy-start.21 = (f32[1024]{0:T(1024)S(1)}, f32[1024]{0:T(1024)}, u32[]{:S(2)}) copy-start(f32[1024]{0:T(1024)} %param.32) | copy-start | bytes 12292
  80.7 91.0 %copy-start.19 = (f32[1024]{0:T(1024)S(1)}, f32[1024]{0:T(1024)}, u32[]{:S(2)}) copy-start(f32[1024]{0:T(1024)} %param.36) | copy-start | bytes 12292
  82.5 0.6 copy-start.25
  88.2 4.9 %copy-start.14 = (bf16[1024,32]{0,1:T(8,128)(2,1)S(1)}, bf16[1024,32]{0,1:T(8,128)(2,1)}, u32[]{:S(2)}) copy-start(bf16[1024,32]{0,1:T(8,128)(2,1)} %param.34) | copy-start | bytes 196612
  88.2 5.1 %copy-start.5 = (bf16[1024,256]{1,0:T(8,128)(2,1)S(1)}, bf16[1024,256]{1,0:T(8,128)(2,1)}, u32[]{:S(2)}) copy-start(bf16[1024,256]{1,0:T(8,128)(2,1)} %param.33) | copy-start | bytes 1572868
  89.4 1.5 copy-start.3
  90.9 0.6 copy-start.8
  90.9 1.3 copy-start.10
  183.4 8.2 %copy-start.31 = (s32[16]{0:T(128)S(1)}, s32[16]{0:T(128)}, u32[]{:S(2)}) copy-start(s32[16]{0:T(128)} %get-tuple-element.26) | copy-start | bytes 196
  183.4 58.3 %all-to-all-start.3 = ((f32[32,16,1024]{2,1,0:T(8,128)}), f32[32,16,1024]{2,1,0:T(8,128)}, u32[]{:S(2)}, u32[]{:S(2)}) async-start(f32[32,16,1024]{2,1,0:T(8,128)} %scatter_fusion.7), calls=%async_computation.3 | async-start | bytes 4194304 | tf_op jit(solution)/shard_map/all_to_all | solution.py:133
  191.6 11.8 %copy-start.4 = (f32[16,3,1024]{2,1,0:T(4,128)S(1)}, f32[16,3,1024]{2,1,0:T(4,128)}, u32[]{:S(2)}) copy-start(f32[16,3,1024]{2,1,0:T(4,128)} %copy-done.3) | copy-start | bytes 589828
  191.6 11.8 %copy-start.7 = (f32[16,1,1024]{2,1,0:T(1,128)S(1)}, f32[16,1,1024]{2,1,0:T(1,128)}, u32[]{:S(2)}) copy-start(f32[16,1,1024]{2,1,0:T(1,128)} %fusion.24) | copy-start | bytes 196612
  198.1 0.6 copy-start.17
  207.7 6.7 %copy-start.26 = (pred[16]{0:T(512)(128)(4,1)S(1)}, pred[16]{0:T(512)(128)(4,1)}, u32[]{:S(2)}) copy-start(pred[16]{0:T(512)(128)(4,1)} %copy-done.25) | copy-start | bytes 52
  214.4 3.3 %copy-start.24 = (bf16[16,128]{1,0:T(8,128)(2,1)S(1)}, bf16[16,128]{1,0:T(8,128)(2,1)}, u32[]{:S(2)}) copy-start(bf16[16,128]{1,0:T(8,128)(2,1)} %get-tuple-element.42) | copy-start | bytes 12292
  214.4 5.5 %copy-start.23 = (bf16[16,128]{1,0:T(8,128)(2,1)S(1)}, bf16[16,128]{1,0:T(8,128)(2,1)}, u32[]{:S(2)}) copy-start(bf16[16,128]{1,0:T(8,128)(2,1)} %get-tuple-element.40) | copy-start | bytes 12292
  214.4 7.8 %copy-start.15 = (bf16[16,4,128]{2,1,0:T(4,128)(2,1)S(1)}, bf16[16,4,128]{2,1,0:T(4,128)(2,1)}, u32[]{:S(2)}) copy-start(bf16[16,4,128]{2,1,0:T(4,128)(2,1)} %reshape.471) | copy-start | bytes 49156
  214.4 7.8 %copy-start.20 = (pred[16,256]{1,0:T(8,128)(4,1)S(1)}, pred[16,256]{1,0:T(8,128)(4,1)}, u32[]{:S(2)}) copy-start(pred[16,256]{1,0:T(8,128)(4,1)} %iota_compare_fusion) | copy-start | bytes 12292
  217.8 7.9 %copy-start.18 = (bf16[1,16,512]{2,1,0:T(8,128)(2,1)S(1)}, bf16[1,16,512]{2,1,0:T(8,128)(2,1)}, u32[]{:S(2)}) copy-start(bf16[1,16,512]{2,1,0:T(8,128)(2,1)} %stack_reshape.6) | copy-start | bytes 49156
  222.2 22.0 %copy-start.2 = (f32[16,16,1024]{2,1,0:T(8,128)S(1)}, f32[16,16,1024]{2,1,0:T(8,128)}, u32[]{:S(2)}) copy-start(f32[16,16,1024]{2,1,0:T(8,128)} %get-tuple-element.19) | copy-start | bytes 3145732
  222.2 22.0 %copy-start.13 = (f32[16,1024]{1,0:T(8,128)S(1)}, f32[16,1024]{1,0:T(8,128)}, u32[]{:S(2)}) copy-start(f32[16,1024]{1,0:T(8,128)} %get-tuple-element.22) | copy-start | bytes 196612
  244.1 2.6 %copy-start.9 = (f32[16,1024]{1,0:T(8,128)S(1)}, f32[16,1024]{1,0:T(8,128)}, u32[]{:S(2)}) copy-start(f32[16,1024]{1,0:T(8,128)} %copy-done.8) | copy-start | bytes 196612
  244.1 2.6 %copy-start.11 = (f32[16,1024]{1,0:T(8,128)S(1)}, f32[16,1024]{1,0:T(8,128)}, u32[]{:S(2)}) copy-start(f32[16,1024]{1,0:T(8,128)} %copy-done.10) | copy-start | bytes 196612
  244.1 2.6 %copy-start.12 = (f32[16,1024]{1,0:T(8,128)S(1)}, f32[16,1024]{1,0:T(8,128)}, u32[]{:S(2)}) copy-start(f32[16,1024]{1,0:T(8,128)} %get-tuple-element.18) | copy-start | bytes 196612
  244.1 2.6 %copy-start.16 = (bf16[2,16,1024]{2,1,0:T(8,128)(2,1)S(1)}, bf16[2,16,1024]{2,1,0:T(8,128)(2,1)}, u32[]{:S(2)}) copy-start(bf16[2,16,1024]{2,1,0:T(8,128)(2,1)} %param.30) | copy-start | bytes 196612
  244.2 2.6 %copy-start.22 = (f32[1024]{0:T(1024)S(1)}, f32[1024]{0:T(1024)}, u32[]{:S(2)}) copy-start(f32[1024]{0:T(1024)} %param.32) | copy-start | bytes 12292
  244.2 2.6 %copy-start.30 = (f32[1024]{0:T(1024)S(1)}, f32[1024]{0:T(1024)}, u32[]{:S(2)}) copy-start(f32[1024]{0:T(1024)} %param.38) | copy-start | bytes 12292
where the time goes:
time: 249 us; the launch traced here: 247 us
  blocking collectives  77.9 us (31%)
  local copies, waits for them, and re-layouts  60.1 us (24%)
  waiting for transfers between devices  43.6 us (18%)
  starting transfers between devices  33.7 us (14%)
  other arithmetic  20.2 us (8%)
  matrix products  10.8 us (4%)
    psum x1, blocking collectives, mamba_step(): lax.psum((jnp.dot(mixed_in, dt_down, preferred_element_type=jnp.float32),...  77.9 us
    all_to_all x1, waiting for transfers between devices, shards(): lax.all_to_all(pack_moving(key_cache), 'replica', split_axis=0, concat_ax...  20.6 us
    all_to_all x1, waiting for transfers between devices, shards(): lax.all_to_all(pack_moving(state_one), 'replica', split_axis=0, concat_ax...  15.5 us
    all_to_all x1, starting transfers between devices, shards(): lax.all_to_all(pack_moving(conv_one), 'replica', split_axis=0, concat_axi...  14.2 us
    gather x4, local copies, waits for them, and re-layouts, take_arrived(): return keep_where(arrived, received[source_rep], local_rows)  11.6 us
    scatter x4, local copies, waits for them, and re-layouts, pack_moving(): return empty.at[leave_dest].set(local_rows[leave_slot])  10 us
    all_to_all x1, starting transfers between devices, shards(): lax.all_to_all(pack_moving(state_one), 'replica', split_axis=0, concat_ax...  8.14 us
    all_to_all x1, waiting for transfers between devices, shards(): lax.all_to_all(pack_moving(conv_one), 'replica', split_axis=0, concat_axi...  7.53 us
  transfers between devices with their start and end apart: 4, of which 3 were waited for; matrix products, arithmetic and copies ran while one was open for 31% of the time, Pallas kernels for 0%

commit v1 on v0

v1 whole, which is shorter than its diff:
```python
import functools
import math

import jax
import jax.numpy as jnp
from jax import lax
from jax.experimental import pallas as pl
from jax.experimental.pallas import tpu as pltpu
from jax.sharding import PartitionSpec as P

HD = 128
SLOTS = 16
MOVES = 8
HEADS = 4
DS = 16
PIECES = 8
STATE_ROWS = DS * PIECES
CONV_ROWS = 4 * PIECES
BACK = STATE_ROWS + CONV_ROWS
SLOT_ROWS = BACK + 16
BF = jnp.bfloat16
F32 = jnp.float32

VMEM = pl.BlockSpec(memory_space=pltpu.VMEM)
SMEM = pl.BlockSpec(memory_space=pltpu.SMEM)


def out_move(me, moves, j, replicas):
    row = me * MOVES + j
    return moves[0, row] & (SLOTS - 1), lax.shift_right_logical(moves[1, row], 4)


def in_move(me, moves, j, replicas):
    target = lax.shift_right_logical(moves[1, me * MOVES + j], 4)
    source = (2 * me - target + replicas) & (replicas - 1)
    return moves[1, source * MOVES + j] & (SLOTS - 1), source


def pack_kernel(replicas, rep, moves, ssm, conv, x, q, nk, nv, send, small):
    me = rep[0]
    width = CONV_ROWS + 16
    rows = [conv[k] for k in range(3)] + [x[0].astype(F32)]
    pieces = [row[:, c * HD : (c + 1) * HD] for row in rows for c in range(PIECES)]
    pieces += [q[1, :, h * HD : (h + 1) * HD].astype(F32) for h in range(HEADS)]
    pieces += [nk[1].astype(F32), nv[1].astype(F32)]
    for i in range(width):
        piece = pieces[i] if i < len(pieces) else jnp.zeros((SLOTS, HD), F32)
        small[pl.ds(i, SLOTS, stride=width), :] = piece
    for j in range(MOVES):
        slot, target = out_move(me, moves, j, replicas)
        got, source = in_move(me, moves, j, replicas)
        for c in range(PIECES):
            lanes = slice(c * HD, (c + 1) * HD)
            send[target, c * DS : (c + 1) * DS, :] = ssm[slot, :, lanes].astype(BF)
        start = pl.multiple_of(slot * width, 16)
        send[target, STATE_ROWS:BACK, :] = small[pl.ds(start, CONV_ROWS), :].astype(BF)
        start = pl.multiple_of(got * width + CONV_ROWS, 16)
        send[source, BACK:SLOT_ROWS, :] = small[pl.ds(start, 16), :].astype(BF)


def attend_slots(qs, lens, pages, keys, values, fresh_k, fresh_v, me, second, result):
    scale = 1.0 / math.sqrt(HD)
    position = lax.broadcasted_iota(jnp.int32, (8, HD), 1)
    nt = (((1,), (1,)), ((), ()))
    for s in range(SLOTS):
        length = lens[me * SLOTS + s]
        wide = qs[s * 8 : s * 8 + 8, :]
        narrow = wide.astype(BF)
        page0 = pages[0, s]
        page1 = pages[1, s]
        score0 = lax.dot_general(narrow, keys[page0], nt, preferred_element_type=F32) * scale
        score1 = lax.dot_general(narrow, keys[page1], nt, preferred_element_type=F32) * scale
        score0 = jnp.where(position < length, score0, -1e30)
        score1 = jnp.where(position + HD < length, score1, -1e30)
        extra0 = jnp.sum(wide * fresh_k[s : s + 1, :], axis=1, keepdims=True) * scale
        largest = jnp.maximum(jnp.max(jnp.maximum(score0, score1), axis=1, keepdims=True), extra0)
        if second:
            extra1 = jnp.sum(wide * wide[HEADS : HEADS + 1, :], axis=1, keepdims=True) * scale
            largest = jnp.maximum(largest, extra1)
        part0 = jnp.exp(score0 - largest)
        part1 = jnp.exp(score1 - largest)
        new0 = jnp.exp(extra0 - largest)
        total = jnp.sum(part0 + part1, axis=1, keepdims=True) + new0
        if second:
            new1 = jnp.exp(extra1 - largest)
            total = total + new1
        attended = jnp.dot(
            (part0 / total).astype(BF), values[page0], preferred_element_type=F32
        ) + jnp.dot((part1 / total).astype(BF), values[page1], preferred_element_type=F32)
        attended = attended + (new0 / total).astype(BF).astype(F32) * fresh_v[s : s + 1, :]
        if second:
            attended = (
                attended
                + (new1 / total).astype(BF).astype(F32) * wide[HEADS + 1 : HEADS + 2, :]
            )
        result[s * 8 : s * 8 + 8, :] = attended


def place_queries(q, qs):
    for h in range(HEADS):
        qs[pl.ds(h, SLOTS, stride=8), :] = q[:, h * HD : (h + 1) * HD].astype(F32)


def attend_one_kernel(rep, lens, pages, keys, values, q, nk, nv, out, qs, fk, fv, result):
    me = rep[0]
    qs[...] = jnp.zeros_like(qs)
    place_queries(q[0], qs)
    fk[...] = nk[0].astype(F32)
    fv[...] = nv[0].astype(F32)
    attend_slots(qs, lens, pages, keys, values, fk, fv, me, False, result)
    for h in range(HEADS):
        out[:, h * HD : (h + 1) * HD] = result[pl.ds(h, SLOTS, stride=8), :].astype(BF)


def attend_two_kernel(
    replicas, rep, moves, lens, pages, recv, keys, values, q, nk, nv, result, send, qs, fk, fv
):
    me = rep[0]
    qs[...] = jnp.zeros_like(qs)
    place_queries(q[1], qs)
    qs[pl.ds(HEADS, SLOTS, stride=8), :] = nk[1].astype(F32)
    qs[pl.ds(HEADS + 1, SLOTS, stride=8), :] = nv[1].astype(F32)
    fk[...] = nk[0].astype(F32)
    fv[...] = nv[0].astype(F32)
    for j in range(MOVES):
        slot, target = out_move(me, moves, j, replicas)
        got = recv[target, BACK:SLOT_ROWS, :].astype(F32)
        qs[pl.ds(pl.multiple_of(slot * 8, 8), 8), :] = got[:8, :]
    attend_slots(qs, lens, pages, keys, values, fk, fv, me, True, result)
    for j in range(MOVES):
        slot, target = out_move(me, moves, j, replicas)
        send[target, :, :] = result[pl.ds(pl.multiple_of(slot * 8, 8), 8), :]


def join_kernel(replicas, rep, moves, first, own, recv, out, rows):
    me = rep[0]
    rows[...] = own[...]
    for j in range(MOVES):
        slot, source = in_move(me, moves, j, replicas)
        rows[pl.ds(pl.multiple_of(slot * 8, 8), 8), :] = recv[source, :, :]
    out[0] = first[...]
    for h in range(HEADS):
        out[1, :, h * HD : (h + 1) * HD] = rows[pl.ds(h, SLOTS, stride=8), :].astype(BF)


def silu(value):
    return value / (1.0 + jnp.exp(-value))


def project_kernel(replicas, rep, moves, recv, conv, x, cw, cb, down, bct, sums, mixed, last, rows):
    me = rep[0]
    x0 = x[0].astype(F32)
    x1 = x[1].astype(F32)
    own = [conv[0], conv[1], conv[2], x0]
    for i in range(CONV_ROWS):
        k, c = divmod(i, PIECES)
        rows[pl.ds(i, SLOTS, stride=CONV_ROWS), :] = own[k][:, c * HD : (c + 1) * HD]
    for j in range(MOVES):
        slot, source = in_move(me, moves, j, replicas)
        start = pl.multiple_of(slot * CONV_ROWS, CONV_ROWS)
        rows[pl.ds(start, CONV_ROWS), :] = recv[source, STATE_ROWS:BACK, :].astype(F32)
    occ = [
        jnp.concatenate(
            [
                rows[pl.ds(k * PIECES + c, SLOTS, stride=CONV_ROWS), :]
                for c in range(PIECES)
            ],
            axis=1,
        )
        for k in range(4)
    ]
    tap = [cw[k : k + 1, :] for k in range(4)]
    bias = cb[...]
    base = conv[0] * tap[0] + conv[1] * tap[1] + conv[2] * tap[2] + x0 * tap[3] + bias
    mixed[0:16] = silu(base)
    base = occ[0] * tap[0] + occ[1] * tap[1] + occ[2] * tap[2] + occ[3] * tap[3] + bias
    mixed[16:32] = silu(base)
    base = occ[1] * tap[0] + occ[2] * tap[1] + occ[3] * tap[2] + x1 * tap[3] + bias
    mixed[32:48] = silu(base)
    last[0] = occ[2]
    last[1] = occ[3]
    last[2] = x1
    narrow = mixed[...].astype(BF)
    mixed[...] = narrow.astype(F32)
    sums[0:48, :] = jnp.dot(narrow, down[...], preferred_element_type=F32)
    maps = lax.dot_general(
        bct[...], narrow, (((1,), (1,)), ((), ())), preferred_element_type=F32
    )
    sums[48:64, :] = jnp.zeros((16, 256), F32)
    sums[48:64, 0:48] = maps[0:DS]
    sums[48:64, 128:176] = maps[DS:]


def scan_kernel(
    replicas,
    rep,
    moves,
    sums,
    mixed,
    recv,
    ssm,
    z,
    up,
    db,
    alog,
    skip,
    out,
    final,
    step,
    yrows,
    origin,
):
    me = rep[0]
    for s in range(SLOTS):
        origin[s] = -1
    for j in range(MOVES):
        slot, source = in_move(me, moves, j, replicas)
        origin[slot] = source
    dt = jnp.dot(sums[0:48, :].astype(BF), up[...], preferred_element_type=F32) + db[...]
    dt = jnp.maximum(dt, 0.0) + jnp.log1p(jnp.exp(-jnp.abs(dt)))
    step[...] = dt
    rate = -jnp.exp(alog[...])

    def advance(state, row):
        dts = step[row : row + 1, :]
        grown = jnp.exp(dts * rate) * state
        b = sums[48:64, row : row + 1]
        return grown + b * (dts * mixed[row : row + 1, :])

    def read(state, row):
        c = sums[48:64, 128 + row : 129 + row]
        return jnp.sum(c * state, axis=0, keepdims=True)

    for s in range(SLOTS):
        own = ssm[s]
        yrows[s : s + 1, :] = read(advance(own, s), s)
        source = origin[s]
        came = recv.at[jnp.maximum(source, 0)]
        moved = jnp.concatenate(
            [came[c * DS : (c + 1) * DS, :] for c in range(PIECES)], axis=1
        ).astype(F32)
        start = jnp.where(source >= 0, moved, own)
        state = advance(advance(start, 16 + s), 32 + s)
        final[s] = state
        yrows[16 + s : 17 + s, :] = read(state, 32 + s)
    gain = skip[...]
    out[0] = ((yrows[0:16] + gain * mixed[0:16]) * silu(z[0].astype(F32))).astype(BF)
    out[1] = ((yrows[16:32] + gain * mixed[32:48]) * silu(z[1].astype(F32))).astype(BF)


def call(kernel, kinds, outs, scratch):
    return pl.pallas_call(
        kernel,
        in_specs=[SMEM if kind == "s" else VMEM for kind in kinds],
        out_specs=[VMEM] * len(outs) if len(outs) > 1 else VMEM,
        out_shape=list(outs) if len(outs) > 1 else outs[0],
        scratch_shapes=scratch,
        compiler_params=pltpu.CompilerParams(vmem_limit_bytes=40 * 1024 * 1024),
    )


def shards(
    lengths,
    page_table,
    key_pool,
    value_pool,
    queries,
    new_keys,
    new_values,
    conv_state,
    ssm_state,
    mamba_x,
    mamba_z,
    conv_weight,
    conv_bias,
    dt_down,
    bc_proj,
    dt_up,
    dt_bias,
    a_log,
    skip_d,
    moves,
):
    replicas = lax.axis_size("replica")
    tensors = lax.axis_size("tensor")
    channels = ssm_state.shape[2]
    rep = lax.axis_index("replica").astype(jnp.int32).reshape(1)
    moves = moves.T
    pages = page_table.T
    conv = conv_state.transpose(1, 0, 2)
    shape = jax.ShapeDtypeStruct

    send = call(
        functools.partial(pack_kernel, replicas),
        "ssvvvvvv",
        [shape((replicas, SLOT_ROWS, HD), BF)],
        [
            pltpu.VMEM((SLOTS * (CONV_ROWS + 16), HD), F32),
        ],
    )(rep, moves, ssm_state, conv, mamba_x, queries, new_keys, new_values)
    recv = lax.all_to_all(send, "replica", split_axis=0, concat_axis=0, tiled=True)

    wide = (SLOTS * 8, HD)
    first = call(
        attend_one_kernel,
        "sssvvvvv",
        [shape((SLOTS, HEADS * HD), BF)],
        [pltpu.VMEM(wide, F32), pltpu.VMEM((SLOTS, HD), F32), pltpu.VMEM((SLOTS, HD), F32), pltpu.VMEM(wide, F32)],
    )(rep, lengths, pages, key_pool, value_pool, queries, new_keys, new_values)

    second, results = call(
        functools.partial(attend_two_kernel, replicas),
        "ssssvvvvvv",
        [shape(wide, F32), shape((replicas, 8, HD), F32)],
        [pltpu.VMEM(wide, F32), pltpu.VMEM((SLOTS, HD), F32), pltpu.VMEM((SLOTS, HD), F32)],
    )(rep, moves, lengths, pages, recv, key_pool, value_pool, queries, new_keys, new_values)
    back = lax.all_to_all(results, "replica", split_axis=0, concat_axis=0, tiled=True)

    sums, mixed, last = call(
        functools.partial(project_kernel, replicas),
        "ssvvvvvvv",
        [shape((64, 256), F32), shape((48, channels), F32), shape((3, SLOTS, channels), F32)],
        [pltpu.VMEM((SLOTS * CONV_ROWS, HD), F32)],
    )(rep, moves, recv, conv, mamba_x, conv_weight, conv_bias[None], dt_down, bc_proj.T)
    bit = 1
    while bit < tensors:
        sums = sums + lax.ppermute(sums, "tensor", [(i, i ^ bit) for i in range(tensors)])
        bit *= 2

    mamba_out, final_ssm = call(
        functools.partial(scan_kernel, replicas),
        "ssvvvvvvvvv",
        [shape((2, SLOTS, channels), BF), shape((SLOTS, DS, channels), F32)],
        [
            pltpu.VMEM((48, channels), F32),
            pltpu.VMEM((32, channels), F32),
            pltpu.SMEM((SLOTS,), jnp.int32),
        ],
    )(rep, moves, sums, mixed, recv, ssm_state, mamba_z, dt_up, dt_bias[None], a_log, skip_d[None])

    attention = call(
        functools.partial(join_kernel, replicas),
        "ssvvv",
        [shape((2, SLOTS, HEADS * HD), BF)],
        [pltpu.VMEM(wide, F32)],
    )(rep, moves, first, second, back)
    return attention, mamba_out, final_ssm, last.transpose(1, 0, 2)


def solution(mesh):
    in_specs = (
        P(),
        P("replica", None),
        P("replica", None, "tensor"),
        P("replica", None, "tensor"),
        P(None, "replica", "tensor"),
        P(None, "replica", "tensor"),
        P(None, "replica", "tensor"),
        P("replica", None, "tensor"),
        P("replica", None, "tensor"),
        P(None, "replica", "tensor"),
        P(None, "replica", "tensor"),
        P(None, "tensor"),
        P("tensor"),
        P("tensor", None),
        P("tensor", None),
        P(None, "tensor"),
        P("tensor"),
        P(None, "tensor"),
        P("tensor"),
        P(),
    )
    out_specs = (
        P(None, "replica", "tensor"),
        P(None, "replica", "tensor"),
        P("replica", None, "tensor"),
        P("replica", None, "tensor"),
    )
    return jax.shard_map(shards, mesh=mesh, in_specs=in_specs, out_specs=out_specs, check_vma=False)
```

time: 249 us -> 101 us (0.41)
  local copies, waits for them, and re-layouts: 60.1 us -> 13.6 us
  waiting for transfers between devices: 43.6 us -> 3.66 us
  blocking collectives: 77.9 us -> 52.9 us
  starting transfers between devices: 33.7 us -> 10.1 us
  other arithmetic: 20.2 us -> 0.03 us
  Pallas kernels: 0 us -> 18.8 us
  matrix products: 10.8 us -> 0 us
    psum x1 -> x0, blocking collectives: 77.9 us -> none  [mamba_step(): lax.psum((jnp.dot(mixed_in, dt_down, preferred_element_type=jnp.float32),...]
    all_to_all x0 -> x1, blocking collectives: none -> 52.9 us  [shards(): lax.all_to_all(send, 'replica', split_axis=0, concat_axis=0, tiled=True)]
    all_to_all x4 -> x1, waiting for transfers between devices: 43.6 us -> 0.01 us  [shards(): lax.all_to_all(results, 'replica', split_axis=0, concat_axis=0, tiled=True)]
    all_to_all x4 -> x1, starting transfers between devices: 33.7 us -> 5.09 us  [shards(): lax.all_to_all(results, 'replica', split_axis=0, concat_axis=0, tiled=True)]
    gather x11 -> x0, local copies, waits for them, and re-layouts: 20.4 us -> none  [the longest x4 11.6 us: take_arrived(): return keep_where(arrived, received[source_rep], local_rows)]
    pallas_call x0 -> x6, Pallas kernels: none -> 18.8 us  [the longest x1 5.86 us: shards(): call(functools.partial(attend_two_kernel, replicas), 'ssssvvvvvv', [shape...]
    scatter x8 -> x0, local copies, waits for them, and re-layouts: 17.1 us -> none  [the longest x4 10 us: pack_moving(): return empty.at[leave_dest].set(local_rows[leave_slot])]
    dot_general x10 -> x0, matrix products: 10.8 us -> none  [the longest x2 3.39 us: attend(): jnp.einsum('skgp,spkd->skgd', weights, value_heads, preferred_element_typ...]
  transfers between devices with their start and end apart: 4 -> 4, of which waited for: 3 -> 2; matrix products, arithmetic and copies ran while one was open for 31% -> 0% of each run, Pallas kernels for 0% -> 11%
where the time goes in v1:
time: 101 us; the launch traced here: 100 us
  blocking collectives  52.9 us (52%)
  Pallas kernels  18.8 us (19%)
  local copies, waits for them, and re-layouts  13.6 us (13%)
  starting transfers between devices  10.1 us (10%)
  waiting for transfers between devices  3.66 us (4%)
    all_to_all x1, blocking collectives, shards(): lax.all_to_all(send, 'replica', split_axis=0, concat_axis=0, tiled=True)  52.9 us
    unnamed x74, local copies, waits for them, and re-layouts  13.6 us
    pallas_call x1, Pallas kernels, shards(): call(functools.partial(attend_two_kernel, replicas), 'ssssvvvvvv', [shape...  5.86 us
    pallas_call x1, Pallas kernels, shards(): call(attend_one_kernel, 'sssvvvvv', [shape((SLOTS, HEADS * HD), BF)], [pl...  5.78 us
    all_to_all x1, starting transfers between devices, shards(): lax.all_to_all(results, 'replica', split_axis=0, concat_axis=0, tiled=True)  5.09 us
    ppermute x3, starting transfers between devices, shards(): lax.ppermute(sums, 'tensor', [(i, i ^ bit) for i in range(tensors)])  5.01 us
    ppermute x3, waiting for transfers between devices, shards(): lax.ppermute(sums, 'tensor', [(i, i ^ bit) for i in range(tensors)])  3.66 us
    pallas_call x1, Pallas kernels, shards(): call(functools.partial(scan_kernel, replicas), 'ssvvvvvvvvv', [shape((2,...  3.17 us
  transfers between devices with their start and end apart: 4, of which 2 were waited for; matrix products, arithmetic and copies ran while one was open for 0% of the time, Pallas kernels for 11%

profile of v1, /device:TPU:8, one launch (start us, length us, event | category | flops | bytes accessed | tf_op | source)
XLA Modules:
  0.0 100.1 jit_solution(12497236369255925509)
XLA Ops:
  0.6 0.0 copy-start.2
  0.6 1.2 %copy-done.2 = f32[16,16,1024]{2,1,0:T(8,128)S(1)} copy-done((f32[16,16,1024]{2,1,0:T(8,128)S(1)}, f32[16,16,1024]{2,1,0:T(8,128)}, u32[]{:S(2)}) %copy-start.2) | copy-done | bytes 1048600
  1.9 0.9 copy-done.4
  2.8 0.8 copy-done.8
  3.6 0.8 copy-done.11
  4.4 0.7 copy-done.14
  5.1 0.7 copy-done.16
  5.8 0.7 copy-done.25
  6.5 0.7 shard_map.220
  7.2 0.0 copy-start
  7.2 0.0 copy-start.1
  7.2 0.0 copy-start.9
  7.3 0.0 copy-start.30
  7.3 0.0 copy-start.32
  7.3 52.9 %all_to_all.10.recv = bf16[32,176,128]{2,1,0:T(8,128)(2,1)S(1)} all-to-all(bf16[32,176,128]{2,1,0:T(8,128)(2,1)S(1)} %shard_map.220), channel_id=1, replica_groups=mesh['replica'=32,'tensor'=8] {'replica'}, dimensions={0} | all-to-all | bytes 2883584 | tf_op jit(solution)/shard_map/all_to_all | solution.py:301
  60.2 0.0 copy-done
  60.2 0.0 copy-done.1
  60.2 0.0 copy-done.9
  60.2 0.0 copy-done.30
  60.2 0.0 copy-done.32
  60.3 5.9 %shard_map.221 = (f32[128,128]{1,0:T(8,128)S(1)}, f32[32,8,128]{2,1,0:T(8,128)S(1)}) custom-call(s32[1]{0:T(128)} %bitcast.rep, s32[2,256]{1,0:T(2,128)S(1)} %bitcast.13, s32[512]{0:T(512)S(1)} %copy-done.30, s32[2,16]{1,0:T(2,128)S(1)} %bitcast.17, bf16[32,176,128]{2,1,0:T(8,128)(2,1)S(1)} %all_to_all.10.recv, bf16[32,128,128]{2,1,0:T(8,128)(2,1)S(1)} %copy-done, ...), custom_call_target="tpu_custom_call" | custom-call | tf_op jit(solution)/shard_map/pallas_call | solution.py:311
  66.1 0.0 copy-start.13
  66.1 0.6 copy-done.13
  66.8 0.6 copy-done.23
  67.4 5.1 %all-to-all-start.1 = ((f32[32,8,128]{2,1,0:T(8,128)}), f32[32,8,128]{2,1,0:T(8,128)}, u32[]{:S(2)}, u32[]{:S(2)}) async-start(f32[32,8,128]{2,1,0:T(8,128)} %copy-done.13), calls=%async_computation.1 | async-start | bytes 262144 | tf_op jit(solution)/shard_map/all_to_all | solution.py:317
  72.5 0.0 copy-start.31
  72.5 0.0 copy-start.33
  72.6 0.0 copy-start.5
  72.6 0.9 copy-done.5
  73.5 1.0 %copy-done.7 = bf16[1024,256]{1,0:T(8,128)(2,1)S(1)} copy-done((bf16[1024,256]{1,0:T(8,128)(2,1)S(1)}, bf16[1024,256]{1,0:T(8,128)(2,1)}, u32[]{:S(2)}) %copy-start.7) | copy-done | bytes 524312
  74.5 0.8 copy-done.12
  75.4 0.8 copy-done.20
  76.2 0.7 copy-done.26
  76.9 0.7 copy-done.29
  77.6 0.7 copy-done.34
  78.3 1.7 %shard_map.223 = (f32[64,256]{1,0:T(8,128)S(1)}, f32[48,1024]{1,0:T(8,128)S(1)}, f32[3,16,1024]{2,1,0:T(8,128)}) custom-call(s32[1]{0:T(128)} %bitcast.rep, s32[2,256]{1,0:T(2,128)S(1)} %bitcast.14, bf16[32,176,128]{2,1,0:T(8,128)(2,1)S(1)} %all_to_all.10.recv, f32[3,16,1024]{2,1,0:T(8,128)S(1)} %bitcast.10, bf16[2,16,1024]{2,1,0:T(8,128)(2,1)S(1)} %copy-done.12, ...), custom_call_target="tpu_custom_call" | custom-call | tf_op jit(solution)/shard_map/pallas_call | solution.py:319
  80.0 0.0 copy-start.27
  80.0 0.0 copy-start.35
  80.0 0.0 copy-start.36
  80.0 0.1 collective-permute-start
  80.1 1.2 %collective-permute-done = f32[64,256]{1,0:T(8,128)S(1)} collective-permute-done((f32[64,256]{1,0:T(8,128)S(1)}, f32[64,256]{1,0:T(8,128)S(1)}, u32[]{:S(2)}, u32[]{:S(2)}) %collective-permute-start) | collective-permute-done | bytes 65568 | tf_op jit(solution)/shard_map/ppermute | solution.py:327
  81.4 2.5 %collective-permute-start.1 = (f32[64,256]{1,0:T(8,128)S(1)}, f32[64,256]{1,0:T(8,128)S(1)}, u32[]{:S(2)}, u32[]{:S(2)}) collective-permute-start(f32[64,256]{1,0:T(8,128)S(1)} %add.9), channel_id=1, source_target_pairs={{0,2},{1,3},{2,0},{3,1},{4,6},{5,7},{6,4},{7,5},{8,10},{9,11},{10,... | collective-permute-start | bytes 196616 | tf_op jit(solution)/shard_map/ppermute | solution.py:327
  83.9 2.4 %collective-permute-done.1 = f32[64,256]{1,0:T(8,128)S(1)} collective-permute-done((f32[64,256]{1,0:T(8,128)S(1)}, f32[64,256]{1,0:T(8,128)S(1)}, u32[]{:S(2)}, u32[]{:S(2)}) %collective-permute-start.1) | collective-permute-done | bytes 65568 | tf_op jit(solution)/shard_map/ppermute | solution.py:327
  86.3 2.4 %collective-permute-start.2 = (f32[64,256]{1,0:T(8,128)S(1)}, f32[64,256]{1,0:T(8,128)S(1)}, u32[]{:S(2)}, u32[]{:S(2)}) collective-permute-start(f32[64,256]{1,0:T(8,128)S(1)} %add.10), channel_id=1, source_target_pairs={{0,4},{1,5},{2,6},{3,7},{4,0},{5,1},{6,2},{7,3},{8,12},{9,13},{10,... | collective-permute-start | bytes 196616 | tf_op jit(solution)/shard_map/ppermute | solution.py:327
  88.7 0.0 copy-done.15
  88.7 0.0 copy-done.17
  88.7 0.0 copy-done.31
  88.7 0.0 copy-done.33
  88.8 0.0 copy-done.10
  88.8 5.8 %shard_map.219.first = bf16[16,512]{1,0:T(8,128)(2,1)S(1)} custom-call(s32[1]{0:T(128)} %bitcast.rep, s32[512]{0:T(512)S(1)} %copy-done.31, s32[2,16]{1,0:T(2,128)S(1)} %bitcast.18, bf16[32,128,128]{2,1,0:T(8,128)(2,1)S(1)} %copy-done, bf16[32,128,128]{2,1,0:T(8,128)(2,1)S(1)} %copy-done.1, bf16[2,16,512]{2,1,0:T(8,128)(2,1)S(1)} %copy-done.10, ...), custom_call_target="tpu_custom_call" | custom-call | tf_op jit(solution)/shard_map/pallas_call | solution.py:304
  94.6 0.6 copy-done.18
  95.2 0.0 collective-permute-done.2
  95.2 0.0 copy-done.3
  95.2 0.0 copy-done.6
  95.2 0.0 copy-done.21
  95.2 0.0 copy-done.22
  95.2 0.0 copy-done.27
  95.2 0.0 copy-done.35
  95.3 0.0 copy-start.19
  95.3 0.0 copy-start.28
  95.3 3.2 %shard_map.224 = (bf16[2,16,1024]{2,1,0:T(8,128)(2,1)}, f32[16,16,1024]{2,1,0:T(8,128)}) custom-call(s32[1]{0:T(128)} %bitcast.rep, s32[2,256]{1,0:T(2,128)S(1)} %bitcast.15, f32[64,256]{1,0:T(8,128)S(1)} %add.11.sums, f32[48,1024]{1,0:T(8,128)S(1)} %get-tuple-element.14.mixed, bf16[32,176,128]{2,1,0:T(8,128)(2,1)S(1)} %all_to_all.10.recv, ...), custom_call_target="tpu_custom_call" | custom-call | tf_op jit(solution)/shard_map/pallas_call | solution.py:330
  98.5 0.0 all-to-all-done.1.recv
  98.5 0.0 copy-done.24
  98.5 1.6 %shard_map.222 = bf16[2,16,512]{2,1,0:T(8,128)(2,1)} custom-call(s32[1]{0:T(128)} %bitcast.rep, s32[2,256]{1,0:T(2,128)S(1)} %bitcast.16, bf16[16,512]{1,0:T(8,128)(2,1)S(1)} %copy-done.19, f32[128,128]{1,0:T(8,128)S(1)} %copy-done.24, f32[32,8,128]{2,1,0:T(8,128)} %all-to-all-done.1.recv), custom_call_target="tpu_custom_call" | custom-call | tf_op jit(solution)/shard_map/pallas_call | solution.py:341
  (28 shorter events, 0.1 us)
Async XLA Ops:
  0.6 1.2 %copy-start.2 = (f32[16,16,1024]{2,1,0:T(8,128)S(1)}, f32[16,16,1024]{2,1,0:T(8,128)}, u32[]{:S(2)}) copy-start(f32[16,16,1024]{2,1,0:T(8,128)} %ssm.3) | copy-start | bytes 3145732
  1.9 0.9 copy-start.4
  2.8 0.8 copy-start.8
  3.5 0.8 copy-start.11
  4.4 0.7 copy-start.14
  5.1 0.7 copy-start.16
  5.8 0.7 copy-start.25
  7.2 53.0 %copy-start = (bf16[32,128,128]{2,1,0:T(8,128)(2,1)S(1)}, bf16[32,128,128]{2,1,0:T(8,128)(2,1)}, u32[]{:S(2)}) copy-start(bf16[32,128,128]{2,1,0:T(8,128)(2,1)} %keys.3) | copy-start | bytes 3145732
  7.2 53.0 %copy-start.1 = (bf16[32,128,128]{2,1,0:T(8,128)(2,1)S(1)}, bf16[32,128,128]{2,1,0:T(8,128)(2,1)}, u32[]{:S(2)}) copy-start(bf16[32,128,128]{2,1,0:T(8,128)(2,1)} %values.3) | copy-start | bytes 3145732
  7.2 53.0 %copy-start.9 = (bf16[2,16,512]{2,1,0:T(8,128)(2,1)S(1)}, bf16[2,16,512]{2,1,0:T(8,128)(2,1)}, u32[]{:S(2)}) copy-start(bf16[2,16,512]{2,1,0:T(8,128)(2,1)} %q.5) | copy-start | bytes 98308
  7.3 53.0 %copy-start.30 = (s32[512]{0:T(512)S(1)}, s32[512]{0:T(512)}, u32[]{:S(2)}) copy-start(s32[512]{0:T(512)} %lens.3) | copy-start | bytes 6148
  7.3 53.0 %copy-start.32 = (s32[16,2]{0,1:T(2,128)S(1)}, s32[16,2]{0,1:T(2,128)}, u32[]{:S(2)}) copy-start(s32[16,2]{0,1:T(2,128)} %param.21) | copy-start | bytes 388
  66.1 0.7 copy-start.13
  66.8 0.6 copy-start.23
  67.4 21.3 %copy-start.15 = (bf16[2,16,128]{2,1,0:T(8,128)(2,1)S(1)}, bf16[2,16,128]{2,1,0:T(8,128)(2,1)}, u32[]{:S(2)}) copy-start(bf16[2,16,128]{2,1,0:T(8,128)(2,1)} %nk.5) | copy-start | bytes 24580
  67.4 21.3 %copy-start.17 = (bf16[2,16,128]{2,1,0:T(8,128)(2,1)S(1)}, bf16[2,16,128]{2,1,0:T(8,128)(2,1)}, u32[]{:S(2)}) copy-start(bf16[2,16,128]{2,1,0:T(8,128)(2,1)} %nv.5) | copy-start | bytes 24580
  67.4 31.0 %all-to-all-start.1 = ((f32[32,8,128]{2,1,0:T(8,128)}), f32[32,8,128]{2,1,0:T(8,128)}, u32[]{:S(2)}, u32[]{:S(2)}) async-start(f32[32,8,128]{2,1,0:T(8,128)} %copy-done.13), calls=%async_computation.1 | async-start | bytes 262144 | tf_op jit(solution)/shard_map/all_to_all | solution.py:317
  72.5 16.2 %copy-start.31 = (s32[512]{0:T(512)S(1)}, s32[512]{0:T(512)}, u32[]{:S(2)}) copy-start(s32[512]{0:T(512)} %lens.3) | copy-start | bytes 6148
  72.5 16.2 %copy-start.33 = (s32[16,2]{0,1:T(2,128)S(1)}, s32[16,2]{0,1:T(2,128)}, u32[]{:S(2)}) copy-start(s32[16,2]{0,1:T(2,128)} %param.21) | copy-start | bytes 388
  72.6 0.9 copy-start.5
  73.5 1.0 %copy-start.7 = (bf16[1024,256]{1,0:T(8,128)(2,1)S(1)}, bf16[1024,256]{1,0:T(8,128)(2,1)}, u32[]{:S(2)}) copy-start(bf16[1024,256]{1,0:T(8,128)(2,1)} %down.1) | copy-start | bytes 1572868
  74.5 0.8 copy-start.12
  75.4 0.8 copy-start.20
  76.2 0.7 copy-start.26
  76.9 0.7 copy-start.29
  77.6 0.7 copy-start.34
  78.3 10.5 %copy-start.10 = (bf16[2,16,512]{2,1,0:T(8,128)(2,1)S(1)}, bf16[2,16,512]{2,1,0:T(8,128)(2,1)}, u32[]{:S(2)}) copy-start(bf16[2,16,512]{2,1,0:T(8,128)(2,1)} %q.5) | copy-start | bytes 98308
  80.0 15.2 %copy-start.3 = (f32[16,16,1024]{2,1,0:T(8,128)S(1)}, f32[16,16,1024]{2,1,0:T(8,128)}, u32[]{:S(2)}) copy-start(f32[16,16,1024]{2,1,0:T(8,128)} %ssm.3) | copy-start | bytes 3145732
  80.0 15.2 %copy-start.6 = (bf16[256,1024]{1,0:T(8,128)(2,1)S(1)}, bf16[256,1024]{1,0:T(8,128)(2,1)}, u32[]{:S(2)}) copy-start(bf16[256,1024]{1,0:T(8,128)(2,1)} %up.1) | copy-start | bytes 1572868
  80.0 15.2 %copy-start.21 = (bf16[2,16,1024]{2,1,0:T(8,128)(2,1)S(1)}, bf16[2,16,1024]{2,1,0:T(8,128)(2,1)}, u32[]{:S(2)}) copy-start(bf16[2,16,1024]{2,1,0:T(8,128)(2,1)} %z.1) | copy-start | bytes 196612
  80.0 15.2 %copy-start.22 = (f32[16,1024]{1,0:T(8,128)S(1)}, f32[16,1024]{1,0:T(8,128)}, u32[]{:S(2)}) copy-start(f32[16,1024]{1,0:T(8,128)} %alog.1) | copy-start | bytes 196612
  80.0 15.2 %copy-start.27 = (s32[256,2]{0,1:T(2,128)S(1)}, s32[256,2]{0,1:T(2,128)}, u32[]{:S(2)}) copy-start(s32[256,2]{0,1:T(2,128)} %param.39) | copy-start | bytes 6148
  80.0 15.2 %copy-start.35 = (f32[1024]{0:T(1024)S(1)}, f32[1024]{0:T(1024)}, u32[]{:S(2)}) copy-start(f32[1024]{0:T(1024)} %param.36) | copy-start | bytes 12292
  80.0 15.2 %copy-start.36 = (f32[1024]{0:T(1024)S(1)}, f32[1024]{0:T(1024)}, u32[]{:S(2)}) copy-start(f32[1024]{0:T(1024)} %param.38) | copy-start | bytes 12292
  80.0 1.3 %collective-permute-start = (f32[64,256]{1,0:T(8,128)S(1)}, f32[64,256]{1,0:T(8,128)S(1)}, u32[]{:S(2)}, u32[]{:S(2)}) collective-permute-start(f32[64,256]{1,0:T(8,128)S(1)} %get-tuple-element.13), channel_id=1, source_target_pairs={{0,1},{1,0},{2,3},{3,2},{4,5},{5,4},{6,7},{7,6},{8,9},{9,8},{10,11... | collective-permute-start | bytes 196616 | tf_op jit(solution)/shard_map/ppermute | solution.py:327
  81.4 4.9 %collective-permute-start.1 = (f32[64,256]{1,0:T(8,128)S(1)}, f32[64,256]{1,0:T(8,128)S(1)}, u32[]{:S(2)}, u32[]{:S(2)}) collective-permute-start(f32[64,256]{1,0:T(8,128)S(1)} %add.9), channel_id=1, source_target_pairs={{0,2},{1,3},{2,0},{3,1},{4,6},{5,7},{6,4},{7,5},{8,10},{9,11},{10,... | collective-permute-start | bytes 196616 | tf_op jit(solution)/shard_map/ppermute | solution.py:327
  86.3 8.8 %collective-permute-start.2 = (f32[64,256]{1,0:T(8,128)S(1)}, f32[64,256]{1,0:T(8,128)S(1)}, u32[]{:S(2)}, u32[]{:S(2)}) collective-permute-start(f32[64,256]{1,0:T(8,128)S(1)} %add.10), channel_id=1, source_target_pairs={{0,4},{1,5},{2,6},{3,7},{4,0},{5,1},{6,2},{7,3},{8,12},{9,13},{10,... | collective-permute-start | bytes 196616 | tf_op jit(solution)/shard_map/ppermute | solution.py:327
  94.5 0.6 copy-start.18
  95.3 3.2 %copy-start.19 = (bf16[16,512]{1,0:T(8,128)(2,1)S(1)}, bf16[16,512]{1,0:T(8,128)(2,1)}, u32[]{:S(2)}) copy-start(bf16[16,512]{1,0:T(8,128)(2,1)} %copy-done.18) | copy-start | bytes 49156
  95.3 3.2 %copy-start.24 = (f32[128,128]{1,0:T(8,128)S(1)}, f32[128,128]{1,0:T(8,128)}, u32[]{:S(2)}) copy-start(f32[128,128]{1,0:T(8,128)} %copy-done.23) | copy-start | bytes 196612
  95.3 3.2 %copy-start.28 = (s32[256,2]{0,1:T(2,128)S(1)}, s32[256,2]{0,1:T(2,128)}, u32[]{:S(2)}) copy-start(s32[256,2]{0,1:T(2,128)} %param.39) | copy-start | bytes 6148

commit v2 on v1

v2 whole, which is shorter than its diff:
```python
import functools
import math

import jax
import jax.numpy as jnp
from jax import lax
from jax.experimental import pallas as pl
from jax.experimental.pallas import tpu as pltpu
from jax.sharding import PartitionSpec as P

HD = 128
SLOTS = 16
MOVES = 8
HEADS = 4
DS = 16
PIECES = 8
STATE_ROWS = DS * PIECES
CONV_ROWS = 4 * PIECES
SMALL_ROWS = CONV_ROWS + 16
LARGE_ROWS = STATE_ROWS + 16
REPLICAS = 32
FAR = 4
PLANE = 16
BF = jnp.bfloat16
F32 = jnp.float32

SPECS = {
    "s": pl.BlockSpec(memory_space=pltpu.SMEM),
    "v": pl.BlockSpec(memory_space=pltpu.VMEM),
    "d": pl.BlockSpec(),
    "a": pl.BlockSpec(memory_space=pl.ANY),
}


def out_move(me, moves, j):
    row = me * MOVES + j
    return moves[0, row] & (SLOTS - 1), lax.shift_right_logical(moves[1, row], 4)


def in_move(me, moves, j):
    target = lax.shift_right_logical(moves[1, me * MOVES + j], 4)
    source = (2 * me - target + REPLICAS) & (REPLICAS - 1)
    return moves[1, source * MOVES + j] & (SLOTS - 1), source


def crosses(one, other):
    return lax.shift_right_logical((one ^ other) & FAR, 2)


def place(replica):
    return lax.shift_left(lax.shift_right_logical(replica, 3), 2) | (replica & 3)


def pack_small_kernel(
    rep, moves, conv_in, x_in, q_in, nk_in, nv_in, send, conv, x, q, nk, nv, small, read
):
    me = rep[0]
    pairs = ((conv_in, conv), (x_in.at[0], x), (q_in.at[1], q), (nk_in.at[1], nk), (nv_in.at[1], nv))
    copies = [
        pltpu.make_async_copy(source, target, read.at[i])
        for i, (source, target) in enumerate(pairs)
    ]
    for copy in copies:
        copy.start()
    for copy in copies:
        copy.wait()
    zero = jnp.zeros((SLOTS, HD), F32)
    rows = [conv[k] for k in range(3)] + [x[...].astype(F32)]
    pieces = [row[:, c * HD : (c + 1) * HD] for row in rows for c in range(PIECES)]
    pieces += [nk[...].astype(F32), nv[...].astype(F32), zero, zero]
    pieces += [q[:, h * HD : (h + 1) * HD].astype(F32) for h in range(HEADS)]
    pieces += [zero] * (SMALL_ROWS - len(pieces))
    for i in range(SMALL_ROWS):
        small[pl.ds(i, SLOTS, stride=SMALL_ROWS), :] = pieces[i]
    for j in range(MOVES):
        slot, _ = out_move(me, moves, j)
        start = pl.multiple_of(slot * SMALL_ROWS, 16)
        send[j, :CONV_ROWS, :] = small[pl.ds(start, CONV_ROWS), :].astype(BF)
        slot, _ = in_move(me, moves, j)
        start = pl.multiple_of(slot * SMALL_ROWS + CONV_ROWS, 16)
        send[j, CONV_ROWS:, :] = small[pl.ds(start, 16), :].astype(BF)


def route_small_kernel(rep, moves, own, other, send):
    me = rep[0]
    for j in range(MOVES):
        _, target = out_move(me, moves, j)
        flip = crosses(me, target)
        _, target = out_move(me ^ (flip * FAR), moves, j)
        to = place(target) * 2 + flip
        send[to, :CONV_ROWS, :] = jnp.where(flip == 1, other[j, :CONV_ROWS, :], own[j, :CONV_ROWS, :])
        _, source = in_move(me, moves, j)
        flip = crosses(me, source)
        _, source = in_move(me ^ (flip * FAR), moves, j)
        to = place(source) * 2 + flip
        send[to, CONV_ROWS:, :] = jnp.where(flip == 1, other[j, CONV_ROWS:, :], own[j, CONV_ROWS:, :])


def pack_state_kernel(rep, moves, ssm, _, send, held, arrived):
    me = rep[0]
    copies = []
    for j in range(MOVES):
        slot, _ = out_move(me, moves, j)
        copies.append(pltpu.make_async_copy(ssm.at[slot], held.at[j], arrived.at[j]))
        copies[j].start()
    for j in range(MOVES):
        copies[j].wait()
        for c in range(PIECES):
            send[j, c * DS : (c + 1) * DS, :] = held[j, :, c * HD : (c + 1) * HD].astype(BF)


NT = (((1,), (1,)), ((), ()))
SCALE = 1.0 / math.sqrt(HD)


def spread(rows, value):
    for h in range(8):
        rows[pl.ds(h, SLOTS, stride=8), :] = value


def attend_slots(slots, lens, pages, keys, values, qs, first_k, first_v, next_k, next_v, both, score, limit, result):
    count = len(slots)
    wide = qs[...]
    for i, (slot, length) in enumerate(slots):
        page0, page1 = pages[0, slot], pages[1, slot]
        cached = jnp.concatenate([keys[page0], keys[page1]], axis=0)
        score[i * 8 : i * 8 + 8, :] = lax.dot_general(
            wide[i * 8 : i * 8 + 8, :].astype(BF), cached, NT, preferred_element_type=F32
        )
        limit[i * 8 : i * 8 + 8, :] = jnp.full((8, HD), length, jnp.int32)
    position = lax.broadcasted_iota(jnp.int32, (count * 8, HD), 1)
    ends = limit[...]
    score0 = jnp.where(position < ends, score[:, :HD] * SCALE, -1e30)
    score1 = jnp.where(position + HD < ends, score[:, HD:] * SCALE, -1e30)
    extra0 = jnp.sum(wide * first_k, axis=1, keepdims=True) * SCALE
    extra1 = jnp.sum(wide * next_k, axis=1, keepdims=True) * SCALE
    if both:
        row = lax.broadcasted_iota(jnp.int32, (count * 8, 1), 0) & 7
        extra1 = jnp.where(row >= HEADS, extra1, -1e30)
    largest = jnp.max(jnp.maximum(score0, score1), axis=1, keepdims=True)
    largest = jnp.maximum(largest, jnp.maximum(extra0, extra1))
    part0 = jnp.exp(score0 - largest)
    part1 = jnp.exp(score1 - largest)
    new0 = jnp.exp(extra0 - largest)
    new1 = jnp.exp(extra1 - largest)
    total = jnp.sum(part0 + part1, axis=1, keepdims=True) + new0 + new1
    score[:, :HD] = part0 / total
    score[:, HD:] = part1 / total
    new0 = (new0 / total).astype(BF).astype(F32)
    new1 = (new1 / total).astype(BF).astype(F32)
    added = new0 * first_v + new1 * next_v
    for i, (slot, length) in enumerate(slots):
        page0, page1 = pages[0, slot], pages[1, slot]
        cached = jnp.concatenate([values[page0], values[page1]], axis=0)
        result[i * 8 : i * 8 + 8, :] = (
            jnp.dot(score[i * 8 : i * 8 + 8, :].astype(BF), cached, preferred_element_type=F32)
            + added[i * 8 : i * 8 + 8, :]
        )


def attend_home_kernel(
    rep, lens, pages, keys, values, q, nk, nv, result, qs, fk, fv, gk, gv, score, limit
):
    me = rep[0]
    for step in range(2):
        for h in range(HEADS):
            qs[pl.ds(step * HEADS + h, SLOTS, stride=8), :] = q[
                step, :, h * HD : (h + 1) * HD
            ].astype(F32)
    spread(fk, nk[0].astype(F32))
    spread(fv, nv[0].astype(F32))
    spread(gk, nk[1].astype(F32))
    spread(gv, nv[1].astype(F32))
    slots = [(s, lens[me * SLOTS + s]) for s in range(SLOTS)]
    attend_slots(
        slots, lens, pages, keys, values, qs, fk[...], fv[...], gk[...], gv[...], True, score, limit, result
    )


def attend_away_kernel(
    rep, moves, lens, pages, recv, keys, values, nk, nv, own, other, _, send, qs, fk, fv, score, limit, result
):
    me = rep[0]
    spread(fk, nk[0].astype(F32))
    spread(fv, nv[0].astype(F32))
    slots = []
    first_k, first_v, next_k, next_v = [], [], [], []
    for j in range(MOVES):
        slot, target = out_move(me, moves, j)
        flip = crosses(me, target)
        got = recv[place(target) * 2 + flip, CONV_ROWS:, :].astype(F32)[:8, :]
        qs[j * 8 : j * 8 + 8, :] = got
        start = pl.multiple_of(slot * 8, 8)
        first_k.append(fk[pl.ds(start, 8), :])
        first_v.append(fv[pl.ds(start, 8), :])
        next_k.append(jnp.broadcast_to(got[0:1, :], (8, HD)))
        next_v.append(jnp.broadcast_to(got[1:2, :], (8, HD)))
        slots.append((slot, lens[me * SLOTS + slot]))
        origin = me ^ (flip * FAR)
        _, held_target = out_move(origin, moves, j)
        to = place(held_target) * 2 + flip
        send[to, :STATE_ROWS, :] = jnp.where(flip == 1, other[j], own[j])
    join = functools.partial(jnp.concatenate, axis=0)
    attend_slots(
        slots,
        lens,
        pages,
        keys,
        values,
        qs,
        join(first_k),
        join(first_v),
        join(next_k),
        join(next_v),
        False,
        score,
        limit,
        result,
    )
    blank = jnp.zeros((8, HD), F32)
    for j in range(MOVES):
        _, target = out_move(me, moves, j)
        to = place(target) * 2 + crosses(me, target)
        send[to, STATE_ROWS:, :] = join([result[j * 8 : j * 8 + 8, :], blank]).astype(BF)


def forward_kernel(rep, moves, recv, send):
    partner = rep[0] ^ FAR
    for j in range(MOVES):
        _, source = in_move(partner, moves, j)
        send[j] = recv[place(source) * 2 + 1, STATE_ROWS:, :]


def join_kernel(rep, moves, home, recv, other, out, rows):
    me = rep[0]
    rows[...] = home[...]
    second = lax.broadcasted_iota(jnp.int32, (8, HD), 0) >= HEADS
    for j in range(MOVES):
        slot, source = in_move(me, moves, j)
        near = recv[place(source) * 2, STATE_ROWS:, :]
        came = jnp.where(crosses(me, source) == 1, other[j], near).astype(F32)[:8, :]
        start = pl.multiple_of(slot * 8, 8)
        rows[pl.ds(start, 8), :] = jnp.where(second, came, rows[pl.ds(start, 8), :])
    for step in range(2):
        for h in range(HEADS):
            out[step, :, h * HD : (h + 1) * HD] = rows[
                pl.ds(step * HEADS + h, SLOTS, stride=8), :
            ].astype(BF)


def silu(value):
    return value / (1.0 + jnp.exp(-value))


def project_kernel(rep, moves, recv, conv, x, cw, cb, down, bct, sums, mixed, last, rows):
    me = rep[0]
    x0 = x[0].astype(F32)
    x1 = x[1].astype(F32)
    own = [conv[0], conv[1], conv[2], x0]
    for i in range(CONV_ROWS):
        k, c = divmod(i, PIECES)
        rows[pl.ds(i, SLOTS, stride=CONV_ROWS), :] = own[k][:, c * HD : (c + 1) * HD]
    for j in range(MOVES):
        slot, source = in_move(me, moves, j)
        start = pl.multiple_of(slot * CONV_ROWS, CONV_ROWS)
        rows[pl.ds(start, CONV_ROWS), :] = recv[
            place(source) * 2 + crosses(me, source), :CONV_ROWS, :
        ].astype(F32)
    occ = [
        jnp.concatenate(
            [
                rows[pl.ds(k * PIECES + c, SLOTS, stride=CONV_ROWS), :]
                for c in range(PIECES)
            ],
            axis=1,
        )
        for k in range(4)
    ]
    tap = [cw[k : k + 1, :] for k in range(4)]
    bias = cb[...]
    base = conv[0] * tap[0] + conv[1] * tap[1] + conv[2] * tap[2] + x0 * tap[3] + bias
    mixed[0:16] = silu(base)
    base = occ[0] * tap[0] + occ[1] * tap[1] + occ[2] * tap[2] + occ[3] * tap[3] + bias
    mixed[16:32] = silu(base)
    base = occ[1] * tap[0] + occ[2] * tap[1] + occ[3] * tap[2] + x1 * tap[3] + bias
    mixed[32:48] = silu(base)
    last[0] = occ[2]
    last[1] = occ[3]
    last[2] = x1
    narrow = mixed[...].astype(BF)
    mixed[...] = narrow.astype(F32)
    sums[0:48, :] = jnp.dot(narrow, down[...], preferred_element_type=F32)
    maps = lax.dot_general(
        bct[...], narrow, (((1,), (1,)), ((), ())), preferred_element_type=F32
    )
    sums[48:64, :] = jnp.zeros((16, 256), F32)
    sums[48:64, 0:48] = maps[0:DS]
    sums[48:64, 128:176] = maps[DS:]


def scan_kernel(
    rep,
    moves,
    sums,
    mixed,
    recv,
    ssm,
    z,
    up,
    db,
    alog,
    skip,
    out,
    final,
    step,
    yrows,
    origin,
):
    me = rep[0]
    for s in range(SLOTS):
        origin[s] = -1
    for j in range(MOVES):
        slot, source = in_move(me, moves, j)
        origin[slot] = place(source) * 2 + crosses(me, source)
    dt = jnp.dot(sums[0:48, :].astype(BF), up[...], preferred_element_type=F32) + db[...]
    dt = jnp.maximum(dt, 0.0) + jnp.log1p(jnp.exp(-jnp.abs(dt)))
    step[...] = dt
    rate = -jnp.exp(alog[...])

    def advance(state, row):
        dts = step[row : row + 1, :]
        grown = jnp.exp(dts * rate) * state
        b = sums[48:64, row : row + 1]
        return grown + b * (dts * mixed[row : row + 1, :])

    def read(state, row):
        c = sums[48:64, 128 + row : 129 + row]
        return jnp.sum(c * state, axis=0, keepdims=True)

    for s in range(SLOTS):
        own = ssm[s]
        yrows[s : s + 1, :] = read(advance(own, s), s)
        source = origin[s]
        came = recv.at[jnp.maximum(source, 0)]
        moved = jnp.concatenate(
            [came[c * DS : (c + 1) * DS, :] for c in range(PIECES)], axis=1
        ).astype(F32)
        start = jnp.where(source >= 0, moved, own)
        state = advance(advance(start, 16 + s), 32 + s)
        final[s] = state
        yrows[16 + s : 17 + s, :] = read(state, 32 + s)
    gain = skip[...]
    out[0] = ((yrows[0:16] + gain * mixed[0:16]) * silu(z[0].astype(F32))).astype(BF)
    out[1] = ((yrows[16:32] + gain * mixed[32:48]) * silu(z[1].astype(F32))).astype(BF)


def call(kernel, kinds, outs, scratch, flops=0, room=32):
    outs_specs = [SPECS[kind] for kind, _ in outs]
    shapes = [shape for _, shape in outs]
    return pl.pallas_call(
        kernel,
        in_specs=[SPECS[kind] for kind in kinds],
        out_specs=outs_specs if len(outs) > 1 else outs_specs[0],
        out_shape=shapes if len(outs) > 1 else shapes[0],
        scratch_shapes=scratch,
        cost_estimate=pl.CostEstimate(flops=flops, bytes_accessed=0, transcendentals=0),
        compiler_params=pltpu.CompilerParams(vmem_limit_bytes=room * 1024 * 1024),
    )


def shards(
    lengths,
    page_table,
    key_pool,
    value_pool,
    queries,
    new_keys,
    new_values,
    conv_state,
    ssm_state,
    mamba_x,
    mamba_z,
    conv_weight,
    conv_bias,
    dt_down,
    bc_proj,
    dt_up,
    dt_bias,
    a_log,
    skip_d,
    moves,
):
    tensors = lax.axis_size("tensor")
    channels = ssm_state.shape[2]
    rep = lax.axis_index("replica").astype(jnp.int32).reshape(1)
    moves = moves.T
    pages = page_table.T
    conv = conv_state.transpose(1, 0, 2)
    shape = jax.ShapeDtypeStruct
    across = [(i, i ^ FAR) for i in range(REPLICAS)]
    planes = [[i for i in range(REPLICAS) if i & FAR == side] for side in (0, FAR)]
    rows = SLOTS * 8

    near_small = call(
        pack_small_kernel,
        "ssaaaaa",
        [("v", shape((MOVES, SMALL_ROWS, HD), BF))],
        [
            pltpu.VMEM((3, SLOTS, channels), F32),
            pltpu.VMEM((SLOTS, channels), BF),
            pltpu.VMEM((SLOTS, HEADS * HD), BF),
            pltpu.VMEM((SLOTS, HD), BF),
            pltpu.VMEM((SLOTS, HD), BF),
            pltpu.VMEM((SLOTS * SMALL_ROWS, HD), F32),
            pltpu.SemaphoreType.DMA((5,)),
        ],
        room=60,
    )(rep, moves, conv, mamba_x, queries, new_keys, new_values)
    far_small = lax.ppermute(near_small, "replica", across)

    own = call(
        pack_state_kernel,
        "ssaa",
        [("v", shape((MOVES, STATE_ROWS, HD), BF))],
        [pltpu.VMEM((MOVES, DS, channels), F32), pltpu.SemaphoreType.DMA((MOVES,))],
        room=60,
    )(rep, moves, ssm_state, near_small)
    other = lax.ppermute(own, "replica", across)

    small = call(
        route_small_kernel,
        "ssvv",
        [("v", shape((REPLICAS, SMALL_ROWS, HD), BF))],
        [],
    )(rep, moves, near_small, far_small)
    small = lax.all_to_all(
        small, "replica", split_axis=0, concat_axis=0, tiled=True, axis_index_groups=planes
    )

    home = call(
        attend_home_kernel,
        "sssvvddd",
        [("v", shape((rows, HD), F32))],
        [pltpu.VMEM((rows, HD), F32)] * 5
        + [pltpu.VMEM((rows, 2 * HD), F32), pltpu.VMEM((rows, HD), jnp.int32)],
        flops=4_000_000_000,
    )(rep, lengths, pages, key_pool, value_pool, queries, new_keys, new_values)

    away = MOVES * 8
    large = call(
        attend_away_kernel,
        "ssssvvvddvva",
        [("v", shape((REPLICAS, LARGE_ROWS, HD), BF))],
        [
            pltpu.VMEM((away, HD), F32),
            pltpu.VMEM((rows, HD), F32),
            pltpu.VMEM((rows, HD), F32),
            pltpu.VMEM((away, 2 * HD), F32),
            pltpu.VMEM((away, HD), jnp.int32),
            pltpu.VMEM((away, HD), F32),
        ],
    )(rep, moves, lengths, pages, small, key_pool, value_pool, new_keys, new_values, own, other, home)
    large = lax.all_to_all(
        large, "replica", split_axis=0, concat_axis=0, tiled=True, axis_index_groups=planes
    )

    sums, mixed, last = call(
        project_kernel,
        "ssvdddddd",
        [
            ("v", shape((64, 256), F32)),
            ("v", shape((48, channels), F32)),
            ("d", shape((3, SLOTS, channels), F32)),
        ],
        [pltpu.VMEM((SLOTS * CONV_ROWS, HD), F32)],
        flops=2_000_000_000,
    )(rep, moves, small, conv, mamba_x, conv_weight, conv_bias[None], dt_down, bc_proj.T)
    bit = 1
    while bit < tensors:
        sums = sums + lax.ppermute(sums, "tensor", [(i, i ^ bit) for i in range(tensors)])
        bit *= 2

    far = call(
        forward_kernel,
        "ssv",
        [("v", shape((MOVES, 16, HD), BF))],
        [],
    )(rep, moves, large)
    far = lax.ppermute(far, "replica", across)

    mamba_out, final_ssm = call(
        scan_kernel,
        "ssvvvvvvvvv",
        [
            ("d", shape((2, SLOTS, channels), BF)),
            ("d", shape((SLOTS, DS, channels), F32)),
        ],
        [
            pltpu.VMEM((48, channels), F32),
            pltpu.VMEM((32, channels), F32),
            pltpu.SMEM((SLOTS,), jnp.int32),
        ],
        flops=3_000_000_000,
    )(rep, moves, sums, mixed, large, ssm_state, mamba_z, dt_up, dt_bias[None], a_log, skip_d[None])

    attention = call(
        join_kernel,
        "ssvvv",
        [("d", shape((2, SLOTS, HEADS * HD), BF))],
        [pltpu.VMEM((rows, HD), F32)],
    )(rep, moves, home, large, far)
    return attention, mamba_out, final_ssm, last.transpose(1, 0, 2)


def solution(mesh):
    in_specs = (
        P(),
        P("replica", None),
        P("replica", None, "tensor"),
        P("replica", None, "tensor"),
        P(None, "replica", "tensor"),
        P(None, "replica", "tensor"),
        P(None, "replica", "tensor"),
        P("replica", None, "tensor"),
        P("replica", None, "tensor"),
        P(None, "replica", "tensor"),
        P(None, "replica", "tensor"),
        P(None, "tensor"),
        P("tensor"),
        P("tensor", None),
        P("tensor", None),
        P(None, "tensor"),
        P("tensor"),
        P(None, "tensor"),
        P("tensor"),
        P(),
    )
    out_specs = (
        P(None, "replica", "tensor"),
        P(None, "replica", "tensor"),
        P("replica", None, "tensor"),
        P("replica", None, "tensor"),
    )
    return jax.shard_map(shards, mesh=mesh, in_specs=in_specs, out_specs=out_specs, check_vma=False)
```

time: 101 us -> 68.9 us (0.68)
  blocking collectives: 52.9 us -> 0 us
  starting transfers between devices: 10.1 us -> 36.1 us
  local copies, waits for them, and re-layouts: 13.6 us -> 2.55 us
  waiting for transfers between devices: 3.66 us -> 12 us
  Pallas kernels: 18.8 us -> 16.7 us
    all_to_all x1 -> x0, blocking collectives: 52.9 us -> none  [shards(): lax.all_to_all(send, 'replica', split_axis=0, concat_axis=0, tiled=True)]
    ppermute x0 -> x3, starting transfers between devices: none -> 14.2 us  [the longest x1 7.28 us: shards(): far_small = lax.ppermute(near_small, 'replica', across)]
    unnamed x74 -> x46, local copies, waits for them, and re-layouts: 13.6 us -> 2.55 us
    all_to_all x1 -> x2, starting transfers between devices: 5.09 us -> 12.9 us  [the longest x1 7.39 us: shards(): lax.all_to_all(small, 'replica', split_axis=0, concat_axis=0, tiled=True,...]
    ppermute x3, starting transfers between devices: 5.01 us -> 9.1 us  [shards(): lax.ppermute(sums, 'tensor', [(i, i ^ bit) for i in range(tensors)])]
    ppermute x3, waiting for transfers between devices: 3.66 us -> 6.57 us  [shards(): lax.ppermute(sums, 'tensor', [(i, i ^ bit) for i in range(tensors)])]
    ppermute x0 -> x3, waiting for transfers between devices: none -> 2.72 us  [the longest x1 2.38 us: shards(): other = lax.ppermute(own, 'replica', across)]
    all_to_all x1 -> x2, waiting for transfers between devices: 0.01 us -> 2.7 us  [the longest x1 2.7 us: shards(): lax.all_to_all(small, 'replica', split_axis=0, concat_axis=0, tiled=True,...]
  transfers between devices with their start and end apart: 4 -> 8, of which waited for: 2 -> 6; matrix products, arithmetic and copies ran while one was open for 0% -> 0% of each run, Pallas kernels for 11% -> 15%
where the time goes in v2:
time: 68.9 us; the launch traced here: 68.3 us
  starting transfers between devices  36.1 us (52%)
  Pallas kernels  16.7 us (24%)
  waiting for transfers between devices  12 us (17%)
  local copies, waits for them, and re-layouts  2.55 us (4%)
  between operations  0.92 us (1%)
    ppermute x3, starting transfers between devices, shards(): lax.ppermute(sums, 'tensor', [(i, i ^ bit) for i in range(tensors)])  9.1 us
    all_to_all x1, starting transfers between devices, shards(): lax.all_to_all(small, 'replica', split_axis=0, concat_axis=0, tiled=True,...  7.39 us
    ppermute x1, starting transfers between devices, shards(): far_small = lax.ppermute(near_small, 'replica', across)  7.28 us
    ppermute x1, starting transfers between devices, shards(): far = lax.ppermute(far, 'replica', across)  6.66 us
    ppermute x3, waiting for transfers between devices, shards(): lax.ppermute(sums, 'tensor', [(i, i ^ bit) for i in range(tensors)])  6.57 us
    all_to_all x1, starting transfers between devices, shards(): lax.all_to_all(large, 'replica', split_axis=0, concat_axis=0, tiled=True,...  5.46 us
    pallas_call x1, Pallas kernels, shards(): call(scan_kernel, 'ssvvvvvvvvv', [('d', shape((2, SLOTS, channels), BF)),...  3.14 us
    all_to_all x1, waiting for transfers between devices, shards(): lax.all_to_all(small, 'replica', split_axis=0, concat_axis=0, tiled=True,...  2.7 us
  transfers between devices with their start and end apart: 8, of which 6 were waited for; matrix products, arithmetic and copies ran while one was open for 0% of the time, Pallas kernels for 15%

profile of v2, /device:TPU:8, one launch (start us, length us, event | category | flops | bytes accessed | tf_op | source)
XLA Modules:
  0.0 68.3 jit_solution(10949056905885749249)
XLA Ops:
  0.6 0.0 copy-start.7
  0.6 2.5 %shard_map.220.own._ = bf16[8,48,128]{2,1,0:T(8,128)(2,1)} custom-call(s32[1]{0:T(128)} %bitcast.rep, s32[2,256]{1,0:T(2,128)} %bitcast.11, f32[3,16,1024]{2,1,0:T(8,128)} %bitcast.9, bf16[2,16,1024]{2,1,0:T(8,128)(2,1)} %x.1, bf16[2,16,512]{2,1,0:T(8,128)(2,1)} %q_in.1, bf16[2,16,128]{2,1,0:T(8,128)(2,1)} %nk.3, bf16[2,16,128]{2,1,0:T(8,128)(2,1)} %nv.3), custom_call_target="tpu_custom_call" | custom-call | tf_op jit(solution)/shard_map/pallas_call | solution.py:404
  3.2 0.0 copy-start.5
  3.2 0.0 copy-start.2
  3.2 0.0 copy-start.9
  3.2 0.0 copy-start.10
  3.2 0.0 copy-start.11
  3.2 0.0 copy-start.12
  3.2 0.0 copy-start.13
  3.3 7.3 %collective-permute-start = (bf16[8,48,128]{2,1,0:T(8,128)(2,1)}, bf16[8,48,128]{2,1,0:T(8,128)(2,1)S(1)}, u32[]{:S(2)}, u32[]{:S(2)}) collective-permute-start(bf16[8,48,128]{2,1,0:T(8,128)(2,1)} %shard_map.220.own._), channel_id=1, source_target_pairs={{0,32},{8,40},{16,48},{24,56},{32,0},{40,8},{48,16},{56,24},{64,96... | collective-permute-start | bytes 294920 | tf_op jit(solution)/shard_map/ppermute | solution.py:419
  10.5 2.5 %shard_map.222.own = bf16[8,128,128]{2,1,0:T(8,128)(2,1)} custom-call(s32[1]{0:T(128)} %bitcast.rep, s32[2,256]{1,0:T(2,128)} %bitcast.12, f32[16,16,1024]{2,1,0:T(8,128)} %ssm.3, bf16[8,48,128]{2,1,0:T(8,128)(2,1)} %shard_map.220.own._), custom_call_target="tpu_custom_call" | custom-call | tf_op jit(solution)/shard_map/pallas_call | solution.py:421
  13.1 0.2 collective-permute-start.1
  13.3 0.3 collective-permute-done.other
  13.6 0.0 copy-done.7
  13.6 0.0 copy-done.5
  13.7 1.5 %shard_map.221 = bf16[32,48,128]{2,1,0:T(8,128)(2,1)} custom-call(s32[1]{0:T(128)} %bitcast.rep, s32[2,256]{1,0:T(2,128)S(1)} %bitcast.13, bf16[8,48,128]{2,1,0:T(8,128)(2,1)S(1)} %copy-done.5, bf16[8,48,128]{2,1,0:T(8,128)(2,1)S(1)} %collective-permute-done.other), custom_call_target="tpu_custom_call" | custom-call | tf_op jit(solution)/shard_map/pallas_call | solution.py:430
  15.1 7.4 %all-to-all-start = ((bf16[32,48,128]{2,1,0:T(8,128)(2,1)}), bf16[32,48,128]{2,1,0:T(8,128)(2,1)S(1)}, u32[]{:S(2)}, u32[]{:S(2)}) async-start(bf16[32,48,128]{2,1,0:T(8,128)(2,1)} %shard_map.221), calls=%async_computation | async-start | bytes 786432 | tf_op jit(solution)/shard_map/all_to_all | solution.py:436
  22.5 0.0 copy-done.2
  22.5 0.0 copy-done.9
  22.5 0.0 copy-done.10
  22.5 0.0 copy-done.11
  22.6 0.0 copy-done.12
  22.6 0.0 copy-done.13
  22.6 0.0 copy-start.3
  22.6 1.2 %copy-done.3 = bf16[32,128,128]{2,1,0:T(8,128)(2,1)S(1)} copy-done((bf16[32,128,128]{2,1,0:T(8,128)(2,1)S(1)}, bf16[32,128,128]{2,1,0:T(8,128)(2,1)}, u32[]{:S(2)}) %copy-start.3) | copy-done | bytes 1048600
  23.8 0.0 copy-start
  23.8 1.2 %shard_map.219._.home = f32[128,128]{1,0:T(8,128)S(1)} custom-call(s32[1]{0:T(128)} %bitcast.rep, s32[512]{0:T(512)S(1)} %copy-done.12, s32[2,16]{1,0:T(2,128)S(1)} %bitcast.19, bf16[32,128,128]{2,1,0:T(8,128)(2,1)S(1)} %copy-done.2, bf16[32,128,128]{2,1,0:T(8,128)(2,1)S(1)} %copy-done.3, bf16[2,16,512]{2,1,0:T(8,128)(2,1)S(1)} %copy-done.11, ...), custom_call_target="tpu_custom_call" | custom-call | flops 4000000000 | tf_op jit(solution)/shard_map/pallas_call | solution.py:440
  25.1 2.4 %collective-permute-done.1.other = bf16[8,128,128]{2,1,0:T(8,128)(2,1)S(1)} collective-permute-done((bf16[8,128,128]{2,1,0:T(8,128)(2,1)}, bf16[8,128,128]{2,1,0:T(8,128)(2,1)S(1)}, u32[]{:S(2)}, u32[]{:S(2)}) %collective-permute-start.1) | collective-permute-done | bytes 262176 | tf_op jit(solution)/shard_map/ppermute | solution.py:428
  27.4 2.7 %all-to-all-done.recv = bf16[32,48,128]{2,1,0:T(8,128)(2,1)S(1)} async-done(((bf16[32,48,128]{2,1,0:T(8,128)(2,1)}), bf16[32,48,128]{2,1,0:T(8,128)(2,1)S(1)}, u32[]{:S(2)}, u32[]{:S(2)}) %all-to-all-start) | async-done | bytes 393248 | tf_op jit(solution)/shard_map/all_to_all | solution.py:436
  30.1 0.0 copy-done
  30.1 0.0 copy-start.4
  30.1 1.2 %copy-done.4 = bf16[32,128,128]{2,1,0:T(8,128)(2,1)S(1)} copy-done((bf16[32,128,128]{2,1,0:T(8,128)(2,1)S(1)}, bf16[32,128,128]{2,1,0:T(8,128)(2,1)}, u32[]{:S(2)}) %copy-start.4) | copy-done | bytes 1048600
  31.4 2.2 %shard_map.223 = bf16[32,144,128]{2,1,0:T(8,128)(2,1)} custom-call(s32[1]{0:T(128)} %bitcast.rep, s32[2,256]{1,0:T(2,128)S(1)} %bitcast.14, s32[512]{0:T(512)S(1)} %copy-done.12, s32[2,16]{1,0:T(2,128)S(1)} %bitcast.20, bf16[32,48,128]{2,1,0:T(8,128)(2,1)S(1)} %all-to-all-done.recv, bf16[32,128,128]{2,1,0:T(8,128)(2,1)S(1)} %copy-done.2, ...), custom_call_target="tpu_custom_call" | custom-call | tf_op jit(solution)/shard_map/pallas_call | solution.py:450
  33.6 0.0 copy-start.6
  33.6 0.0 copy-start.19
  33.6 0.0 copy-start.20
  33.6 5.5 %all-to-all-start.1 = ((bf16[32,144,128]{2,1,0:T(8,128)(2,1)}), bf16[32,144,128]{2,1,0:T(8,128)(2,1)S(1)}, u32[]{:S(2)}, u32[]{:S(2)}) async-start(bf16[32,144,128]{2,1,0:T(8,128)(2,1)} %shard_map.223), calls=%async_computation.1 | async-start | bytes 2359296 | tf_op jit(solution)/shard_map/all_to_all | solution.py:463
  39.1 0.0 copy-done.6
  39.1 0.0 copy-done.8
  39.1 0.0 copy-done.14
  39.1 0.0 copy-done.16
  39.1 0.0 copy-done.19
  39.1 0.0 copy-done.20
  39.1 1.7 %shard_map.226 = (f32[64,256]{1,0:T(8,128)S(1)}, f32[48,1024]{1,0:T(8,128)S(1)}, f32[3,16,1024]{2,1,0:T(8,128)}) custom-call(s32[1]{0:T(128)} %bitcast.rep, s32[2,256]{1,0:T(2,128)S(1)} %bitcast.15, bf16[32,48,128]{2,1,0:T(8,128)(2,1)S(1)} %all-to-all-done.recv, f32[3,16,1024]{2,1,0:T(8,128)S(1)} %bitcast.10, bf16[2,16,1024]{2,1,0:T(8,128)(2,1)S(1)} %copy-done.8, ...), custom_call_target="tpu_custom_call" | custom-call | flops 2000000000 | tf_op jit(solution)/shard_map/pallas_call | solution.py:467
  40.8 0.0 copy-start.21
  40.9 0.0 copy-start.22
  40.9 0.1 collective-permute-start.3
  41.0 1.2 %collective-permute-done.3 = f32[64,256]{1,0:T(8,128)S(1)} collective-permute-done((f32[64,256]{1,0:T(8,128)S(1)}, f32[64,256]{1,0:T(8,128)S(1)}, u32[]{:S(2)}, u32[]{:S(2)}) %collective-permute-start.3) | collective-permute-done | bytes 65568 | tf_op jit(solution)/shard_map/ppermute | solution.py:480
  42.2 3.7 %collective-permute-start.4 = (f32[64,256]{1,0:T(8,128)S(1)}, f32[64,256]{1,0:T(8,128)S(1)}, u32[]{:S(2)}, u32[]{:S(2)}) collective-permute-start(f32[64,256]{1,0:T(8,128)S(1)} %add.9), channel_id=1, source_target_pairs={{0,2},{1,3},{2,0},{3,1},{4,6},{5,7},{6,4},{7,5},{8,10},{9,11},{10,... | collective-permute-start | bytes 196616 | tf_op jit(solution)/shard_map/ppermute | solution.py:480
  45.9 2.4 %collective-permute-done.4 = f32[64,256]{1,0:T(8,128)S(1)} collective-permute-done((f32[64,256]{1,0:T(8,128)S(1)}, f32[64,256]{1,0:T(8,128)S(1)}, u32[]{:S(2)}, u32[]{:S(2)}) %collective-permute-start.4) | collective-permute-done | bytes 65568 | tf_op jit(solution)/shard_map/ppermute | solution.py:480
  48.4 5.3 %collective-permute-start.5 = (f32[64,256]{1,0:T(8,128)S(1)}, f32[64,256]{1,0:T(8,128)S(1)}, u32[]{:S(2)}, u32[]{:S(2)}) collective-permute-start(f32[64,256]{1,0:T(8,128)S(1)} %add.10), channel_id=1, source_target_pairs={{0,4},{1,5},{2,6},{3,7},{4,0},{5,1},{6,2},{7,3},{8,12},{9,13},{10,... | collective-permute-start | bytes 196616 | tf_op jit(solution)/shard_map/ppermute | solution.py:480
  53.7 2.9 %collective-permute-done.5 = f32[64,256]{1,0:T(8,128)S(1)} collective-permute-done((f32[64,256]{1,0:T(8,128)S(1)}, f32[64,256]{1,0:T(8,128)S(1)}, u32[]{:S(2)}, u32[]{:S(2)}) %collective-permute-start.5) | collective-permute-done | bytes 65568 | tf_op jit(solution)/shard_map/ppermute | solution.py:480
  56.6 0.0 all-to-all-done.1.recv
  56.6 0.6 shard_map.224
  57.2 6.7 %collective-permute-start.2 = (bf16[8,16,128]{2,1,0:T(8,128)(2,1)S(1)}, bf16[8,16,128]{2,1,0:T(8,128)(2,1)S(1)}, u32[]{:S(2)}, u32[]{:S(2)}) collective-permute-start(bf16[8,16,128]{2,1,0:T(8,128)(2,1)S(1)} %shard_map.224), channel_id=1, source_target_pairs={{0,32},{8,40},{16,48},{24,56},{32,0},{40,8},{48,16},{56,24},{64,96... | collective-permute-start | bytes 98312 | tf_op jit(solution)/shard_map/ppermute | solution.py:489
  63.9 0.0 copy-done.1
  63.9 0.0 copy-done.15
  63.9 0.0 copy-done.17
  63.9 0.0 copy-done.18
  63.9 0.0 copy-done.21
  63.9 0.0 copy-done.22
  63.9 3.1 %shard_map.227 = (bf16[2,16,1024]{2,1,0:T(8,128)(2,1)}, f32[16,16,1024]{2,1,0:T(8,128)}) custom-call(s32[1]{0:T(128)} %bitcast.rep, s32[2,256]{1,0:T(2,128)S(1)} %bitcast.17, f32[64,256]{1,0:T(8,128)S(1)} %add.11.sums, f32[48,1024]{1,0:T(8,128)S(1)} %get-tuple-element.10.mixed, bf16[32,144,128]{2,1,0:T(8,128)(2,1)S(1)} %all-to-all-done.1.recv, ...), custom_call_target="tpu_custom_call" | custom-call | flops 3000000000 | tf_op jit(solution)/shard_map/pallas_call | solution.py:491
  67.1 0.0 collective-permute-done.2.other
  67.1 1.3 %shard_map.225 = bf16[2,16,512]{2,1,0:T(8,128)(2,1)} custom-call(s32[1]{0:T(128)} %bitcast.rep, s32[2,256]{1,0:T(2,128)S(1)} %bitcast.18, f32[128,128]{1,0:T(8,128)S(1)} %shard_map.219._.home, bf16[32,144,128]{2,1,0:T(8,128)(2,1)S(1)} %all-to-all-done.1.recv, bf16[8,16,128]{2,1,0:T(8,128)(2,1)S(1)} %collective-permute-done.2.other), custom_call_target="tpu_custom_call" | custom-call | tf_op jit(solution)/shard_map/pallas_call | solution.py:506
  (10 shorter events, 0.0 us)
Async XLA Ops:
  0.6 13.0 %copy-start.7 = (s32[256,2]{0,1:T(2,128)S(1)}, s32[256,2]{0,1:T(2,128)}, u32[]{:S(2)}) copy-start(s32[256,2]{0,1:T(2,128)} %param.39) | copy-start | bytes 6148
  3.2 10.5 %copy-start.5 = (bf16[8,48,128]{2,1,0:T(8,128)(2,1)S(1)}, bf16[8,48,128]{2,1,0:T(8,128)(2,1)}, u32[]{:S(2)}) copy-start(bf16[8,48,128]{2,1,0:T(8,128)(2,1)} %shard_map.220.own._) | copy-start | bytes 294916
  3.2 19.3 %copy-start.2 = (bf16[32,128,128]{2,1,0:T(8,128)(2,1)S(1)}, bf16[32,128,128]{2,1,0:T(8,128)(2,1)}, u32[]{:S(2)}) copy-start(bf16[32,128,128]{2,1,0:T(8,128)(2,1)} %keys.3) | copy-start | bytes 3145732
  3.2 19.3 %copy-start.9 = (bf16[2,16,128]{2,1,0:T(8,128)(2,1)S(1)}, bf16[2,16,128]{2,1,0:T(8,128)(2,1)}, u32[]{:S(2)}) copy-start(bf16[2,16,128]{2,1,0:T(8,128)(2,1)} %nk.3) | copy-start | bytes 24580
  3.2 19.3 %copy-start.10 = (bf16[2,16,128]{2,1,0:T(8,128)(2,1)S(1)}, bf16[2,16,128]{2,1,0:T(8,128)(2,1)}, u32[]{:S(2)}) copy-start(bf16[2,16,128]{2,1,0:T(8,128)(2,1)} %nv.3) | copy-start | bytes 24580
  3.2 19.3 %copy-start.11 = (bf16[2,16,512]{2,1,0:T(8,128)(2,1)S(1)}, bf16[2,16,512]{2,1,0:T(8,128)(2,1)}, u32[]{:S(2)}) copy-start(bf16[2,16,512]{2,1,0:T(8,128)(2,1)} %q_in.1) | copy-start | bytes 98308
  3.2 19.3 %copy-start.12 = (s32[512]{0:T(512)S(1)}, s32[512]{0:T(512)}, u32[]{:S(2)}) copy-start(s32[512]{0:T(512)} %lens.3) | copy-start | bytes 6148
  3.2 19.3 %copy-start.13 = (s32[16,2]{0,1:T(2,128)S(1)}, s32[16,2]{0,1:T(2,128)}, u32[]{:S(2)}) copy-start(s32[16,2]{0,1:T(2,128)} %param.21) | copy-start | bytes 388
  3.3 10.4 %collective-permute-start = (bf16[8,48,128]{2,1,0:T(8,128)(2,1)}, bf16[8,48,128]{2,1,0:T(8,128)(2,1)S(1)}, u32[]{:S(2)}, u32[]{:S(2)}) collective-permute-start(bf16[8,48,128]{2,1,0:T(8,128)(2,1)} %shard_map.220.own._), channel_id=1, source_target_pairs={{0,32},{8,40},{16,48},{24,56},{32,0},{40,8},{48,16},{56,24},{64,96... | collective-permute-start | bytes 294920 | tf_op jit(solution)/shard_map/ppermute | solution.py:419
  13.1 14.4 %collective-permute-start.1 = (bf16[8,128,128]{2,1,0:T(8,128)(2,1)}, bf16[8,128,128]{2,1,0:T(8,128)(2,1)S(1)}, u32[]{:S(2)}, u32[]{:S(2)}) collective-permute-start(bf16[8,128,128]{2,1,0:T(8,128)(2,1)} %shard_map.222.own), channel_id=1, source_target_pairs={{0,32},{8,40},{16,48},{24,56},{32,0},{40,8},{48,16},{56,24},{64,96... | collective-permute-start | bytes 786440 | tf_op jit(solution)/shard_map/ppermute | solution.py:428
  15.1 15.0 %all-to-all-start = ((bf16[32,48,128]{2,1,0:T(8,128)(2,1)}), bf16[32,48,128]{2,1,0:T(8,128)(2,1)S(1)}, u32[]{:S(2)}, u32[]{:S(2)}) async-start(bf16[32,48,128]{2,1,0:T(8,128)(2,1)} %shard_map.221), calls=%async_computation | async-start | bytes 786432 | tf_op jit(solution)/shard_map/all_to_all | solution.py:436
  22.6 1.2 %copy-start.3 = (bf16[32,128,128]{2,1,0:T(8,128)(2,1)S(1)}, bf16[32,128,128]{2,1,0:T(8,128)(2,1)}, u32[]{:S(2)}) copy-start(bf16[32,128,128]{2,1,0:T(8,128)(2,1)} %values.3) | copy-start | bytes 3145732
  23.8 6.3 %copy-start = (bf16[8,128,128]{2,1,0:T(8,128)(2,1)S(1)}, bf16[8,128,128]{2,1,0:T(8,128)(2,1)}, u32[]{:S(2)}) copy-start(bf16[8,128,128]{2,1,0:T(8,128)(2,1)} %shard_map.222.own) | copy-start | bytes 786436
  30.1 1.2 %copy-start.4 = (bf16[32,128,128]{2,1,0:T(8,128)(2,1)S(1)}, bf16[32,128,128]{2,1,0:T(8,128)(2,1)}, u32[]{:S(2)}) copy-start(bf16[32,128,128]{2,1,0:T(8,128)(2,1)} %values.3) | copy-start | bytes 3145732
  33.6 5.5 %copy-start.6 = (f32[16,3,1024]{2,0,1:T(8,128)S(1)}, f32[16,3,1024]{2,0,1:T(8,128)}, u32[]{:S(2)}) copy-start(f32[16,3,1024]{2,0,1:T(8,128)} %param.27) | copy-start | bytes 589828
  33.6 5.5 %copy-start.8 = (bf16[2,16,1024]{2,1,0:T(8,128)(2,1)S(1)}, bf16[2,16,1024]{2,1,0:T(8,128)(2,1)}, u32[]{:S(2)}) copy-start(bf16[2,16,1024]{2,1,0:T(8,128)(2,1)} %x.1) | copy-start | bytes 196612
  33.6 5.5 %copy-start.14 = (bf16[1024,256]{1,0:T(8,128)(2,1)S(1)}, bf16[1024,256]{1,0:T(8,128)(2,1)}, u32[]{:S(2)}) copy-start(bf16[1024,256]{1,0:T(8,128)(2,1)} %down.1) | copy-start | bytes 1572868
  33.6 5.5 %copy-start.16 = (bf16[1024,32]{0,1:T(8,128)(2,1)S(1)}, bf16[1024,32]{0,1:T(8,128)(2,1)}, u32[]{:S(2)}) copy-start(bf16[1024,32]{0,1:T(8,128)(2,1)} %param.34) | copy-start | bytes 196612
  33.6 5.5 %copy-start.19 = (f32[4,1024]{1,0:T(4,128)S(1)}, f32[4,1024]{1,0:T(4,128)}, u32[]{:S(2)}) copy-start(f32[4,1024]{1,0:T(4,128)} %cw.1) | copy-start | bytes 49156
  33.6 5.5 %copy-start.20 = (f32[1024]{0:T(1024)S(1)}, f32[1024]{0:T(1024)}, u32[]{:S(2)}) copy-start(f32[1024]{0:T(1024)} %param.32) | copy-start | bytes 12292
  33.6 23.0 %all-to-all-start.1 = ((bf16[32,144,128]{2,1,0:T(8,128)(2,1)}), bf16[32,144,128]{2,1,0:T(8,128)(2,1)S(1)}, u32[]{:S(2)}, u32[]{:S(2)}) async-start(bf16[32,144,128]{2,1,0:T(8,128)(2,1)} %shard_map.223), calls=%async_computation.1 | async-start | bytes 2359296 | tf_op jit(solution)/shard_map/all_to_all | solution.py:463
  40.8 23.0 %copy-start.1 = (f32[16,16,1024]{2,1,0:T(8,128)S(1)}, f32[16,16,1024]{2,1,0:T(8,128)}, u32[]{:S(2)}) copy-start(f32[16,16,1024]{2,1,0:T(8,128)} %ssm.3) | copy-start | bytes 3145732
  40.8 23.0 %copy-start.15 = (bf16[256,1024]{1,0:T(8,128)(2,1)S(1)}, bf16[256,1024]{1,0:T(8,128)(2,1)}, u32[]{:S(2)}) copy-start(bf16[256,1024]{1,0:T(8,128)(2,1)} %up.1) | copy-start | bytes 1572868
  40.8 23.0 %copy-start.17 = (bf16[2,16,1024]{2,1,0:T(8,128)(2,1)S(1)}, bf16[2,16,1024]{2,1,0:T(8,128)(2,1)}, u32[]{:S(2)}) copy-start(bf16[2,16,1024]{2,1,0:T(8,128)(2,1)} %z.1) | copy-start | bytes 196612
  40.8 23.0 %copy-start.18 = (f32[16,1024]{1,0:T(8,128)S(1)}, f32[16,1024]{1,0:T(8,128)}, u32[]{:S(2)}) copy-start(f32[16,1024]{1,0:T(8,128)} %alog.1) | copy-start | bytes 196612
  40.8 23.0 %copy-start.21 = (f32[1024]{0:T(1024)S(1)}, f32[1024]{0:T(1024)}, u32[]{:S(2)}) copy-start(f32[1024]{0:T(1024)} %param.36) | copy-start | bytes 12292
  40.9 23.0 %copy-start.22 = (f32[1024]{0:T(1024)S(1)}, f32[1024]{0:T(1024)}, u32[]{:S(2)}) copy-start(f32[1024]{0:T(1024)} %param.38) | copy-start | bytes 12292
  40.9 1.3 %collective-permute-start.3 = (f32[64,256]{1,0:T(8,128)S(1)}, f32[64,256]{1,0:T(8,128)S(1)}, u32[]{:S(2)}, u32[]{:S(2)}) collective-permute-start(f32[64,256]{1,0:T(8,128)S(1)} %get-tuple-element.9), channel_id=1, source_target_pairs={{0,1},{1,0},{2,3},{3,2},{4,5},{5,4},{6,7},{7,6},{8,9},{9,8},{10,11... | collective-permute-start | bytes 196616 | tf_op jit(solution)/shard_map/ppermute | solution.py:480
  42.2 6.1 %collective-permute-start.4 = (f32[64,256]{1,0:T(8,128)S(1)}, f32[64,256]{1,0:T(8,128)S(1)}, u32[]{:S(2)}, u32[]{:S(2)}) collective-permute-start(f32[64,256]{1,0:T(8,128)S(1)} %add.9), channel_id=1, source_target_pairs={{0,2},{1,3},{2,0},{3,1},{4,6},{5,7},{6,4},{7,5},{8,10},{9,11},{10,... | collective-permute-start | bytes 196616 | tf_op jit(solution)/shard_map/ppermute | solution.py:480
  48.4 8.2 %collective-permute-start.5 = (f32[64,256]{1,0:T(8,128)S(1)}, f32[64,256]{1,0:T(8,128)S(1)}, u32[]{:S(2)}, u32[]{:S(2)}) collective-permute-start(f32[64,256]{1,0:T(8,128)S(1)} %add.10), channel_id=1, source_target_pairs={{0,4},{1,5},{2,6},{3,7},{4,0},{5,1},{6,2},{7,3},{8,12},{9,13},{10,... | collective-permute-start | bytes 196616 | tf_op jit(solution)/shard_map/ppermute | solution.py:480
  57.2 9.8 %collective-permute-start.2 = (bf16[8,16,128]{2,1,0:T(8,128)(2,1)S(1)}, bf16[8,16,128]{2,1,0:T(8,128)(2,1)S(1)}, u32[]{:S(2)}, u32[]{:S(2)}) collective-permute-start(bf16[8,16,128]{2,1,0:T(8,128)(2,1)S(1)} %shard_map.224), channel_id=1, source_target_pairs={{0,32},{8,40},{16,48},{24,56},{32,0},{40,8},{48,16},{56,24},{64,96... | collective-permute-start | bytes 98312 | tf_op jit(solution)/shard_map/ppermute | solution.py:489

commit v3 on v2

v3 whole, which is shorter than its diff:
```python
import functools
import math

import jax
import jax.numpy as jnp
from jax import lax
from jax.experimental import pallas as pl
from jax.experimental.pallas import tpu as pltpu
from jax.sharding import PartitionSpec as P

HD = 128
SLOTS = 16
MOVES = 8
HEADS = 4
DS = 16
PIECES = 8
STATE_ROWS = DS * PIECES
PAIR_ROWS = 2 * PIECES
SMALL_ROWS = PAIR_ROWS + 16
HELD_ROWS = STATE_ROWS + PAIR_ROWS
LARGE_ROWS = HELD_ROWS + 16
REPLICAS = 32
FAR = 4
PLANE = 16
BF = jnp.bfloat16
F32 = jnp.float32

SPECS = {
    "s": pl.BlockSpec(memory_space=pltpu.SMEM),
    "v": pl.BlockSpec(memory_space=pltpu.VMEM),
    "d": pl.BlockSpec(),
    "a": pl.BlockSpec(memory_space=pl.ANY),
}


def out_move(me, moves, j):
    row = me * MOVES + j
    return moves[0, row] & (SLOTS - 1), lax.shift_right_logical(moves[1, row], 4)


def in_move(me, moves, j):
    target = lax.shift_right_logical(moves[1, me * MOVES + j], 4)
    source = (2 * me - target + REPLICAS) & (REPLICAS - 1)
    return moves[1, source * MOVES + j] & (SLOTS - 1), source


def crosses(one, other):
    return lax.shift_right_logical((one ^ other) & FAR, 2)


def place(replica):
    return lax.shift_left(lax.shift_right_logical(replica, 3), 2) | (replica & 3)


def silu(value):
    return value / (1.0 + jnp.exp(-value))


def cut(rows):
    return [row[:, c * HD : (c + 1) * HD] for row in rows for c in range(PIECES)]


def whole(rows, k):
    pieces = [rows[pl.ds(k * PIECES + c, SLOTS, stride=PAIR_ROWS), :] for c in range(PIECES)]
    return jnp.concatenate(pieces, axis=1)


def pack_small_kernel(
    rep, moves, conv_in, x_in, q_in, nk_in, nv_in, cw_in, cb_in, send, conv, x, q, nk, nv, cw, cb, small, read
):
    me = rep[0]
    pairs = (
        (conv_in, conv),
        (x_in.at[0], x),
        (q_in.at[1], q),
        (nk_in.at[1], nk),
        (nv_in.at[1], nv),
        (cw_in, cw),
        (cb_in, cb),
    )
    copies = [
        pltpu.make_async_copy(source, target, read.at[i])
        for i, (source, target) in enumerate(pairs)
    ]
    for copy in copies:
        copy.start()
    for copy in copies:
        copy.wait()
    zero = jnp.zeros((SLOTS, HD), F32)
    x0 = x[...].astype(F32)
    tap = [cw[k : k + 1, :] for k in range(4)]
    bias = cb[...]
    mixed = silu(conv[0] * tap[0] + conv[1] * tap[1] + conv[2] * tap[2] + x0 * tap[3] + bias)
    later = conv[1] * tap[0] + conv[2] * tap[1] + x0 * tap[2] + bias
    pieces = cut([mixed, later])
    pieces += [nk[...].astype(F32), nv[...].astype(F32), zero, zero]
    pieces += [q[:, h * HD : (h + 1) * HD].astype(F32) for h in range(HEADS)]
    width = PAIR_ROWS + 8
    for i in range(width):
        small[pl.ds(i, SLOTS, stride=width), :] = pieces[i]
    back = []
    for j in range(MOVES):
        slot, _ = out_move(me, moves, j)
        start = pl.multiple_of(slot * width, 8)
        send[j * 16 : j * 16 + 16, :] = small[pl.ds(start, PAIR_ROWS), :].astype(BF)
        slot, _ = in_move(me, moves, j)
        start = pl.multiple_of(slot * width + PAIR_ROWS, 8)
        back.append(small[pl.ds(start, 8), :])
    for j in range(0, MOVES, 2):
        start = MOVES * 16 + j * 8
        send[start : start + 16, :] = jnp.concatenate(back[j : j + 2], axis=0).astype(BF)


def route_small_kernel(rep, moves, own, other, send):
    me = rep[0]
    blank = jnp.zeros((8, HD), F32)
    for j in range(MOVES):
        _, target = out_move(me, moves, j)
        flip = crosses(me, target)
        _, target = out_move(me ^ (flip * FAR), moves, j)
        to = place(target) * 2 + flip
        lines = slice(j * 16, j * 16 + 16)
        send[to, :PAIR_ROWS, :] = jnp.where(flip == 1, other[lines, :], own[lines, :])
        _, source = in_move(me, moves, j)
        flip = crosses(me, source)
        _, source = in_move(me ^ (flip * FAR), moves, j)
        to = place(source) * 2 + flip
        start = MOVES * 16 + j // 2 * 16
        lines = slice(start, start + 16)
        both = jnp.where(flip == 1, other[lines, :], own[lines, :]).astype(F32)
        part = both[j % 2 * 8 : j % 2 * 8 + 8, :]
        send[to, PAIR_ROWS:, :] = jnp.concatenate([part, blank], axis=0).astype(BF)


def pack_state_kernel(rep, moves, ssm, conv_in, x_in, _, send, held, conv, x, small, arrived, read):
    me = rep[0]
    copies = []
    for j in range(MOVES):
        slot, _ = out_move(me, moves, j)
        copies.append(pltpu.make_async_copy(ssm.at[slot], held.at[j], arrived.at[j]))
    copies.append(pltpu.make_async_copy(conv_in.at[2], conv, read.at[0]))
    copies.append(pltpu.make_async_copy(x_in.at[0], x, read.at[1]))
    for copy in copies:
        copy.start()
    for copy in copies:
        copy.wait()
    for i, piece in enumerate(cut([conv[...], x[...].astype(F32)])):
        small[pl.ds(i, SLOTS, stride=PAIR_ROWS), :] = piece
    for j in range(MOVES):
        for c in range(PIECES):
            send[j, c * DS : (c + 1) * DS, :] = held[j, :, c * HD : (c + 1) * HD].astype(BF)
        slot, _ = out_move(me, moves, j)
        start = pl.multiple_of(slot * PAIR_ROWS, 16)
        send[j, STATE_ROWS:, :] = small[pl.ds(start, PAIR_ROWS), :].astype(BF)


NT = (((1,), (1,)), ((), ()))
SCALE = 1.0 / math.sqrt(HD)


def spread(rows, value):
    for h in range(8):
        rows[pl.ds(h, SLOTS, stride=8), :] = value


def attend_slots(slots, qs, first_k, first_v, next_k, next_v, both, score, limit, result):
    count = len(slots)
    wide = qs[...]
    for i, (length, keys, _) in enumerate(slots):
        score[i * 8 : i * 8 + 8, :] = lax.dot_general(
            wide[i * 8 : i * 8 + 8, :].astype(BF), keys(), NT, preferred_element_type=F32
        )
        limit[i * 8 : i * 8 + 8, :] = jnp.full((8, HD), length, jnp.int32)
    position = lax.broadcasted_iota(jnp.int32, (count * 8, HD), 1)
    ends = limit[...]
    score0 = jnp.where(position < ends, score[:, :HD] * SCALE, -1e30)
    score1 = jnp.where(position + HD < ends, score[:, HD:] * SCALE, -1e30)
    extra0 = jnp.sum(wide * first_k, axis=1, keepdims=True) * SCALE
    extra1 = jnp.sum(wide * next_k, axis=1, keepdims=True) * SCALE
    if both:
        row = lax.broadcasted_iota(jnp.int32, (count * 8, 1), 0) & 7
        extra1 = jnp.where(row >= HEADS, extra1, -1e30)
    largest = jnp.max(jnp.maximum(score0, score1), axis=1, keepdims=True)
    largest = jnp.maximum(largest, jnp.maximum(extra0, extra1))
    part0 = jnp.exp(score0 - largest)
    part1 = jnp.exp(score1 - largest)
    new0 = jnp.exp(extra0 - largest)
    new1 = jnp.exp(extra1 - largest)
    total = jnp.sum(part0 + part1, axis=1, keepdims=True) + new0 + new1
    score[:, :HD] = part0 / total
    score[:, HD:] = part1 / total
    new0 = (new0 / total).astype(BF).astype(F32)
    new1 = (new1 / total).astype(BF).astype(F32)
    added = new0 * first_v + new1 * next_v
    for i, (_, _, values) in enumerate(slots):
        result[i * 8 : i * 8 + 8, :] = (
            jnp.dot(score[i * 8 : i * 8 + 8, :].astype(BF), values(), preferred_element_type=F32)
            + added[i * 8 : i * 8 + 8, :]
        )


def attend_home_kernel(
    rep, moves, lens, pages, keys, values, q, nk, nv, result, kept, qs, fk, fv, gk, gv, score, limit
):
    me = rep[0]
    for step in range(2):
        for h in range(HEADS):
            qs[pl.ds(step * HEADS + h, SLOTS, stride=8), :] = q[
                step, :, h * HD : (h + 1) * HD
            ].astype(F32)
    spread(fk, nk[0].astype(F32))
    spread(fv, nv[0].astype(F32))
    spread(gk, nk[1].astype(F32))
    spread(gv, nv[1].astype(F32))

    def both_pages(pool, slot):
        return jnp.concatenate([pool[pages[0, slot]], pool[pages[1, slot]]], axis=0)

    slots = [
        (
            lens[me * SLOTS + s],
            functools.partial(both_pages, keys, s),
            functools.partial(both_pages, values, s),
        )
        for s in range(SLOTS)
    ]
    attend_slots(slots, qs, fk[...], fv[...], gk[...], gv[...], True, score, limit, result)
    for j in range(MOVES):
        slot, _ = out_move(me, moves, j)
        kept[j, 0] = both_pages(keys, slot)
        kept[j, 1] = both_pages(values, slot)


def attend_away_kernel(
    rep, moves, lens, recv, kept, nk, nv, send, qs, fk, fv, score, limit, result
):
    me = rep[0]
    spread(fk, nk[0].astype(F32))
    spread(fv, nv[0].astype(F32))
    slots = []
    first_k, first_v, next_k, next_v = [], [], [], []
    for j in range(MOVES):
        slot, target = out_move(me, moves, j)
        flip = crosses(me, target)
        got = recv[place(target) * 2 + flip, PAIR_ROWS:, :].astype(F32)[:8, :]
        qs[j * 8 : j * 8 + 8, :] = got
        start = pl.multiple_of(slot * 8, 8)
        first_k.append(fk[pl.ds(start, 8), :])
        first_v.append(fv[pl.ds(start, 8), :])
        next_k.append(jnp.broadcast_to(got[0:1, :], (8, HD)))
        next_v.append(jnp.broadcast_to(got[1:2, :], (8, HD)))
        slots.append(
            (
                lens[me * SLOTS + slot],
                functools.partial(lambda i: kept[i, 0], j),
                functools.partial(lambda i: kept[i, 1], j),
            )
        )
    join = functools.partial(jnp.concatenate, axis=0)
    attend_slots(
        slots, qs, join(first_k), join(first_v), join(next_k), join(next_v), False, score, limit, result
    )
    send[...] = result[...].astype(BF)


def route_large_kernel(rep, moves, own, other, near, far, send):
    me = rep[0]
    blank = jnp.zeros((8, HD), F32)
    for j in range(MOVES):
        _, target = out_move(me, moves, j)
        flip = crosses(me, target)
        _, target = out_move(me ^ (flip * FAR), moves, j)
        to = place(target) * 2 + flip
        send[to, :HELD_ROWS, :] = jnp.where(flip == 1, other[j], own[j])
        lines = slice(j // 2 * 16, j // 2 * 16 + 16)
        both = jnp.where(flip == 1, far[lines, :], near[lines, :]).astype(F32)
        part = both[j % 2 * 8 : j % 2 * 8 + 8, :]
        send[to, HELD_ROWS:, :] = jnp.concatenate([part, blank], axis=0).astype(BF)


def project_kernel(rep, moves, recv, conv, x, cw, cb, down, bct, sums, mixed, rows):
    me = rep[0]
    x0 = x[0].astype(F32)
    x1 = x[1].astype(F32)
    tap = [cw[k : k + 1, :] for k in range(4)]
    bias = cb[...]
    now = silu(conv[0] * tap[0] + conv[1] * tap[1] + conv[2] * tap[2] + x0 * tap[3] + bias)
    later = conv[1] * tap[0] + conv[2] * tap[1] + x0 * tap[2] + bias
    for i, piece in enumerate(cut([now, later])):
        rows[pl.ds(i, SLOTS, stride=PAIR_ROWS), :] = piece
    for j in range(MOVES):
        slot, source = in_move(me, moves, j)
        start = pl.multiple_of(slot * PAIR_ROWS, PAIR_ROWS)
        came = recv[place(source) * 2 + crosses(me, source), :PAIR_ROWS, :]
        rows[pl.ds(start, PAIR_ROWS), :] = came.astype(F32)
    mixed[0:16] = now
    mixed[16:32] = whole(rows, 0)
    mixed[32:48] = silu(whole(rows, 1) + x1 * tap[3])
    narrow = mixed[...].astype(BF)
    mixed[...] = narrow.astype(F32)
    sums[0:48, :] = jnp.dot(narrow, down[...], preferred_element_type=F32)
    maps = lax.dot_general(
        bct[...], narrow, (((1,), (1,)), ((), ())), preferred_element_type=F32
    )
    sums[48:64, :] = jnp.zeros((16, 256), F32)
    sums[48:64, 0:48] = maps[0:DS]
    sums[48:64, 128:176] = maps[DS:]


def advance(state, sums, step, mixed, rate, row):
    dts = step[row : row + 1, :]
    grown = jnp.exp(dts * rate) * state
    b = sums[48:64, row : row + 1]
    return grown + b * (dts * mixed[row : row + 1, :])


def read(state, sums, row):
    c = sums[48:64, 128 + row : 129 + row]
    return jnp.sum(c * state, axis=0, keepdims=True)


def first_scan_kernel(sums, mixed, ssm, z, up, db, alog, skip, step, states, out, yrows):
    dt = jnp.dot(sums[0:48, :].astype(BF), up[...], preferred_element_type=F32) + db[...]
    step[...] = jnp.maximum(dt, 0.0) + jnp.log1p(jnp.exp(-jnp.abs(dt)))
    rate = -jnp.exp(alog[...])
    for s in range(SLOTS):
        state = advance(ssm[s], sums, step, mixed, rate, s)
        states[s] = state
        yrows[s : s + 1, :] = read(state, sums, s)
    out[...] = ((yrows[...] + skip[...] * mixed[0:16]) * silu(z[0].astype(F32))).astype(BF)


def last_scan_kernel(
    rep,
    moves,
    sums,
    mixed,
    step,
    states,
    first,
    recv,
    z,
    alog,
    skip,
    conv,
    x,
    home,
    out,
    final,
    last,
    attention,
    held,
    yrows,
    rows,
    lines,
    origin,
    left,
):
    me = rep[0]
    for s in range(SLOTS):
        origin[s] = -1
    for i, piece in enumerate(cut([conv[...], x[0].astype(F32)])):
        rows[pl.ds(i, SLOTS, stride=PAIR_ROWS), :] = piece
    lines[...] = home[...]
    second = lax.broadcasted_iota(jnp.int32, (8, HD), 0) >= HEADS
    for j in range(MOVES):
        slot, source = in_move(me, moves, j)
        index = place(source) * 2 + crosses(me, source)
        origin[slot] = index
        start = pl.multiple_of(slot * PAIR_ROWS, PAIR_ROWS)
        rows[pl.ds(start, PAIR_ROWS), :] = recv[index, STATE_ROWS:HELD_ROWS, :].astype(F32)
        came = recv[index, HELD_ROWS:, :].astype(F32)[:8, :]
        start = pl.multiple_of(slot * 8, 8)
        lines[pl.ds(start, 8), :] = jnp.where(second, came, lines[pl.ds(start, 8), :])
    rate = -jnp.exp(alog[...])
    copies = []
    for s in range(SLOTS):
        source = origin[s]
        came = recv.at[jnp.maximum(source, 0)]
        moved = jnp.concatenate(
            [came[c * DS : (c + 1) * DS, :] for c in range(PIECES)], axis=1
        ).astype(F32)
        moved = advance(moved, sums, step, mixed, rate, 16 + s)
        state = jnp.where(source >= 0, moved, states[s])
        state = advance(state, sums, step, mixed, rate, 32 + s)
        held[s] = state
        copies.append(pltpu.make_async_copy(held.at[s], final.at[s], left.at[s]))
        copies[s].start()
        yrows[s : s + 1, :] = read(state, sums, 32 + s)
    last[0] = whole(rows, 0)
    last[1] = whole(rows, 1)
    last[2] = x[1].astype(F32)
    out[0] = first[...]
    out[1] = ((yrows[...] + skip[...] * mixed[32:48]) * silu(z[1].astype(F32))).astype(BF)
    for step_number in range(2):
        for h in range(HEADS):
            attention[step_number, :, h * HD : (h + 1) * HD] = lines[
                pl.ds(step_number * HEADS + h, SLOTS, stride=8), :
            ].astype(BF)
    for copy in copies:
        copy.wait()


def call(kernel, kinds, outs, scratch, flops=0, room=32):
    outs_specs = [SPECS[kind] for kind, _ in outs]
    shapes = [shape for _, shape in outs]
    return pl.pallas_call(
        kernel,
        in_specs=[SPECS[kind] for kind in kinds],
        out_specs=outs_specs if len(outs) > 1 else outs_specs[0],
        out_shape=shapes if len(outs) > 1 else shapes[0],
        scratch_shapes=scratch,
        cost_estimate=pl.CostEstimate(flops=flops, bytes_accessed=0, transcendentals=0),
        compiler_params=pltpu.CompilerParams(vmem_limit_bytes=room * 1024 * 1024),
    )


def shards(
    lengths,
    page_table,
    key_pool,
    value_pool,
    queries,
    new_keys,
    new_values,
    conv_state,
    ssm_state,
    mamba_x,
    mamba_z,
    conv_weight,
    conv_bias,
    dt_down,
    bc_proj,
    dt_up,
    dt_bias,
    a_log,
    skip_d,
    moves,
):
    tensors = lax.axis_size("tensor")
    channels = ssm_state.shape[2]
    rep = lax.axis_index("replica").astype(jnp.int32).reshape(1)
    moves = moves.T
    pages = page_table.T
    conv = conv_state.transpose(1, 0, 2)
    shape = jax.ShapeDtypeStruct
    across = [(i, i ^ FAR) for i in range(REPLICAS)]
    planes = [[i for i in range(REPLICAS) if i & FAR == side] for side in (0, FAR)]
    rows = SLOTS * 8

    near_small = call(
        pack_small_kernel,
        "ssaaaaaaa",
        [("v", shape((MOVES * 24, HD), BF))],
        [
            pltpu.VMEM((3, SLOTS, channels), F32),
            pltpu.VMEM((SLOTS, channels), BF),
            pltpu.VMEM((SLOTS, HEADS * HD), BF),
            pltpu.VMEM((SLOTS, HD), BF),
            pltpu.VMEM((SLOTS, HD), BF),
            pltpu.VMEM((4, channels), F32),
            pltpu.VMEM((1, channels), F32),
            pltpu.VMEM((SLOTS * (PAIR_ROWS + 8), HD), F32),
            pltpu.SemaphoreType.DMA((7,)),
        ],
        room=60,
    )(rep, moves, conv, mamba_x, queries, new_keys, new_values, conv_weight, conv_bias[None])
    far_small = lax.ppermute(near_small, "replica", across)

    own = call(
        pack_state_kernel,
        "ssaaaa",
        [("v", shape((MOVES, HELD_ROWS, HD), BF))],
        [
            pltpu.VMEM((MOVES, DS, channels), F32),
            pltpu.VMEM((SLOTS, channels), F32),
            pltpu.VMEM((SLOTS, channels), BF),
            pltpu.VMEM((SLOTS * PAIR_ROWS, HD), F32),
            pltpu.SemaphoreType.DMA((MOVES,)),
            pltpu.SemaphoreType.DMA((2,)),
        ],
        room=60,
    )(rep, moves, ssm_state, conv, mamba_x, near_small)
    other = lax.ppermute(own, "replica", across)

    small = call(
        route_small_kernel,
        "ssvv",
        [("v", shape((REPLICAS, SMALL_ROWS, HD), BF))],
        [],
    )(rep, moves, near_small, far_small)
    small = lax.all_to_all(
        small, "replica", split_axis=0, concat_axis=0, tiled=True, axis_index_groups=planes
    )

    home, kept = call(
        attend_home_kernel,
        "ssssvvddd",
        [("v", shape((rows, HD), F32)), ("v", shape((MOVES, 2, 2 * HD, HD), BF))],
        [pltpu.VMEM((rows, HD), F32)] * 5
        + [pltpu.VMEM((rows, 2 * HD), F32), pltpu.VMEM((rows, HD), jnp.int32)],
        flops=4_000_000_000,
    )(rep, moves, lengths, pages, key_pool, value_pool, queries, new_keys, new_values)

    away = MOVES * 8
    near = call(
        attend_away_kernel,
        "sssvvdd",
        [("v", shape((away, HD), BF))],
        [
            pltpu.VMEM((away, HD), F32),
            pltpu.VMEM((rows, HD), F32),
            pltpu.VMEM((rows, HD), F32),
            pltpu.VMEM((away, 2 * HD), F32),
            pltpu.VMEM((away, HD), jnp.int32),
            pltpu.VMEM((away, HD), F32),
        ],
    )(rep, moves, lengths, small, kept, new_keys, new_values)
    far = lax.ppermute(near, "replica", across)

    sums, mixed = call(
        project_kernel,
        "ssvdddddd",
        [("v", shape((64, 256), F32)), ("v", shape((48, channels), F32))],
        [pltpu.VMEM((SLOTS * PAIR_ROWS, HD), F32)],
        flops=2_000_000_000,
    )(rep, moves, small, conv, mamba_x, conv_weight, conv_bias[None], dt_down, bc_proj.T)
    large = call(
        route_large_kernel,
        "ssvvvv",
        [("v", shape((REPLICAS, LARGE_ROWS, HD), BF))],
        [],
    )(rep, moves, own, other, near, far)
    large = lax.all_to_all(
        large, "replica", split_axis=0, concat_axis=0, tiled=True, axis_index_groups=planes
    )

    bit = 1
    while bit < tensors:
        sums = sums + lax.ppermute(sums, "tensor", [(i, i ^ bit) for i in range(tensors)])
        bit *= 2

    step, states, first = call(
        first_scan_kernel,
        "vvvvvvvv",
        [
            ("v", shape((48, channels), F32)),
            ("v", shape((SLOTS, DS, channels), F32)),
            ("v", shape((SLOTS, channels), BF)),
        ],
        [pltpu.VMEM((SLOTS, channels), F32)],
        flops=3_000_000_000,
    )(sums, mixed, ssm_state, mamba_z, dt_up, dt_bias[None], a_log, skip_d[None])

    mamba_out, final_ssm, last, attention = call(
        last_scan_kernel,
        "ssvvvvvvvvvvvv",
        [
            ("d", shape((2, SLOTS, channels), BF)),
            ("a", shape((SLOTS, DS, channels), F32)),
            ("d", shape((3, SLOTS, channels), F32)),
            ("d", shape((2, SLOTS, HEADS * HD), BF)),
        ],
        [
            pltpu.VMEM((SLOTS, DS, channels), F32),
            pltpu.VMEM((SLOTS, channels), F32),
            pltpu.VMEM((SLOTS * PAIR_ROWS, HD), F32),
            pltpu.VMEM((rows, HD), F32),
            pltpu.SMEM((SLOTS,), jnp.int32),
            pltpu.SemaphoreType.DMA((SLOTS,)),
        ],
    )(
        rep,
        moves,
        sums,
        mixed,
        step,
        states,
        first,
        large,
        mamba_z,
        a_log,
        skip_d[None],
        conv[2],
        mamba_x,
        home,
    )
    return attention, mamba_out, final_ssm, last.transpose(1, 0, 2)


def solution(mesh):
    in_specs = (
        P(),
        P("replica", None),
        P("replica", None, "tensor"),
        P("replica", None, "tensor"),
        P(None, "replica", "tensor"),
        P(None, "replica", "tensor"),
        P(None, "replica", "tensor"),
        P("replica", None, "tensor"),
        P("replica", None, "tensor"),
        P(None, "replica", "tensor"),
        P(None, "replica", "tensor"),
        P(None, "tensor"),
        P("tensor"),
        P("tensor", None),
        P("tensor", None),
        P(None, "tensor"),
        P("tensor"),
        P(None, "tensor"),
        P("tensor"),
        P(),
    )
    out_specs = (
        P(None, "replica", "tensor"),
        P(None, "replica", "tensor"),
        P("replica", None, "tensor"),
        P("replica", None, "tensor"),
    )
    return jax.shard_map(shards, mesh=mesh, in_specs=in_specs, out_specs=out_specs, check_vma=False)
```

time: 68.9 us -> 65.6 us (0.952)
  starting transfers between devices: 36.1 us -> 29.9 us
  waiting for transfers between devices: 12 us -> 15.6 us
  Pallas kernels: 16.7 us -> 15.6 us
    ppermute x3, starting transfers between devices: 9.1 us -> 3.85 us  [shards(): lax.ppermute(sums, 'tensor', [(i, i ^ bit) for i in range(tensors)])]
    all_to_all x1, waiting for transfers between devices: 0.01 us -> 3.69 us  [shards(): lax.all_to_all(large, 'replica', split_axis=0, concat_axis=0, tiled=True,...]
    ppermute x1, waiting for transfers between devices: 2.38 us -> 0.01 us  [shards(): other = lax.ppermute(own, 'replica', across)]
    ppermute x1, waiting for transfers between devices: 0.01 us -> 1.74 us  [shards(): far = lax.ppermute(near, 'replica', across)]
    pallas_call x1, Pallas kernels: 1.7 us -> 0.9 us  [shards(): call(project_kernel, 'ssvdddddd', [('v', shape((64, 256), F32)), ('v', sh...]
    unnamed x46 -> x44, local copies, waits for them, and re-layouts: 2.55 us -> 2.56 us
  transfers between devices with their start and end apart: 8 -> 8, of which waited for: 6 -> 6; matrix products, arithmetic and copies ran while one was open for 0% -> 0% of each run, Pallas kernels for 15% -> 13%
where the time goes in v3:
time: 65.6 us; the launch traced here: 64.6 us
  starting transfers between devices  29.9 us (46%)
  Pallas kernels  15.6 us (24%)
  waiting for transfers between devices  15.6 us (24%)
  local copies, waits for them, and re-layouts  2.57 us (4%)
  between operations  0.98 us (1%)
    all_to_all x1, starting transfers between devices, shards(): lax.all_to_all(small, 'replica', split_axis=0, concat_axis=0, tiled=True,...  7.39 us
    ppermute x1, starting transfers between devices, shards(): far_small = lax.ppermute(near_small, 'replica', across)  7.28 us
    ppermute x3, waiting for transfers between devices, shards(): lax.ppermute(sums, 'tensor', [(i, i ^ bit) for i in range(tensors)])  7.08 us
    ppermute x1, starting transfers between devices, shards(): far = lax.ppermute(near, 'replica', across)  5.97 us
    all_to_all x1, starting transfers between devices, shards(): lax.all_to_all(large, 'replica', split_axis=0, concat_axis=0, tiled=True,...  5.31 us
    ppermute x3, starting transfers between devices, shards(): lax.ppermute(sums, 'tensor', [(i, i ^ bit) for i in range(tensors)])  3.85 us
    all_to_all x1, waiting for transfers between devices, shards(): lax.all_to_all(large, 'replica', split_axis=0, concat_axis=0, tiled=True,...  3.69 us
    all_to_all x1, waiting for transfers between devices, shards(): lax.all_to_all(small, 'replica', split_axis=0, concat_axis=0, tiled=True,...  3.04 us
  transfers between devices with their start and end apart: 8, of which 6 were waited for; matrix products, arithmetic and copies ran while one was open for 0% of the time, Pallas kernels for 13%

profile of v3, /device:TPU:8, one launch (start us, length us, event | category | flops | bytes accessed | tf_op | source)
XLA Modules:
  0.0 64.6 jit_solution(11901825865978966052)
XLA Ops:
  0.6 0.0 copy-start.5
  0.6 2.5 %shard_map.219.own._ = bf16[192,128]{1,0:T(8,128)(2,1)} custom-call(s32[1]{0:T(128)} %bitcast.rep, s32[2,256]{1,0:T(2,128)} %bitcast.15, f32[3,16,1024]{2,1,0:T(8,128)} %bitcast.11, bf16[2,16,1024]{2,1,0:T(8,128)(2,1)} %x.3, bf16[2,16,512]{2,1,0:T(8,128)(2,1)} %q.1, bf16[2,16,128]{2,1,0:T(8,128)(2,1)} %nk.3, bf16[2,16,128]{2,1,0:T(8,128)(2,1)} %nv.3, ...), custom_call_target="tpu_custom_call" | custom-call | tf_op jit(solution)/shard_map/pallas_call | solution.py:451
  3.1 0.0 copy-start.4
  3.1 0.0 copy-start.8
  3.1 0.0 copy-start.9
  3.1 0.0 copy-start.10
  3.2 0.0 copy-start.14
  3.2 0.0 copy-start.21
  3.2 7.3 %collective-permute-start = (bf16[192,128]{1,0:T(8,128)(2,1)}, bf16[192,128]{1,0:T(8,128)(2,1)S(1)}, u32[]{:S(2)}, u32[]{:S(2)}) collective-permute-start(bf16[192,128]{1,0:T(8,128)(2,1)} %shard_map.219.own._), channel_id=1, source_target_pairs={{0,32},{8,40},{16,48},{24,56},{32,0},{40,8},{48,16},{56,24},{64,96... | collective-permute-start | bytes 147464 | tf_op jit(solution)/shard_map/ppermute | solution.py:468
  10.5 2.7 %shard_map.223.own = bf16[8,144,128]{2,1,0:T(8,128)(2,1)} custom-call(s32[1]{0:T(128)} %bitcast.rep, s32[2,256]{1,0:T(2,128)} %bitcast.16, f32[16,16,1024]{2,1,0:T(8,128)} %ssm.3, f32[3,16,1024]{2,1,0:T(8,128)} %bitcast.12, bf16[2,16,1024]{2,1,0:T(8,128)(2,1)} %x.3, bf16[192,128]{1,0:T(8,128)(2,1)} %shard_map.219.own._), custom_call_target="tpu_custom_call" | custom-call | tf_op jit(solution)/shard_map/pallas_call | solution.py:470
  13.1 0.1 collective-permute-start.4
  13.2 0.0 collective-permute-done.other
  13.3 0.0 copy-done.5
  13.3 0.0 copy-done.4
  13.3 1.4 %shard_map.220 = bf16[32,32,128]{2,1,0:T(8,128)(2,1)} custom-call(s32[1]{0:T(128)} %bitcast.rep, s32[2,256]{1,0:T(2,128)S(1)} %bitcast.17, bf16[192,128]{1,0:T(8,128)(2,1)S(1)} %copy-done.4, bf16[192,128]{1,0:T(8,128)(2,1)S(1)} %collective-permute-done.other), custom_call_target="tpu_custom_call" | custom-call | tf_op jit(solution)/shard_map/pallas_call | solution.py:486
  14.7 7.4 %all-to-all-start = ((bf16[32,32,128]{2,1,0:T(8,128)(2,1)}), bf16[32,32,128]{2,1,0:T(8,128)(2,1)S(1)}, u32[]{:S(2)}, u32[]{:S(2)}) async-start(bf16[32,32,128]{2,1,0:T(8,128)(2,1)} %shard_map.220), calls=%async_computation | async-start | bytes 524288 | tf_op jit(solution)/shard_map/all_to_all | solution.py:492
  22.1 0.0 copy-done.8
  22.1 0.0 copy-done.9
  22.1 0.0 copy-done.10
  22.1 0.0 copy-done.14
  22.1 0.0 copy-done.21
  22.1 0.0 copy-start.15
  22.1 1.2 %copy-done.15 = bf16[32,128,128]{2,1,0:T(8,128)(2,1)S(1)} copy-done((bf16[32,128,128]{2,1,0:T(8,128)(2,1)S(1)}, bf16[32,128,128]{2,1,0:T(8,128)(2,1)}, u32[]{:S(2)}) %copy-start.15) | copy-done | bytes 1048600
  23.4 1.2 %copy-done.16 = bf16[32,128,128]{2,1,0:T(8,128)(2,1)S(1)} copy-done((bf16[32,128,128]{2,1,0:T(8,128)(2,1)S(1)}, bf16[32,128,128]{2,1,0:T(8,128)(2,1)}, u32[]{:S(2)}) %copy-start.16) | copy-done | bytes 1048600
  24.6 1.4 %shard_map.224 = (f32[128,128]{1,0:T(8,128)S(1)}, bf16[8,2,256,128]{3,2,1,0:T(8,128)(2,1)S(1)}) custom-call(s32[1]{0:T(128)} %bitcast.rep, s32[2,256]{1,0:T(2,128)S(1)} %bitcast.18, s32[512]{0:T(512)S(1)} %copy-done.14, s32[2,16]{1,0:T(2,128)S(1)} %bitcast.29, bf16[32,128,128]{2,1,0:T(8,128)(2,1)S(1)} %copy-done.15, bf16[32,128,128]{2,1,0:T(8,128)(2,1)S(1)} %copy-done.16, ...), custom_call_target="tpu_custom_call" | custom-call | flops 4000000000 | tf_op jit(solution)/shard_map/pallas_call | solution.py:496
  26.0 0.0 copy-start
  26.0 3.0 %all-to-all-done.recv = bf16[32,32,128]{2,1,0:T(8,128)(2,1)S(1)} async-done(((bf16[32,32,128]{2,1,0:T(8,128)(2,1)}), bf16[32,32,128]{2,1,0:T(8,128)(2,1)S(1)}, u32[]{:S(2)}, u32[]{:S(2)}) %all-to-all-start) | async-done | bytes 262176 | tf_op jit(solution)/shard_map/all_to_all | solution.py:492
  29.1 1.1 %shard_map.225.near = bf16[64,128]{1,0:T(8,128)(2,1)S(1)} custom-call(s32[1]{0:T(128)} %bitcast.rep, s32[2,256]{1,0:T(2,128)S(1)} %bitcast.19, s32[512]{0:T(512)S(1)} %copy-done.14, bf16[32,32,128]{2,1,0:T(8,128)(2,1)S(1)} %all-to-all-done.recv, bf16[8,2,256,128]{3,2,1,0:T(8,128)(2,1)S(1)} %get-tuple-element.20.kept, bf16[2,16,128]{2,1,0:T(8,128)(2,1)S(1)} %copy-done.8, ...), custom_call_target="tpu_custom_call" | custom-call | tf_op jit(solution)/shard_map/pallas_call | solution.py:506
  30.2 6.0 %collective-permute-start.5 = (bf16[64,128]{1,0:T(8,128)(2,1)S(1)}, bf16[64,128]{1,0:T(8,128)(2,1)S(1)}, u32[]{:S(2)}, u32[]{:S(2)}) collective-permute-start(bf16[64,128]{1,0:T(8,128)(2,1)S(1)} %shard_map.225.near), channel_id=1, source_target_pairs={{0,32},{8,40},{16,48},{24,56},{32,0},{40,8},{48,16},{56,24},{64,96... | collective-permute-start | bytes 49160 | tf_op jit(solution)/shard_map/ppermute | solution.py:519
  36.2 0.0 collective-permute-done.4.other
  36.2 1.7 %collective-permute-done.5.far = bf16[64,128]{1,0:T(8,128)(2,1)S(1)} collective-permute-done((bf16[64,128]{1,0:T(8,128)(2,1)S(1)}, bf16[64,128]{1,0:T(8,128)(2,1)S(1)}, u32[]{:S(2)}, u32[]{:S(2)}) %collective-permute-start.5) | collective-permute-done | bytes 16416 | tf_op jit(solution)/shard_map/ppermute | solution.py:519
  37.9 0.0 copy-done
  37.9 1.8 %shard_map.226 = bf16[32,160,128]{2,1,0:T(8,128)(2,1)} custom-call(s32[1]{0:T(128)} %bitcast.rep, s32[2,256]{1,0:T(2,128)S(1)} %bitcast.20, bf16[8,144,128]{2,1,0:T(8,128)(2,1)S(1)} %copy-done, bf16[8,144,128]{2,1,0:T(8,128)(2,1)S(1)} %collective-permute-done.4.other, bf16[64,128]{1,0:T(8,128)(2,1)S(1)} %shard_map.225.near, ...), custom_call_target="tpu_custom_call" | custom-call | tf_op jit(solution)/shard_map/pallas_call | solution.py:528
  39.7 0.0 copy-start.17
  39.7 0.0 copy-start.19
  39.8 5.3 %all-to-all-start.1 = ((bf16[32,160,128]{2,1,0:T(8,128)(2,1)}), bf16[32,160,128]{2,1,0:T(8,128)(2,1)S(1)}, u32[]{:S(2)}, u32[]{:S(2)}) async-start(bf16[32,160,128]{2,1,0:T(8,128)(2,1)} %shard_map.226), calls=%async_computation.1 | async-start | bytes 2621440 | tf_op jit(solution)/shard_map/all_to_all | solution.py:534
  45.1 0.0 copy-done.1
  45.1 0.0 copy-done.3
  45.1 0.0 copy-done.11
  45.1 0.0 copy-done.12
  45.1 0.0 copy-done.17
  45.1 0.0 copy-done.19
  45.1 0.0 copy-start.2
  45.1 0.0 copy-start.6
  45.1 0.0 copy-start.7
  45.2 0.0 copy-start.13
  45.2 0.0 copy-start.18
  45.2 0.0 copy-start.20
  45.2 0.9 %shard_map.221 = (f32[64,256]{1,0:T(8,128)S(1)}, f32[48,1024]{1,0:T(8,128)S(1)}) custom-call(s32[1]{0:T(128)} %bitcast.rep, s32[2,256]{1,0:T(2,128)S(1)} %bitcast.21, bf16[32,32,128]{2,1,0:T(8,128)(2,1)S(1)} %all-to-all-done.recv, f32[3,16,1024]{2,1,0:T(8,128)S(1)} %bitcast.13, bf16[2,16,1024]{2,1,0:T(8,128)(2,1)S(1)} %copy-done.3, ...), custom_call_target="tpu_custom_call" | custom-call | flops 2000000000 | tf_op jit(solution)/shard_map/pallas_call | solution.py:521
  46.1 0.1 collective-permute-start.1
  46.2 1.2 %collective-permute-done.1 = f32[64,256]{1,0:T(8,128)S(1)} collective-permute-done((f32[64,256]{1,0:T(8,128)S(1)}, f32[64,256]{1,0:T(8,128)S(1)}, u32[]{:S(2)}, u32[]{:S(2)}) %collective-permute-start.1) | collective-permute-done | bytes 65568 | tf_op jit(solution)/shard_map/ppermute | solution.py:540
  47.5 1.6 %collective-permute-start.2 = (f32[64,256]{1,0:T(8,128)S(1)}, f32[64,256]{1,0:T(8,128)S(1)}, u32[]{:S(2)}, u32[]{:S(2)}) collective-permute-start(f32[64,256]{1,0:T(8,128)S(1)} %add.9), channel_id=1, source_target_pairs={{0,2},{1,3},{2,0},{3,1},{4,6},{5,7},{6,4},{7,5},{8,10},{9,11},{10,... | collective-permute-start | bytes 196616 | tf_op jit(solution)/shard_map/ppermute | solution.py:540
  49.1 2.8 %collective-permute-done.2 = f32[64,256]{1,0:T(8,128)S(1)} collective-permute-done((f32[64,256]{1,0:T(8,128)S(1)}, f32[64,256]{1,0:T(8,128)S(1)}, u32[]{:S(2)}, u32[]{:S(2)}) %collective-permute-start.2) | collective-permute-done | bytes 65568 | tf_op jit(solution)/shard_map/ppermute | solution.py:540
  51.8 2.2 %collective-permute-start.3 = (f32[64,256]{1,0:T(8,128)S(1)}, f32[64,256]{1,0:T(8,128)S(1)}, u32[]{:S(2)}, u32[]{:S(2)}) collective-permute-start(f32[64,256]{1,0:T(8,128)S(1)} %add.10), channel_id=1, source_target_pairs={{0,4},{1,5},{2,6},{3,7},{4,0},{5,1},{6,2},{7,3},{8,12},{9,13},{10,... | collective-permute-start | bytes 196616 | tf_op jit(solution)/shard_map/ppermute | solution.py:540
  54.0 3.1 %collective-permute-done.3 = f32[64,256]{1,0:T(8,128)S(1)} collective-permute-done((f32[64,256]{1,0:T(8,128)S(1)}, f32[64,256]{1,0:T(8,128)S(1)}, u32[]{:S(2)}, u32[]{:S(2)}) %collective-permute-start.3) | collective-permute-done | bytes 65568 | tf_op jit(solution)/shard_map/ppermute | solution.py:540
  57.1 0.0 copy-done.2
  57.1 0.0 copy-done.6
  57.1 0.0 copy-done.7
  57.1 0.0 copy-done.13
  57.1 0.0 copy-done.18
  57.1 0.0 copy-done.20
  57.1 0.8 %shard_map.222 = (f32[48,1024]{1,0:T(8,128)S(1)}, f32[16,16,1024]{2,1,0:T(8,128)S(1)}, bf16[16,1024]{1,0:T(8,128)(2,1)S(1)}) custom-call(f32[64,256]{1,0:T(8,128)S(1)} %add.11.sums, f32[48,1024]{1,0:T(8,128)S(1)} %get-tuple-element.16.mixed, f32[16,16,1024]{2,1,0:T(8,128)S(1)} %copy-done.2, bf16[2,16,1024]{2,1,0:T(8,128)(2,1)S(1)} %copy-done.6, ...), custom_call_target="tpu_custom_call" | custom-call | flops 3000000000 | tf_op jit(solution)/shard_map/pallas_call | solution.py:543
  57.9 3.7 %all-to-all-done.1.recv = bf16[32,160,128]{2,1,0:T(8,128)(2,1)S(1)} async-done(((bf16[32,160,128]{2,1,0:T(8,128)(2,1)}), bf16[32,160,128]{2,1,0:T(8,128)(2,1)S(1)}, u32[]{:S(2)}, u32[]{:S(2)}) %all-to-all-start.1) | async-done | bytes 1310752 | tf_op jit(solution)/shard_map/all_to_all | solution.py:534
  61.6 3.0 %shard_map.227 = (bf16[2,16,1024]{2,1,0:T(8,128)(2,1)}, f32[16,16,1024]{2,1,0:T(8,128)}, f32[3,16,1024]{2,1,0:T(8,128)}, bf16[2,16,512]{2,1,0:T(8,128)(2,1)}) custom-call(s32[1]{0:T(128)} %bitcast.rep, s32[2,256]{1,0:T(2,128)S(1)} %bitcast.22, f32[64,256]{1,0:T(8,128)S(1)} %add.11.sums, f32[48,1024]{1,0:T(8,128)S(1)} %get-tuple-element.16.mixed, ...), custom_call_target="tpu_custom_call" | custom-call | tf_op jit(solution)/shard_map/pallas_call | solution.py:555
  (9 shorter events, 0.0 us)
Async XLA Ops:
  0.6 12.6 %copy-start.5 = (s32[256,2]{0,1:T(2,128)S(1)}, s32[256,2]{0,1:T(2,128)}, u32[]{:S(2)}) copy-start(s32[256,2]{0,1:T(2,128)} %param.39) | copy-start | bytes 6148
  3.1 10.2 %copy-start.4 = (bf16[192,128]{1,0:T(8,128)(2,1)S(1)}, bf16[192,128]{1,0:T(8,128)(2,1)}, u32[]{:S(2)}) copy-start(bf16[192,128]{1,0:T(8,128)(2,1)} %shard_map.219.own._) | copy-start | bytes 147460
  3.1 19.0 %copy-start.8 = (bf16[2,16,128]{2,1,0:T(8,128)(2,1)S(1)}, bf16[2,16,128]{2,1,0:T(8,128)(2,1)}, u32[]{:S(2)}) copy-start(bf16[2,16,128]{2,1,0:T(8,128)(2,1)} %nk.3) | copy-start | bytes 24580
  3.1 19.0 %copy-start.9 = (bf16[2,16,128]{2,1,0:T(8,128)(2,1)S(1)}, bf16[2,16,128]{2,1,0:T(8,128)(2,1)}, u32[]{:S(2)}) copy-start(bf16[2,16,128]{2,1,0:T(8,128)(2,1)} %nv.3) | copy-start | bytes 24580
  3.1 19.0 %copy-start.10 = (bf16[2,16,512]{2,1,0:T(8,128)(2,1)S(1)}, bf16[2,16,512]{2,1,0:T(8,128)(2,1)}, u32[]{:S(2)}) copy-start(bf16[2,16,512]{2,1,0:T(8,128)(2,1)} %q.1) | copy-start | bytes 98308
  3.2 18.9 %copy-start.14 = (s32[512]{0:T(512)S(1)}, s32[512]{0:T(512)}, u32[]{:S(2)}) copy-start(s32[512]{0:T(512)} %lens.3) | copy-start | bytes 6148
  3.2 18.9 %copy-start.21 = (s32[16,2]{0,1:T(2,128)S(1)}, s32[16,2]{0,1:T(2,128)}, u32[]{:S(2)}) copy-start(s32[16,2]{0,1:T(2,128)} %param.21) | copy-start | bytes 388
  3.2 10.1 %collective-permute-start = (bf16[192,128]{1,0:T(8,128)(2,1)}, bf16[192,128]{1,0:T(8,128)(2,1)S(1)}, u32[]{:S(2)}, u32[]{:S(2)}) collective-permute-start(bf16[192,128]{1,0:T(8,128)(2,1)} %shard_map.219.own._), channel_id=1, source_target_pairs={{0,32},{8,40},{16,48},{24,56},{32,0},{40,8},{48,16},{56,24},{64,96... | collective-permute-start | bytes 147464 | tf_op jit(solution)/shard_map/ppermute | solution.py:468
  13.1 23.0 %collective-permute-start.4 = (bf16[8,144,128]{2,1,0:T(8,128)(2,1)}, bf16[8,144,128]{2,1,0:T(8,128)(2,1)S(1)}, u32[]{:S(2)}, u32[]{:S(2)}) collective-permute-start(bf16[8,144,128]{2,1,0:T(8,128)(2,1)} %shard_map.223.own), channel_id=1, source_target_pairs={{0,32},{8,40},{16,48},{24,56},{32,0},{40,8},{48,16},{56,24},{64,96... | collective-permute-start | bytes 884744 | tf_op jit(solution)/shard_map/ppermute | solution.py:484
  14.7 14.4 %all-to-all-start = ((bf16[32,32,128]{2,1,0:T(8,128)(2,1)}), bf16[32,32,128]{2,1,0:T(8,128)(2,1)S(1)}, u32[]{:S(2)}, u32[]{:S(2)}) async-start(bf16[32,32,128]{2,1,0:T(8,128)(2,1)} %shard_map.220), calls=%async_computation | async-start | bytes 524288 | tf_op jit(solution)/shard_map/all_to_all | solution.py:492
  22.1 1.2 %copy-start.15 = (bf16[32,128,128]{2,1,0:T(8,128)(2,1)S(1)}, bf16[32,128,128]{2,1,0:T(8,128)(2,1)}, u32[]{:S(2)}) copy-start(bf16[32,128,128]{2,1,0:T(8,128)(2,1)} %keys.1) | copy-start | bytes 3145732
  23.4 1.2 %copy-start.16 = (bf16[32,128,128]{2,1,0:T(8,128)(2,1)S(1)}, bf16[32,128,128]{2,1,0:T(8,128)(2,1)}, u32[]{:S(2)}) copy-start(bf16[32,128,128]{2,1,0:T(8,128)(2,1)} %values.1) | copy-start | bytes 3145732
  26.0 11.9 %copy-start = (bf16[8,144,128]{2,1,0:T(8,128)(2,1)S(1)}, bf16[8,144,128]{2,1,0:T(8,128)(2,1)}, u32[]{:S(2)}) copy-start(bf16[8,144,128]{2,1,0:T(8,128)(2,1)} %shard_map.223.own) | copy-start | bytes 884740
  30.2 7.7 %collective-permute-start.5 = (bf16[64,128]{1,0:T(8,128)(2,1)S(1)}, bf16[64,128]{1,0:T(8,128)(2,1)S(1)}, u32[]{:S(2)}, u32[]{:S(2)}) collective-permute-start(bf16[64,128]{1,0:T(8,128)(2,1)S(1)} %shard_map.225.near), channel_id=1, source_target_pairs={{0,32},{8,40},{16,48},{24,56},{32,0},{40,8},{48,16},{56,24},{64,96... | collective-permute-start | bytes 49160 | tf_op jit(solution)/shard_map/ppermute | solution.py:519
  39.7 5.4 %copy-start.1 = (f32[16,3,1024]{2,0,1:T(8,128)S(1)}, f32[16,3,1024]{2,0,1:T(8,128)}, u32[]{:S(2)}) copy-start(f32[16,3,1024]{2,0,1:T(8,128)} %param.27) | copy-start | bytes 589828
  39.7 5.4 %copy-start.3 = (bf16[2,16,1024]{2,1,0:T(8,128)(2,1)S(1)}, bf16[2,16,1024]{2,1,0:T(8,128)(2,1)}, u32[]{:S(2)}) copy-start(bf16[2,16,1024]{2,1,0:T(8,128)(2,1)} %x.3) | copy-start | bytes 196612
  39.7 5.4 %copy-start.11 = (f32[4,1024]{1,0:T(4,128)S(1)}, f32[4,1024]{1,0:T(4,128)}, u32[]{:S(2)}) copy-start(f32[4,1024]{1,0:T(4,128)} %cw.1) | copy-start | bytes 49156
  39.7 5.4 %copy-start.12 = (f32[1024]{0:T(1024)S(1)}, f32[1024]{0:T(1024)}, u32[]{:S(2)}) copy-start(f32[1024]{0:T(1024)} %param.32) | copy-start | bytes 12292
  39.7 5.4 %copy-start.17 = (bf16[1024,256]{1,0:T(8,128)(2,1)S(1)}, bf16[1024,256]{1,0:T(8,128)(2,1)}, u32[]{:S(2)}) copy-start(bf16[1024,256]{1,0:T(8,128)(2,1)} %down.1) | copy-start | bytes 1572868
  39.7 5.4 %copy-start.19 = (bf16[1024,32]{0,1:T(8,128)(2,1)S(1)}, bf16[1024,32]{0,1:T(8,128)(2,1)}, u32[]{:S(2)}) copy-start(bf16[1024,32]{0,1:T(8,128)(2,1)} %param.34) | copy-start | bytes 196612
  39.8 21.9 %all-to-all-start.1 = ((bf16[32,160,128]{2,1,0:T(8,128)(2,1)}), bf16[32,160,128]{2,1,0:T(8,128)(2,1)S(1)}, u32[]{:S(2)}, u32[]{:S(2)}) async-start(bf16[32,160,128]{2,1,0:T(8,128)(2,1)} %shard_map.226), calls=%async_computation.1 | async-start | bytes 2621440 | tf_op jit(solution)/shard_map/all_to_all | solution.py:534
  45.1 12.0 %copy-start.2 = (f32[16,16,1024]{2,1,0:T(8,128)S(1)}, f32[16,16,1024]{2,1,0:T(8,128)}, u32[]{:S(2)}) copy-start(f32[16,16,1024]{2,1,0:T(8,128)} %ssm.3) | copy-start | bytes 3145732
  45.1 12.0 %copy-start.6 = (bf16[2,16,1024]{2,1,0:T(8,128)(2,1)S(1)}, bf16[2,16,1024]{2,1,0:T(8,128)(2,1)}, u32[]{:S(2)}) copy-start(bf16[2,16,1024]{2,1,0:T(8,128)(2,1)} %z.3) | copy-start | bytes 196612
  45.1 12.0 %copy-start.7 = (f32[16,1024]{1,0:T(8,128)S(1)}, f32[16,1024]{1,0:T(8,128)}, u32[]{:S(2)}) copy-start(f32[16,1024]{1,0:T(8,128)} %alog.3) | copy-start | bytes 196612
  45.2 12.0 %copy-start.13 = (f32[1024]{0:T(1024)S(1)}, f32[1024]{0:T(1024)}, u32[]{:S(2)}) copy-start(f32[1024]{0:T(1024)} %param.38) | copy-start | bytes 12292
  45.2 12.0 %copy-start.18 = (bf16[256,1024]{1,0:T(8,128)(2,1)S(1)}, bf16[256,1024]{1,0:T(8,128)(2,1)}, u32[]{:S(2)}) copy-start(bf16[256,1024]{1,0:T(8,128)(2,1)} %up.1) | copy-start | bytes 1572868
  45.2 12.0 %copy-start.20 = (f32[1024]{0:T(1024)S(1)}, f32[1024]{0:T(1024)}, u32[]{:S(2)}) copy-start(f32[1024]{0:T(1024)} %param.36) | copy-start | bytes 12292
  46.1 1.3 %collective-permute-start.1 = (f32[64,256]{1,0:T(8,128)S(1)}, f32[64,256]{1,0:T(8,128)S(1)}, u32[]{:S(2)}, u32[]{:S(2)}) collective-permute-start(f32[64,256]{1,0:T(8,128)S(1)} %get-tuple-element.15), channel_id=1, source_target_pairs={{0,1},{1,0},{2,3},{3,2},{4,5},{5,4},{6,7},{7,6},{8,9},{9,8},{10,11... | collective-permute-start | bytes 196616 | tf_op jit(solution)/shard_map/ppermute | solution.py:540
  47.5 4.4 %collective-permute-start.2 = (f32[64,256]{1,0:T(8,128)S(1)}, f32[64,256]{1,0:T(8,128)S(1)}, u32[]{:S(2)}, u32[]{:S(2)}) collective-permute-start(f32[64,256]{1,0:T(8,128)S(1)} %add.9), channel_id=1, source_target_pairs={{0,2},{1,3},{2,0},{3,1},{4,6},{5,7},{6,4},{7,5},{8,10},{9,11},{10,... | collective-permute-start | bytes 196616 | tf_op jit(solution)/shard_map/ppermute | solution.py:540
  51.8 5.3 %collective-permute-start.3 = (f32[64,256]{1,0:T(8,128)S(1)}, f32[64,256]{1,0:T(8,128)S(1)}, u32[]{:S(2)}, u32[]{:S(2)}) collective-permute-start(f32[64,256]{1,0:T(8,128)S(1)} %add.10), channel_id=1, source_target_pairs={{0,4},{1,5},{2,6},{3,7},{4,0},{5,1},{6,2},{7,3},{8,12},{9,13},{10,... | collective-permute-start | bytes 196616 | tf_op jit(solution)/shard_map/ppermute | solution.py:540

commit v4 on v3

--- a/solution.py
+++ b/solution.py
@@ -66,10 +66,11 @@
 
 
 def pack_small_kernel(
-    rep, moves, conv_in, x_in, q_in, nk_in, nv_in, cw_in, cb_in, send, conv, x, q, nk, nv, cw, cb, small, read
+    moves_in, conv_in, x_in, q_in, nk_in, nv_in, cw_in, cb_in, send, moves, conv, x, q, nk, nv, cw, cb, small, read
 ):
-    me = rep[0]
+    me = lax.axis_index("replica")
     pairs = (
+        (moves_in, moves),
         (conv_in, conv),
         (x_in.at[0], x),
         (q_in.at[1], q),
@@ -111,8 +112,8 @@
         send[start : start + 16, :] = jnp.concatenate(back[j : j + 2], axis=0).astype(BF)
 
 
-def route_small_kernel(rep, moves, own, other, send):
-    me = rep[0]
+def route_small_kernel(moves, own, other, send):
+    me = lax.axis_index("replica")
     blank = jnp.zeros((8, HD), F32)
     for j in range(MOVES):
         _, target = out_move(me, moves, j)
@@ -132,8 +133,8 @@
         send[to, PAIR_ROWS:, :] = jnp.concatenate([part, blank], axis=0).astype(BF)
 
 
-def pack_state_kernel(rep, moves, ssm, conv_in, x_in, _, send, held, conv, x, small, arrived, read):
-    me = rep[0]
+def pack_state_kernel(moves, ssm, conv_in, x_in, _, send, held, conv, x, small, arrived, read):
+    me = lax.axis_index("replica")
     copies = []
     for j in range(MOVES):
         slot, _ = out_move(me, moves, j)
@@ -200,9 +201,9 @@
 
 
 def attend_home_kernel(
-    rep, moves, lens, pages, keys, values, q, nk, nv, result, kept, qs, fk, fv, gk, gv, score, limit
+    moves, lens, pages, keys, values, q, nk, nv, result, kept, qs, fk, fv, gk, gv, score, limit
 ):
-    me = rep[0]
+    me = lax.axis_index("replica")
     for step in range(2):
         for h in range(HEADS):
             qs[pl.ds(step * HEADS + h, SLOTS, stride=8), :] = q[
@@ -232,9 +233,9 @@
 
 
 def attend_away_kernel(
-    rep, moves, lens, recv, kept, nk, nv, send, qs, fk, fv, score, limit, result
+    moves, lens, recv, kept, nk, nv, send, qs, fk, fv, score, limit, result
 ):
-    me = rep[0]
+    me = lax.axis_index("replica")
     spread(fk, nk[0].astype(F32))
     spread(fv, nv[0].astype(F32))
     slots = []
@@ -263,23 +264,44 @@
     send[...] = result[...].astype(BF)
 
 
-def route_large_kernel(rep, moves, own, other, near, far, send):
-    me = rep[0]
-    blank = jnp.zeros((8, HD), F32)
+def route_states_kernel(moves, own, other, _, send, sent):
+    me = lax.axis_index("replica")
+    copies = []
     for j in range(MOVES):
         _, target = out_move(me, moves, j)
         flip = crosses(me, target)
         _, target = out_move(me ^ (flip * FAR), moves, j)
-        to = place(target) * 2 + flip
-        send[to, :HELD_ROWS, :] = jnp.where(flip == 1, other[j], own[j])
+        goal = send.at[place(target) * 2 + flip, pl.ds(0, HELD_ROWS), :]
+        kept = pltpu.make_async_copy(own.at[j], goal, sent.at[j])
+        swapped = pltpu.make_async_copy(other.at[j], goal, sent.at[j])
+        pl.when(flip == 0)(kept.start)
+        pl.when(flip == 1)(swapped.start)
+        copies.append(kept)
+    for copy in copies:
+        copy.wait()
+
+
+def route_results_kernel(moves, near, far, _, send, blocks, sent):
+    me = lax.axis_index("replica")
+    blank = jnp.zeros((8, HD), F32)
+    copies = []
+    for j in range(MOVES):
+        _, target = out_move(me, moves, j)
+        flip = crosses(me, target)
+        _, target = out_move(me ^ (flip * FAR), moves, j)
         lines = slice(j // 2 * 16, j // 2 * 16 + 16)
         both = jnp.where(flip == 1, far[lines, :], near[lines, :]).astype(F32)
         part = both[j % 2 * 8 : j % 2 * 8 + 8, :]
-        send[to, HELD_ROWS:, :] = jnp.concatenate([part, blank], axis=0).astype(BF)
-
-
-def project_kernel(rep, moves, recv, conv, x, cw, cb, down, bct, sums, mixed, rows):
-    me = rep[0]
+        blocks[j] = jnp.concatenate([part, blank], axis=0).astype(BF)
+        goal = send.at[place(target) * 2 + flip, pl.ds(HELD_ROWS, 16), :]
+        copies.append(pltpu.make_async_copy(blocks.at[j], goal, sent.at[j]))
+        copies[j].start()
+    for copy in copies:
+        copy.wait()
+
+
+def project_kernel(moves, recv, conv, x, cw, cb, down, bct, sums, mixed, rows):
+    me = lax.axis_index("replica")
     x0 = x[0].astype(F32)
     x1 = x[1].astype(F32)
     tap = [cw[k : k + 1, :] for k in range(4)]
@@ -307,101 +329,150 @@
     sums[48:64, 128:176] = maps[DS:]
 
 
-def advance(state, sums, step, mixed, rate, row):
-    dts = step[row : row + 1, :]
-    grown = jnp.exp(dts * rate) * state
-    b = sums[48:64, row : row + 1]
-    return grown + b * (dts * mixed[row : row + 1, :])
-
-
-def read(state, sums, row):
-    c = sums[48:64, 128 + row : 129 + row]
-    return jnp.sum(c * state, axis=0, keepdims=True)
-
-
-def first_scan_kernel(sums, mixed, ssm, z, up, db, alog, skip, step, states, out, yrows):
+def lay(row):
+    return jnp.concatenate(cut([row]), axis=0)
+
+
+def first_scan_kernel(
+    moves,
+    sums,
+    mixed,
+    ssm,
+    z,
+    up,
+    db,
+    alog,
+    skip,
+    factor,
+    offset,
+    maps,
+    first,
+    base,
+    gate,
+    read_out,
+    final,
+    step,
+    held,
+    yrows,
+    position,
+    left,
+):
+    me = lax.axis_index("replica")
+    for s in range(SLOTS):
+        position[s] = MOVES
+    for j in range(MOVES):
+        slot, _ = in_move(me, moves, j)
+        position[slot] = j
     dt = jnp.dot(sums[0:48, :].astype(BF), up[...], preferred_element_type=F32) + db[...]
     step[...] = jnp.maximum(dt, 0.0) + jnp.log1p(jnp.exp(-jnp.abs(dt)))
     rate = -jnp.exp(alog[...])
+
+    def terms(row):
+        dts = step[row : row + 1, :]
+        added = sums[48:64, row : row + 1] * (dts * mixed[row : row + 1, :])
+        return jnp.exp(dts * rate), added
+
+    copies = []
     for s in range(SLOTS):
-        state = advance(ssm[s], sums, step, mixed, rate, s)
-        states[s] = state
-        yrows[s : s + 1, :] = read(state, sums, s)
-    out[...] = ((yrows[...] + skip[...] * mixed[0:16]) * silu(z[0].astype(F32))).astype(BF)
+        decay, added = terms(s)
+        state = decay * ssm[s] + added
+        read = sums[48:64, 128 + s : 129 + s] * state
+        yrows[s : s + 1, :] = jnp.sum(read, axis=0, keepdims=True)
+        decay, added = terms(16 + s)
+        later, more = terms(32 + s)
+        at = position[s]
+        factor[at] = decay * later
+        offset[at] = later * added + more
+        column = sums[48:64, 160 + s : 161 + s]
+        maps[at] = jnp.broadcast_to(column, (DS, HD))
+        state = later * state + more
+        held[s] = state
+        copies.append(pltpu.make_async_copy(held.at[s], final.at[s], left.at[s]))
+        copies[s].start()
+        read_out[s * 8 : s * 8 + 8, :] = lay(jnp.sum(column * state, axis=0, keepdims=True))
+    first[...] = ((yrows[...] + skip[...] * mixed[0:16]) * silu(z[0].astype(F32))).astype(BF)
+    base[...] = skip[...] * mixed[32:48]
+    gate[...] = silu(z[1].astype(F32))
+    for copy in copies:
+        copy.wait()
 
 
 def last_scan_kernel(
-    rep,
     moves,
-    sums,
-    mixed,
-    step,
-    states,
+    factor,
+    offset,
+    maps,
     first,
+    base,
+    gate,
+    read_in,
     recv,
-    z,
-    alog,
-    skip,
     conv,
     x,
     home,
+    _,
+    final,
     out,
-    final,
     last,
     attention,
     held,
+    held_out,
+    held_last,
+    held_attention,
     yrows,
     rows,
     lines,
-    origin,
     left,
 ):
-    me = rep[0]
-    for s in range(SLOTS):
-        origin[s] = -1
-    for i, piece in enumerate(cut([conv[...], x[0].astype(F32)])):
+    me = lax.axis_index("replica")
+    copies = []
+
+    def leave(source, target):
+        copies.append(pltpu.make_async_copy(source, target, left.at[len(copies)]))
+        copies[-1].start()
+
+    leave(first, out.at[0])
+    yrows[...] = read_in[...]
+    lines[...] = home[...]
+    for i, piece in enumerate(cut([conv[2], x[0].astype(F32)])):
         rows[pl.ds(i, SLOTS, stride=PAIR_ROWS), :] = piece
-    lines[...] = home[...]
     second = lax.broadcasted_iota(jnp.int32, (8, HD), 0) >= HEADS
     for j in range(MOVES):
         slot, source = in_move(me, moves, j)
         index = place(source) * 2 + crosses(me, source)
-        origin[slot] = index
-        start = pl.multiple_of(slot * PAIR_ROWS, PAIR_ROWS)
-        rows[pl.ds(start, PAIR_ROWS), :] = recv[index, STATE_ROWS:HELD_ROWS, :].astype(F32)
-        came = recv[index, HELD_ROWS:, :].astype(F32)[:8, :]
-        start = pl.multiple_of(slot * 8, 8)
-        lines[pl.ds(start, 8), :] = jnp.where(second, came, lines[pl.ds(start, 8), :])
-    rate = -jnp.exp(alog[...])
-    copies = []
-    for s in range(SLOTS):
-        source = origin[s]
-        came = recv.at[jnp.maximum(source, 0)]
+        came = recv.at[index]
         moved = jnp.concatenate(
             [came[c * DS : (c + 1) * DS, :] for c in range(PIECES)], axis=1
         ).astype(F32)
-        moved = advance(moved, sums, step, mixed, rate, 16 + s)
-        state = jnp.where(source >= 0, moved, states[s])
-        state = advance(state, sums, step, mixed, rate, 32 + s)
-        held[s] = state
-        copies.append(pltpu.make_async_copy(held.at[s], final.at[s], left.at[s]))
-        copies[s].start()
-        yrows[s : s + 1, :] = read(state, sums, 32 + s)
-    last[0] = whole(rows, 0)
-    last[1] = whole(rows, 1)
-    last[2] = x[1].astype(F32)
-    out[0] = first[...]
-    out[1] = ((yrows[...] + skip[...] * mixed[32:48]) * silu(z[1].astype(F32))).astype(BF)
-    for step_number in range(2):
+        state = factor[j] * moved + offset[j]
+        held[j] = state
+        leave(held.at[j], final.at[slot])
+        read = jnp.concatenate([maps[j]] * PIECES, axis=1) * state
+        start = pl.multiple_of(slot * 8, 8)
+        yrows[pl.ds(start, 8), :] = lay(jnp.sum(read, axis=0, keepdims=True))
+        result = came[HELD_ROWS:, :].astype(F32)[:8, :]
+        lines[pl.ds(start, 8), :] = jnp.where(second, result, lines[pl.ds(start, 8), :])
+        start = pl.multiple_of(slot * PAIR_ROWS, PAIR_ROWS)
+        rows[pl.ds(start, PAIR_ROWS), :] = came[STATE_ROWS:HELD_ROWS, :].astype(F32)
+    read = [yrows[pl.ds(c, SLOTS, stride=8), :] for c in range(PIECES)]
+    read = jnp.concatenate(read, axis=1)
+    held_out[...] = ((read + base[...]) * gate[...]).astype(BF)
+    leave(held_out, out.at[1])
+    held_last[0] = whole(rows, 0)
+    held_last[1] = whole(rows, 1)
+    held_last[2] = x[1].astype(F32)
+    leave(held_last, last)
+    for number in range(2):
         for h in range(HEADS):
-            attention[step_number, :, h * HD : (h + 1) * HD] = lines[
-                pl.ds(step_number * HEADS + h, SLOTS, stride=8), :
+            held_attention[number, :, h * HD : (h + 1) * HD] = lines[
+                pl.ds(number * HEADS + h, SLOTS, stride=8), :
             ].astype(BF)
+    leave(held_attention, attention)
     for copy in copies:
         copy.wait()
 
 
-def call(kernel, kinds, outs, scratch, flops=0, room=32):
+def call(kernel, kinds, outs, scratch, flops=0, room=16, aliases={}):
     outs_specs = [SPECS[kind] for kind, _ in outs]
     shapes = [shape for _, shape in outs]
     return pl.pallas_call(
@@ -410,6 +481,7 @@
         out_specs=outs_specs if len(outs) > 1 else outs_specs[0],
         out_shape=shapes if len(outs) > 1 else shapes[0],
         scratch_shapes=scratch,
+        input_output_aliases=aliases,
         cost_estimate=pl.CostEstimate(flops=flops, bytes_accessed=0, transcendentals=0),
         compiler_params=pltpu.CompilerParams(vmem_limit_bytes=room * 1024 * 1024),
     )
@@ -439,7 +511,6 @@
 ):
     tensors = lax.axis_size("tensor")
     channels = ssm_state.shape[2]
-    rep = lax.axis_index("replica").astype(jnp.int32).reshape(1)
     moves = moves.T
     pages = page_table.T
     conv = conv_state.transpose(1, 0, 2)
@@ -450,9 +521,10 @@
 
     near_small = call(
         pack_small_kernel,
-        "ssaaaaaaa",
+        "aaaaaaaa",
         [("v", shape((MOVES * 24, HD), BF))],
         [
+            pltpu.SMEM((2, MOVES * REPLICAS), jnp.int32),
             pltpu.VMEM((3, SLOTS, channels), F32),
             pltpu.VMEM((SLOTS, channels), BF),
             pltpu.VMEM((SLOTS, HEADS * HD), BF),
@@ -461,15 +533,15 @@
             pltpu.VMEM((4, channels), F32),
             pltpu.VMEM((1, channels), F32),
             pltpu.VMEM((SLOTS * (PAIR_ROWS + 8), HD), F32),
-            pltpu.SemaphoreType.DMA((7,)),
+            pltpu.SemaphoreType.DMA((8,)),
         ],
         room=60,
-    )(rep, moves, conv, mamba_x, queries, new_keys, new_values, conv_weight, conv_bias[None])
+    )(moves, conv, mamba_x, queries, new_keys, new_values, conv_weight, conv_bias[None])
     far_small = lax.ppermute(near_small, "replica", across)
 
     own = call(
         pack_state_kernel,
-        "ssaaaa",
+        "saaaa",
         [("v", shape((MOVES, HELD_ROWS, HD), BF))],
         [
             pltpu.VMEM((MOVES, DS, channels), F32),
@@ -480,32 +552,32 @@
             pltpu.SemaphoreType.DMA((2,)),
         ],
         room=60,
-    )(rep, moves, ssm_state, conv, mamba_x, near_small)
+    )(moves, ssm_state, conv, mamba_x, near_small)
     other = lax.ppermute(own, "replica", across)
 
     small = call(
         route_small_kernel,
-        "ssvv",
+        "svv",
         [("v", shape((REPLICAS, SMALL_ROWS, HD), BF))],
         [],
-    )(rep, moves, near_small, far_small)
+    )(moves, near_small, far_small)
     small = lax.all_to_all(
         small, "replica", split_axis=0, concat_axis=0, tiled=True, axis_index_groups=planes
     )
 
     home, kept = call(
         attend_home_kernel,
-        "ssssvvddd",
+        "sssvvddd",
         [("v", shape((rows, HD), F32)), ("v", shape((MOVES, 2, 2 * HD, HD), BF))],
         [pltpu.VMEM((rows, HD), F32)] * 5
         + [pltpu.VMEM((rows, 2 * HD), F32), pltpu.VMEM((rows, HD), jnp.int32)],
         flops=4_000_000_000,
-    )(rep, moves, lengths, pages, key_pool, value_pool, queries, new_keys, new_values)
+    )(moves, lengths, pages, key_pool, value_pool, queries, new_keys, new_values)
 
     away = MOVES * 8
     near = call(
         attend_away_kernel,
-        "sssvvdd",
+        "ssvvdd",
         [("v", shape((away, HD), BF))],
         [
             pltpu.VMEM((away, HD), F32),
@@ -515,22 +587,29 @@
             pltpu.VMEM((away, HD), jnp.int32),
             pltpu.VMEM((away, HD), F32),
         ],
-    )(rep, moves, lengths, small, kept, new_keys, new_values)
+    )(moves, lengths, small, kept, new_keys, new_values)
     far = lax.ppermute(near, "replica", across)
 
     sums, mixed = call(
         project_kernel,
-        "ssvdddddd",
+        "svdddddd",
         [("v", shape((64, 256), F32)), ("v", shape((48, channels), F32))],
         [pltpu.VMEM((SLOTS * PAIR_ROWS, HD), F32)],
         flops=2_000_000_000,
-    )(rep, moves, small, conv, mamba_x, conv_weight, conv_bias[None], dt_down, bc_proj.T)
+    )(moves, small, conv, mamba_x, conv_weight, conv_bias[None], dt_down, bc_proj.T)
     large = call(
-        route_large_kernel,
-        "ssvvvv",
-        [("v", shape((REPLICAS, LARGE_ROWS, HD), BF))],
-        [],
-    )(rep, moves, own, other, near, far)
+        route_states_kernel,
+        "saaa",
+        [("a", shape((REPLICAS, LARGE_ROWS, HD), BF))],
+        [pltpu.SemaphoreType.DMA((MOVES,))],
+    )(moves, own, other, near)
+    large = call(
+        route_results_kernel,
+        "svva",
+        [("a", shape((REPLICAS, LARGE_ROWS, HD), BF))],
+        [pltpu.VMEM((MOVES, 16, HD), BF), pltpu.SemaphoreType.DMA((MOVES,))],
+        aliases={3: 0},
+    )(moves, near, far, large)
     large = lax.all_to_all(
         large, "replica", split_axis=0, concat_axis=0, tiled=True, axis_index_groups=planes
     )
@@ -540,50 +619,51 @@
         sums = sums + lax.ppermute(sums, "tensor", [(i, i ^ bit) for i in range(tensors)])
         bit *= 2
 
-    step, states, first = call(
+    factor, offset, maps, first, base, gate, read, final_ssm = call(
         first_scan_kernel,
-        "vvvvvvvv",
+        "svvvvvvvv",
         [
-            ("v", shape((48, channels), F32)),
-            ("v", shape((SLOTS, DS, channels), F32)),
+            ("v", shape((MOVES + 1, DS, channels), F32)),
+            ("v", shape((MOVES + 1, DS, channels), F32)),
+            ("v", shape((MOVES + 1, DS, HD), F32)),
             ("v", shape((SLOTS, channels), BF)),
-        ],
-        [pltpu.VMEM((SLOTS, channels), F32)],
-        flops=3_000_000_000,
-    )(sums, mixed, ssm_state, mamba_z, dt_up, dt_bias[None], a_log, skip_d[None])
-
-    mamba_out, final_ssm, last, attention = call(
-        last_scan_kernel,
-        "ssvvvvvvvvvvvv",
-        [
-            ("d", shape((2, SLOTS, channels), BF)),
+            ("v", shape((SLOTS, channels), F32)),
+            ("v", shape((SLOTS, channels), F32)),
+            ("v", shape((rows, HD), F32)),
             ("a", shape((SLOTS, DS, channels), F32)),
-            ("d", shape((3, SLOTS, channels), F32)),
-            ("d", shape((2, SLOTS, HEADS * HD), BF)),
         ],
         [
+            pltpu.VMEM((48, channels), F32),
             pltpu.VMEM((SLOTS, DS, channels), F32),
             pltpu.VMEM((SLOTS, channels), F32),
-            pltpu.VMEM((SLOTS * PAIR_ROWS, HD), F32),
-            pltpu.VMEM((rows, HD), F32),
             pltpu.SMEM((SLOTS,), jnp.int32),
             pltpu.SemaphoreType.DMA((SLOTS,)),
         ],
+        flops=3_000_000_000,
+    )(moves, sums, mixed, ssm_state, mamba_z, dt_up, dt_bias[None], a_log, skip_d[None])
+
+    final_ssm, mamba_out, last, attention = call(
+        last_scan_kernel,
+        "svvvvvvvvvvva",
+        [
+            ("a", shape((SLOTS, DS, channels), F32)),
+            ("a", shape((2, SLOTS, channels), BF)),
+            ("a", shape((3, SLOTS, channels), F32)),
+            ("a", shape((2, SLOTS, HEADS * HD), BF)),
+        ],
+        [
+            pltpu.VMEM((MOVES, DS, channels), F32),
+            pltpu.VMEM((SLOTS, channels), BF),
+            pltpu.VMEM((3, SLOTS, channels), F32),
+            pltpu.VMEM((2, SLOTS, HEADS * HD), BF),
+            pltpu.VMEM((rows, HD), F32),
+            pltpu.VMEM((SLOTS * PAIR_ROWS, HD), F32),
+            pltpu.VMEM((rows, HD), F32),
+            pltpu.SemaphoreType.DMA((MOVES + 4,)),
+        ],
+        aliases={12: 0},
     )(
-        rep,
-        moves,
-        sums,
-        mixed,
-        step,
-        states,
-        first,
-        large,
-        mamba_z,
-        a_log,
-        skip_d[None],
-        conv[2],
-        mamba_x,
-        home,
+        moves, factor, offset, maps, first, base, gate, read, large, conv, mamba_x, home, final_ssm
     )
     return attention, mamba_out, final_ssm, last.transpose(1, 0, 2)
 

time: 65.6 us -> 63.1 us (0.962)
  waiting for transfers between devices: 15.6 us -> 12.1 us
  Pallas kernels: 15.6 us -> 16.5 us
    all_to_all x1, waiting for transfers between devices: 3.69 us -> 1.58 us  [shards(): lax.all_to_all(large, 'replica', split_axis=0, concat_axis=0, tiled=True,...]
    ppermute x1, waiting for transfers between devices: 1.74 us -> 0.33 us  [shards(): far = lax.ppermute(near, 'replica', across)]
    pallas_call x9 -> x10, Pallas kernels: 15.6 us -> 16.5 us  [the longest x1 2.95 us: shards(): call(first_scan_kernel, 'svvvvvvvv', [('v', shape((MOVES + 1, DS, channel...]
  transfers between devices with their start and end apart: 8 -> 8, of which waited for: 6 -> 6; matrix products, arithmetic and copies ran while one was open for 0% -> 0% of each run, Pallas kernels for 13% -> 19%
where the time goes in v4:
time: 63.1 us; the launch traced here: 62.1 us
  starting transfers between devices  29.9 us (47%)
  Pallas kernels  16.5 us (26%)
  waiting for transfers between devices  12.1 us (19%)
  local copies, waits for them, and re-layouts  2.57 us (4%)
  between operations  1 us (2%)
    all_to_all x1, starting transfers between devices, shards(): lax.all_to_all(small, 'replica', split_axis=0, concat_axis=0, tiled=True,...  7.4 us
    ppermute x1, starting transfers between devices, shards(): far_small = lax.ppermute(near_small, 'replica', across)  7.28 us
    ppermute x3, waiting for transfers between devices, shards(): lax.ppermute(sums, 'tensor', [(i, i ^ bit) for i in range(tensors)])  7.1 us
    ppermute x1, starting transfers between devices, shards(): far = lax.ppermute(near, 'replica', across)  5.98 us
    all_to_all x1, starting transfers between devices, shards(): lax.all_to_all(large, 'replica', split_axis=0, concat_axis=0, tiled=True,...  5.33 us
    ppermute x3, starting transfers between devices, shards(): lax.ppermute(sums, 'tensor', [(i, i ^ bit) for i in range(tensors)])  3.84 us
    all_to_all x1, waiting for transfers between devices, shards(): lax.all_to_all(small, 'replica', split_axis=0, concat_axis=0, tiled=True,...  3.08 us
    pallas_call x1, Pallas kernels, shards(): call(first_scan_kernel, 'svvvvvvvv', [('v', shape((MOVES + 1, DS, channel...  2.95 us
  transfers between devices with their start and end apart: 8, of which 6 were waited for; matrix products, arithmetic and copies ran while one was open for 0% of the time, Pallas kernels for 19%

profile of v4, /device:TPU:8, one launch (start us, length us, event | category | flops | bytes accessed | tf_op | source)
XLA Modules:
  0.0 62.1 jit_solution(15642441360728549982)
XLA Ops:
  0.6 0.0 copy-start.5
  0.6 1.7 %shard_map.219.own._ = bf16[192,128]{1,0:T(8,128)(2,1)} custom-call(s32[2,256]{1,0:T(2,128)} %bitcast.12, f32[3,16,1024]{2,1,0:T(8,128)} %bitcast.8, bf16[2,16,1024]{2,1,0:T(8,128)(2,1)} %x.3, bf16[2,16,512]{2,1,0:T(8,128)(2,1)} %q.1, bf16[2,16,128]{2,1,0:T(8,128)(2,1)} %nk.3, bf16[2,16,128]{2,1,0:T(8,128)(2,1)} %nv.3, f32[4,1024]{1,0:T(4,128)} %cw.1, ...), custom_call_target="tpu_custom_call" | custom-call | tf_op jit(solution)/shard_map/pallas_call | solution.py:522
  2.4 0.0 copy-start.4
  2.4 0.0 copy-start.6
  2.4 0.0 copy-start.7
  2.4 0.0 copy-start.8
  2.4 0.0 copy-start.11
  2.4 0.0 copy-start.21
  2.4 7.3 %collective-permute-start = (bf16[192,128]{1,0:T(8,128)(2,1)}, bf16[192,128]{1,0:T(8,128)(2,1)S(1)}, u32[]{:S(2)}, u32[]{:S(2)}) collective-permute-start(bf16[192,128]{1,0:T(8,128)(2,1)} %shard_map.219.own._), channel_id=1, source_target_pairs={{0,32},{8,40},{16,48},{24,56},{32,0},{40,8},{48,16},{56,24},{64,96... | collective-permute-start | bytes 147464 | tf_op jit(solution)/shard_map/ppermute | solution.py:540
  9.7 2.7 %shard_map.225.own = bf16[8,144,128]{2,1,0:T(8,128)(2,1)} custom-call(s32[2,256]{1,0:T(2,128)} %bitcast.13, f32[16,16,1024]{2,1,0:T(8,128)} %ssm.3, f32[3,16,1024]{2,1,0:T(8,128)} %bitcast.9, bf16[2,16,1024]{2,1,0:T(8,128)(2,1)} %x.3, bf16[192,128]{1,0:T(8,128)(2,1)} %shard_map.219.own._), custom_call_target="tpu_custom_call" | custom-call | tf_op jit(solution)/shard_map/pallas_call | solution.py:542
  12.4 0.1 collective-permute-start.5
  12.5 0.0 collective-permute-done.other
  12.5 0.0 copy-done.5
  12.5 0.0 copy-done.4
  12.5 1.4 %shard_map.220 = bf16[32,32,128]{2,1,0:T(8,128)(2,1)} custom-call(s32[2,256]{1,0:T(2,128)S(1)} %bitcast.14, bf16[192,128]{1,0:T(8,128)(2,1)S(1)} %copy-done.4, bf16[192,128]{1,0:T(8,128)(2,1)S(1)} %collective-permute-done.other), custom_call_target="tpu_custom_call" | custom-call | tf_op jit(solution)/shard_map/pallas_call | solution.py:558
  14.0 7.4 %all-to-all-start = ((bf16[32,32,128]{2,1,0:T(8,128)(2,1)}), bf16[32,32,128]{2,1,0:T(8,128)(2,1)S(1)}, u32[]{:S(2)}, u32[]{:S(2)}) async-start(bf16[32,32,128]{2,1,0:T(8,128)(2,1)} %shard_map.220), calls=%async_computation | async-start | bytes 524288 | tf_op jit(solution)/shard_map/all_to_all | solution.py:564
  21.4 0.0 copy-done.6
  21.4 0.0 copy-done.7
  21.4 0.0 copy-done.8
  21.4 0.0 copy-done.11
  21.4 0.0 copy-done.21
  21.4 0.0 copy-start.12
  21.4 1.2 %copy-done.12 = bf16[32,128,128]{2,1,0:T(8,128)(2,1)S(1)} copy-done((bf16[32,128,128]{2,1,0:T(8,128)(2,1)S(1)}, bf16[32,128,128]{2,1,0:T(8,128)(2,1)}, u32[]{:S(2)}) %copy-start.12) | copy-done | bytes 1048600
  22.6 1.2 %copy-done.13 = bf16[32,128,128]{2,1,0:T(8,128)(2,1)S(1)} copy-done((bf16[32,128,128]{2,1,0:T(8,128)(2,1)S(1)}, bf16[32,128,128]{2,1,0:T(8,128)(2,1)}, u32[]{:S(2)}) %copy-start.13) | copy-done | bytes 1048600
  23.9 1.4 %shard_map.223 = (f32[128,128]{1,0:T(8,128)S(1)}, bf16[8,2,256,128]{3,2,1,0:T(8,128)(2,1)S(1)}) custom-call(s32[2,256]{1,0:T(2,128)S(1)} %bitcast.15, s32[512]{0:T(512)S(1)} %copy-done.11, s32[2,16]{1,0:T(2,128)S(1)} %bitcast.27, bf16[32,128,128]{2,1,0:T(8,128)(2,1)S(1)} %copy-done.12, bf16[32,128,128]{2,1,0:T(8,128)(2,1)S(1)} %copy-done.13, ...), custom_call_target="tpu_custom_call" | custom-call | flops 4000000000 | tf_op jit(solution)/shard_map/pallas_call | solution.py:568
  25.3 3.1 %all-to-all-done.recv = bf16[32,32,128]{2,1,0:T(8,128)(2,1)S(1)} async-done(((bf16[32,32,128]{2,1,0:T(8,128)(2,1)}), bf16[32,32,128]{2,1,0:T(8,128)(2,1)S(1)}, u32[]{:S(2)}, u32[]{:S(2)}) %all-to-all-start) | async-done | bytes 262176 | tf_op jit(solution)/shard_map/all_to_all | solution.py:564
  28.3 1.1 %shard_map.224._.near = bf16[64,128]{1,0:T(8,128)(2,1)S(1)} custom-call(s32[2,256]{1,0:T(2,128)S(1)} %bitcast.16, s32[512]{0:T(512)S(1)} %copy-done.11, bf16[32,32,128]{2,1,0:T(8,128)(2,1)S(1)} %all-to-all-done.recv, bf16[8,2,256,128]{3,2,1,0:T(8,128)(2,1)S(1)} %get-tuple-element.29.kept, bf16[2,16,128]{2,1,0:T(8,128)(2,1)S(1)} %copy-done.6, ...), custom_call_target="tpu_custom_call" | custom-call | tf_op jit(solution)/shard_map/pallas_call | solution.py:578
  29.5 6.0 %collective-permute-start.4 = (bf16[64,128]{1,0:T(8,128)(2,1)S(1)}, bf16[64,128]{1,0:T(8,128)(2,1)S(1)}, u32[]{:S(2)}, u32[]{:S(2)}) collective-permute-start(bf16[64,128]{1,0:T(8,128)(2,1)S(1)} %shard_map.224._.near), channel_id=1, source_target_pairs={{0,32},{8,40},{16,48},{24,56},{32,0},{40,8},{48,16},{56,24},{64,96... | collective-permute-start | bytes 49160 | tf_op jit(solution)/shard_map/ppermute | solution.py:591
  35.4 0.0 collective-permute-done.5.other
  35.4 0.0 copy-done.1
  35.4 1.4 %shard_map.226._ = bf16[32,160,128]{2,1,0:T(8,128)(2,1)} custom-call(s32[2,256]{1,0:T(2,128)S(1)} %bitcast.17, bf16[8,144,128]{2,1,0:T(8,128)(2,1)S(1)} %copy-done.1, bf16[8,144,128]{2,1,0:T(8,128)(2,1)S(1)} %collective-permute-done.5.other, bf16[64,128]{1,0:T(8,128)(2,1)S(1)} %shard_map.224._.near), custom_call_target="tpu_custom_call" | custom-call | tf_op jit(solution)/shard_map/pallas_call | solution.py:600
  36.9 0.3 collective-permute-done.4.far
  37.2 1.3 %shard_map.227 = bf16[32,160,128]{2,1,0:T(8,128)(2,1)} custom-call(s32[2,256]{1,0:T(2,128)S(1)} %bitcast.18, bf16[64,128]{1,0:T(8,128)(2,1)S(1)} %shard_map.224._.near, bf16[64,128]{1,0:T(8,128)(2,1)S(1)} %collective-permute-done.4.far, bf16[32,160,128]{2,1,0:T(8,128)(2,1)} %shard_map.226._), custom_call_target="tpu_custom_call", output_to_operand_aliasing={{}: (3, {})} | custom-call | tf_op jit(solution)/shard_map/pallas_call | solution.py:606
  38.5 0.0 copy-start
  38.5 0.0 copy-start.3
  38.5 0.0 copy-start.9
  38.5 0.0 copy-start.10
  38.6 0.0 copy-start.14
  38.6 0.0 copy-start.16
  38.6 5.3 %all-to-all-start.1 = ((bf16[32,160,128]{2,1,0:T(8,128)(2,1)}), bf16[32,160,128]{2,1,0:T(8,128)(2,1)S(1)}, u32[]{:S(2)}, u32[]{:S(2)}) async-start(bf16[32,160,128]{2,1,0:T(8,128)(2,1)} %shard_map.227), calls=%async_computation.1 | async-start | bytes 2621440 | tf_op jit(solution)/shard_map/all_to_all | solution.py:613
  43.9 0.0 copy-done
  43.9 0.0 copy-done.3
  43.9 0.0 copy-done.9
  43.9 0.0 copy-done.10
  43.9 0.0 copy-done.14
  44.0 0.0 copy-done.16
  44.0 0.0 copy-start.2
  44.0 0.0 copy-start.15
  44.0 0.0 copy-start.17
  44.0 0.0 copy-start.18
  44.0 0.0 copy-start.19
  44.0 0.0 copy-start.20
  44.0 0.9 %shard_map.221 = (f32[64,256]{1,0:T(8,128)S(1)}, f32[48,1024]{1,0:T(8,128)S(1)}) custom-call(s32[2,256]{1,0:T(2,128)S(1)} %bitcast.19, bf16[32,32,128]{2,1,0:T(8,128)(2,1)S(1)} %all-to-all-done.recv, f32[3,16,1024]{2,1,0:T(8,128)S(1)} %bitcast.10, bf16[2,16,1024]{2,1,0:T(8,128)(2,1)S(1)} %copy-done.3, f32[4,1024]{1,0:T(4,128)S(1)} %copy-done.9, ...), custom_call_target="tpu_custom_call" | custom-call | flops 2000000000 | tf_op jit(solution)/shard_map/pallas_call | solution.py:593
  44.9 0.1 collective-permute-start.1
  45.0 1.2 %collective-permute-done.1 = f32[64,256]{1,0:T(8,128)S(1)} collective-permute-done((f32[64,256]{1,0:T(8,128)S(1)}, f32[64,256]{1,0:T(8,128)S(1)}, u32[]{:S(2)}, u32[]{:S(2)}) %collective-permute-start.1) | collective-permute-done | bytes 65568 | tf_op jit(solution)/shard_map/ppermute | solution.py:619
  46.3 1.6 %collective-permute-start.2 = (f32[64,256]{1,0:T(8,128)S(1)}, f32[64,256]{1,0:T(8,128)S(1)}, u32[]{:S(2)}, u32[]{:S(2)}) collective-permute-start(f32[64,256]{1,0:T(8,128)S(1)} %add.9), channel_id=1, source_target_pairs={{0,2},{1,3},{2,0},{3,1},{4,6},{5,7},{6,4},{7,5},{8,10},{9,11},{10,... | collective-permute-start | bytes 196616 | tf_op jit(solution)/shard_map/ppermute | solution.py:619
  47.9 2.8 %collective-permute-done.2 = f32[64,256]{1,0:T(8,128)S(1)} collective-permute-done((f32[64,256]{1,0:T(8,128)S(1)}, f32[64,256]{1,0:T(8,128)S(1)}, u32[]{:S(2)}, u32[]{:S(2)}) %collective-permute-start.2) | collective-permute-done | bytes 65568 | tf_op jit(solution)/shard_map/ppermute | solution.py:619
  50.7 2.2 %collective-permute-start.3 = (f32[64,256]{1,0:T(8,128)S(1)}, f32[64,256]{1,0:T(8,128)S(1)}, u32[]{:S(2)}, u32[]{:S(2)}) collective-permute-start(f32[64,256]{1,0:T(8,128)S(1)} %add.10), channel_id=1, source_target_pairs={{0,4},{1,5},{2,6},{3,7},{4,0},{5,1},{6,2},{7,3},{8,12},{9,13},{10,... | collective-permute-start | bytes 196616 | tf_op jit(solution)/shard_map/ppermute | solution.py:619
  52.8 3.1 %collective-permute-done.3 = f32[64,256]{1,0:T(8,128)S(1)} collective-permute-done((f32[64,256]{1,0:T(8,128)S(1)}, f32[64,256]{1,0:T(8,128)S(1)}, u32[]{:S(2)}, u32[]{:S(2)}) %collective-permute-start.3) | collective-permute-done | bytes 65568 | tf_op jit(solution)/shard_map/ppermute | solution.py:619
  55.9 0.0 copy-done.2
  55.9 0.0 copy-done.15
  56.0 3.0 %shard_map.222 = (f32[9,16,1024]{2,1,0:T(8,128)S(1)}, f32[9,16,1024]{2,1,0:T(8,128)S(1)}, f32[9,16,128]{2,1,0:T(8,128)S(1)}, bf16[16,1024]{1,0:T(8,128)(2,1)S(1)...) custom-call(s32[2,256]{1,0:T(2,128)S(1)} %bitcast.20, ...), custom_call_target="tpu_custom_call" | custom-call | flops 3000000000 | tf_op jit(solution)/shard_map/pallas_call | solution.py:622
  59.0 1.6 %all-to-all-done.1.recv = bf16[32,160,128]{2,1,0:T(8,128)(2,1)S(1)} async-done(((bf16[32,160,128]{2,1,0:T(8,128)(2,1)}), bf16[32,160,128]{2,1,0:T(8,128)(2,1)S(1)}, u32[]{:S(2)}, u32[]{:S(2)}) %all-to-all-start.1) | async-done | bytes 1310752 | tf_op jit(solution)/shard_map/all_to_all | solution.py:613
  60.5 1.6 %shard_map.228 = (f32[16,16,1024]{2,1,0:T(8,128)}, bf16[2,16,1024]{2,1,0:T(8,128)(2,1)}, f32[3,16,1024]{2,1,0:T(8,128)}, bf16[2,16,512]{2,1,0:T(8,128)(2,1)}) custom-call(s32[2,256]{1,0:T(2,128)S(1)} %bitcast.21, f32[9,16,1024]{2,1,0:T(8,128)S(1)} %get-tuple-element.22.factor, ...), custom_call_target="tpu_custom_call", output_to_operand_aliasing={{0}: (12, {})} | custom-call | tf_op jit(solution)/shard_map/pallas_call | solution.py:645
  (9 shorter events, 0.0 us)
Async XLA Ops:
  0.6 11.9 %copy-start.5 = (s32[256,2]{0,1:T(2,128)S(1)}, s32[256,2]{0,1:T(2,128)}, u32[]{:S(2)}) copy-start(s32[256,2]{0,1:T(2,128)} %param.39) | copy-start | bytes 6148
  2.4 10.2 %copy-start.4 = (bf16[192,128]{1,0:T(8,128)(2,1)S(1)}, bf16[192,128]{1,0:T(8,128)(2,1)}, u32[]{:S(2)}) copy-start(bf16[192,128]{1,0:T(8,128)(2,1)} %shard_map.219.own._) | copy-start | bytes 147460
  2.4 19.0 %copy-start.6 = (bf16[2,16,128]{2,1,0:T(8,128)(2,1)S(1)}, bf16[2,16,128]{2,1,0:T(8,128)(2,1)}, u32[]{:S(2)}) copy-start(bf16[2,16,128]{2,1,0:T(8,128)(2,1)} %nk.3) | copy-start | bytes 24580
  2.4 19.0 %copy-start.7 = (bf16[2,16,128]{2,1,0:T(8,128)(2,1)S(1)}, bf16[2,16,128]{2,1,0:T(8,128)(2,1)}, u32[]{:S(2)}) copy-start(bf16[2,16,128]{2,1,0:T(8,128)(2,1)} %nv.3) | copy-start | bytes 24580
  2.4 19.0 %copy-start.8 = (bf16[2,16,512]{2,1,0:T(8,128)(2,1)S(1)}, bf16[2,16,512]{2,1,0:T(8,128)(2,1)}, u32[]{:S(2)}) copy-start(bf16[2,16,512]{2,1,0:T(8,128)(2,1)} %q.1) | copy-start | bytes 98308
  2.4 19.0 %copy-start.11 = (s32[512]{0:T(512)S(1)}, s32[512]{0:T(512)}, u32[]{:S(2)}) copy-start(s32[512]{0:T(512)} %lens.3) | copy-start | bytes 6148
  2.4 19.0 %copy-start.21 = (s32[16,2]{0,1:T(2,128)S(1)}, s32[16,2]{0,1:T(2,128)}, u32[]{:S(2)}) copy-start(s32[16,2]{0,1:T(2,128)} %param.21) | copy-start | bytes 388
  2.4 10.1 %collective-permute-start = (bf16[192,128]{1,0:T(8,128)(2,1)}, bf16[192,128]{1,0:T(8,128)(2,1)S(1)}, u32[]{:S(2)}, u32[]{:S(2)}) collective-permute-start(bf16[192,128]{1,0:T(8,128)(2,1)} %shard_map.219.own._), channel_id=1, source_target_pairs={{0,32},{8,40},{16,48},{24,56},{32,0},{40,8},{48,16},{56,24},{64,96... | collective-permute-start | bytes 147464 | tf_op jit(solution)/shard_map/ppermute | solution.py:540
  12.4 23.0 %collective-permute-start.5 = (bf16[8,144,128]{2,1,0:T(8,128)(2,1)}, bf16[8,144,128]{2,1,0:T(8,128)(2,1)S(1)}, u32[]{:S(2)}, u32[]{:S(2)}) collective-permute-start(bf16[8,144,128]{2,1,0:T(8,128)(2,1)} %shard_map.225.own), channel_id=1, source_target_pairs={{0,32},{8,40},{16,48},{24,56},{32,0},{40,8},{48,16},{56,24},{64,96... | collective-permute-start | bytes 884744 | tf_op jit(solution)/shard_map/ppermute | solution.py:556
  14.0 14.4 %all-to-all-start = ((bf16[32,32,128]{2,1,0:T(8,128)(2,1)}), bf16[32,32,128]{2,1,0:T(8,128)(2,1)S(1)}, u32[]{:S(2)}, u32[]{:S(2)}) async-start(bf16[32,32,128]{2,1,0:T(8,128)(2,1)} %shard_map.220), calls=%async_computation | async-start | bytes 524288 | tf_op jit(solution)/shard_map/all_to_all | solution.py:564
  21.4 1.2 %copy-start.12 = (bf16[32,128,128]{2,1,0:T(8,128)(2,1)S(1)}, bf16[32,128,128]{2,1,0:T(8,128)(2,1)}, u32[]{:S(2)}) copy-start(bf16[32,128,128]{2,1,0:T(8,128)(2,1)} %keys.1) | copy-start | bytes 3145732
  22.6 1.2 %copy-start.13 = (bf16[32,128,128]{2,1,0:T(8,128)(2,1)S(1)}, bf16[32,128,128]{2,1,0:T(8,128)(2,1)}, u32[]{:S(2)}) copy-start(bf16[32,128,128]{2,1,0:T(8,128)(2,1)} %values.1) | copy-start | bytes 3145732
  25.3 10.2 %copy-start.1 = (bf16[8,144,128]{2,1,0:T(8,128)(2,1)S(1)}, bf16[8,144,128]{2,1,0:T(8,128)(2,1)}, u32[]{:S(2)}) copy-start(bf16[8,144,128]{2,1,0:T(8,128)(2,1)} %shard_map.225.own) | copy-start | bytes 884740
  29.5 7.7 %collective-permute-start.4 = (bf16[64,128]{1,0:T(8,128)(2,1)S(1)}, bf16[64,128]{1,0:T(8,128)(2,1)S(1)}, u32[]{:S(2)}, u32[]{:S(2)}) collective-permute-start(bf16[64,128]{1,0:T(8,128)(2,1)S(1)} %shard_map.224._.near), channel_id=1, source_target_pairs={{0,32},{8,40},{16,48},{24,56},{32,0},{40,8},{48,16},{56,24},{64,96... | collective-permute-start | bytes 49160 | tf_op jit(solution)/shard_map/ppermute | solution.py:591
  38.5 5.4 %copy-start = (f32[16,3,1024]{2,0,1:T(8,128)S(1)}, f32[16,3,1024]{2,0,1:T(8,128)}, u32[]{:S(2)}) copy-start(f32[16,3,1024]{2,0,1:T(8,128)} %param.27) | copy-start | bytes 589828
  38.5 5.4 %copy-start.3 = (bf16[2,16,1024]{2,1,0:T(8,128)(2,1)S(1)}, bf16[2,16,1024]{2,1,0:T(8,128)(2,1)}, u32[]{:S(2)}) copy-start(bf16[2,16,1024]{2,1,0:T(8,128)(2,1)} %x.3) | copy-start | bytes 196612
  38.5 5.4 %copy-start.9 = (f32[4,1024]{1,0:T(4,128)S(1)}, f32[4,1024]{1,0:T(4,128)}, u32[]{:S(2)}) copy-start(f32[4,1024]{1,0:T(4,128)} %cw.1) | copy-start | bytes 49156
  38.5 5.4 %copy-start.10 = (f32[1024]{0:T(1024)S(1)}, f32[1024]{0:T(1024)}, u32[]{:S(2)}) copy-start(f32[1024]{0:T(1024)} %param.32) | copy-start | bytes 12292
  38.6 5.4 %copy-start.14 = (bf16[1024,256]{1,0:T(8,128)(2,1)S(1)}, bf16[1024,256]{1,0:T(8,128)(2,1)}, u32[]{:S(2)}) copy-start(bf16[1024,256]{1,0:T(8,128)(2,1)} %down.1) | copy-start | bytes 1572868
  38.6 5.4 %copy-start.16 = (bf16[1024,32]{0,1:T(8,128)(2,1)S(1)}, bf16[1024,32]{0,1:T(8,128)(2,1)}, u32[]{:S(2)}) copy-start(bf16[1024,32]{0,1:T(8,128)(2,1)} %param.34) | copy-start | bytes 196612
  38.6 21.9 %all-to-all-start.1 = ((bf16[32,160,128]{2,1,0:T(8,128)(2,1)}), bf16[32,160,128]{2,1,0:T(8,128)(2,1)S(1)}, u32[]{:S(2)}, u32[]{:S(2)}) async-start(bf16[32,160,128]{2,1,0:T(8,128)(2,1)} %shard_map.227), calls=%async_computation.1 | async-start | bytes 2621440 | tf_op jit(solution)/shard_map/all_to_all | solution.py:613
  44.0 12.0 %copy-start.2 = (f32[16,16,1024]{2,1,0:T(8,128)S(1)}, f32[16,16,1024]{2,1,0:T(8,128)}, u32[]{:S(2)}) copy-start(f32[16,16,1024]{2,1,0:T(8,128)} %ssm.3) | copy-start | bytes 3145732
  44.0 12.0 %copy-start.15 = (bf16[256,1024]{1,0:T(8,128)(2,1)S(1)}, bf16[256,1024]{1,0:T(8,128)(2,1)}, u32[]{:S(2)}) copy-start(bf16[256,1024]{1,0:T(8,128)(2,1)} %up.1) | copy-start | bytes 1572868
  44.0 12.0 %copy-start.17 = (bf16[2,16,1024]{2,1,0:T(8,128)(2,1)S(1)}, bf16[2,16,1024]{2,1,0:T(8,128)(2,1)}, u32[]{:S(2)}) copy-start(bf16[2,16,1024]{2,1,0:T(8,128)(2,1)} %z.1) | copy-start | bytes 196612
  44.0 12.0 %copy-start.18 = (f32[16,1024]{1,0:T(8,128)S(1)}, f32[16,1024]{1,0:T(8,128)}, u32[]{:S(2)}) copy-start(f32[16,1024]{1,0:T(8,128)} %alog.1) | copy-start | bytes 196612
  44.0 12.0 %copy-start.19 = (f32[1024]{0:T(1024)S(1)}, f32[1024]{0:T(1024)}, u32[]{:S(2)}) copy-start(f32[1024]{0:T(1024)} %param.36) | copy-start | bytes 12292
  44.0 12.0 %copy-start.20 = (f32[1024]{0:T(1024)S(1)}, f32[1024]{0:T(1024)}, u32[]{:S(2)}) copy-start(f32[1024]{0:T(1024)} %param.38) | copy-start | bytes 12292
  44.9 1.3 %collective-permute-start.1 = (f32[64,256]{1,0:T(8,128)S(1)}, f32[64,256]{1,0:T(8,128)S(1)}, u32[]{:S(2)}, u32[]{:S(2)}) collective-permute-start(f32[64,256]{1,0:T(8,128)S(1)} %get-tuple-element.20), channel_id=1, source_target_pairs={{0,1},{1,0},{2,3},{3,2},{4,5},{5,4},{6,7},{7,6},{8,9},{9,8},{10,11... | collective-permute-start | bytes 196616 | tf_op jit(solution)/shard_map/ppermute | solution.py:619
  46.3 4.4 %collective-permute-start.2 = (f32[64,256]{1,0:T(8,128)S(1)}, f32[64,256]{1,0:T(8,128)S(1)}, u32[]{:S(2)}, u32[]{:S(2)}) collective-permute-start(f32[64,256]{1,0:T(8,128)S(1)} %add.9), channel_id=1, source_target_pairs={{0,2},{1,3},{2,0},{3,1},{4,6},{5,7},{6,4},{7,5},{8,10},{9,11},{10,... | collective-permute-start | bytes 196616 | tf_op jit(solution)/shard_map/ppermute | solution.py:619
  50.7 5.3 %collective-permute-start.3 = (f32[64,256]{1,0:T(8,128)S(1)}, f32[64,256]{1,0:T(8,128)S(1)}, u32[]{:S(2)}, u32[]{:S(2)}) collective-permute-start(f32[64,256]{1,0:T(8,128)S(1)} %add.10), channel_id=1, source_target_pairs={{0,4},{1,5},{2,6},{3,7},{4,0},{5,1},{6,2},{7,3},{8,12},{9,13},{10,... | collective-permute-start | bytes 196616 | tf_op jit(solution)/shard_map/ppermute | solution.py:619

commit v5 on v4

--- a/solution.py
+++ b/solution.py
@@ -16,9 +16,9 @@
 PIECES = 8
 STATE_ROWS = DS * PIECES
 PAIR_ROWS = 2 * PIECES
-SMALL_ROWS = PAIR_ROWS + 16
+SMALL_ROWS = PAIR_ROWS + 8
 HELD_ROWS = STATE_ROWS + PAIR_ROWS
-LARGE_ROWS = HELD_ROWS + 16
+LARGE_ROWS = HELD_ROWS + 8
 REPLICAS = 32
 FAR = 4
 PLANE = 16
@@ -96,7 +96,7 @@
     pieces = cut([mixed, later])
     pieces += [nk[...].astype(F32), nv[...].astype(F32), zero, zero]
     pieces += [q[:, h * HD : (h + 1) * HD].astype(F32) for h in range(HEADS)]
-    width = PAIR_ROWS + 8
+    width = SMALL_ROWS
     for i in range(width):
         small[pl.ds(i, SLOTS, stride=width), :] = pieces[i]
     back = []
@@ -114,7 +114,6 @@
 
 def route_small_kernel(moves, own, other, send):
     me = lax.axis_index("replica")
-    blank = jnp.zeros((8, HD), F32)
     for j in range(MOVES):
         _, target = out_move(me, moves, j)
         flip = crosses(me, target)
@@ -129,8 +128,7 @@
         start = MOVES * 16 + j // 2 * 16
         lines = slice(start, start + 16)
         both = jnp.where(flip == 1, other[lines, :], own[lines, :]).astype(F32)
-        part = both[j % 2 * 8 : j % 2 * 8 + 8, :]
-        send[to, PAIR_ROWS:, :] = jnp.concatenate([part, blank], axis=0).astype(BF)
+        send[to, PAIR_ROWS:, :] = both[j % 2 * 8 : j % 2 * 8 + 8, :].astype(BF)
 
 
 def pack_state_kernel(moves, ssm, conv_in, x_in, _, send, held, conv, x, small, arrived, read):
@@ -243,7 +241,7 @@
     for j in range(MOVES):
         slot, target = out_move(me, moves, j)
         flip = crosses(me, target)
-        got = recv[place(target) * 2 + flip, PAIR_ROWS:, :].astype(F32)[:8, :]
+        got = recv[place(target) * 2 + flip, PAIR_ROWS:, :].astype(F32)
         qs[j * 8 : j * 8 + 8, :] = got
         start = pl.multiple_of(slot * 8, 8)
         first_k.append(fk[pl.ds(start, 8), :])
@@ -283,7 +281,6 @@
 
 def route_results_kernel(moves, near, far, _, send, blocks, sent):
     me = lax.axis_index("replica")
-    blank = jnp.zeros((8, HD), F32)
     copies = []
     for j in range(MOVES):
         _, target = out_move(me, moves, j)
@@ -291,9 +288,8 @@
         _, target = out_move(me ^ (flip * FAR), moves, j)
         lines = slice(j // 2 * 16, j // 2 * 16 + 16)
         both = jnp.where(flip == 1, far[lines, :], near[lines, :]).astype(F32)
-        part = both[j % 2 * 8 : j % 2 * 8 + 8, :]
-        blocks[j] = jnp.concatenate([part, blank], axis=0).astype(BF)
-        goal = send.at[place(target) * 2 + flip, pl.ds(HELD_ROWS, 16), :]
+        blocks[j] = both[j % 2 * 8 : j % 2 * 8 + 8, :].astype(BF)
+        goal = send.at[place(target) * 2 + flip, pl.ds(HELD_ROWS, 8), :]
         copies.append(pltpu.make_async_copy(blocks.at[j], goal, sent.at[j]))
         copies[j].start()
     for copy in copies:
@@ -450,7 +446,7 @@
         read = jnp.concatenate([maps[j]] * PIECES, axis=1) * state
         start = pl.multiple_of(slot * 8, 8)
         yrows[pl.ds(start, 8), :] = lay(jnp.sum(read, axis=0, keepdims=True))
-        result = came[HELD_ROWS:, :].astype(F32)[:8, :]
+        result = came[HELD_ROWS:, :].astype(F32)
         lines[pl.ds(start, 8), :] = jnp.where(second, result, lines[pl.ds(start, 8), :])
         start = pl.multiple_of(slot * PAIR_ROWS, PAIR_ROWS)
         rows[pl.ds(start, PAIR_ROWS), :] = came[STATE_ROWS:HELD_ROWS, :].astype(F32)
@@ -607,7 +603,7 @@
         route_results_kernel,
         "svva",
         [("a", shape((REPLICAS, LARGE_ROWS, HD), BF))],
-        [pltpu.VMEM((MOVES, 16, HD), BF), pltpu.SemaphoreType.DMA((MOVES,))],
+        [pltpu.VMEM((MOVES, 8, HD), BF), pltpu.SemaphoreType.DMA((MOVES,))],
         aliases={3: 0},
     )(moves, near, far, large)
     large = lax.all_to_all(

time: 63.1 us -> 62.1 us (0.984)
  waiting for transfers between devices: 12.1 us -> 11 us
    all_to_all x1, waiting for transfers between devices: 1.58 us -> 0.77 us  [shards(): lax.all_to_all(large, 'replica', split_axis=0, concat_axis=0, tiled=True,...]
where the time goes in v5:
time: 62.1 us; the launch traced here: 60.9 us
  starting transfers between devices  29.8 us (48%)
  Pallas kernels  16.5 us (27%)
  waiting for transfers between devices  11 us (18%)
  local copies, waits for them, and re-layouts  2.57 us (4%)
  between operations  1.01 us (2%)
    all_to_all x1, starting transfers between devices, shards(): lax.all_to_all(small, 'replica', split_axis=0, concat_axis=0, tiled=True,...  7.39 us
    ppermute x1, starting transfers between devices, shards(): far_small = lax.ppermute(near_small, 'replica', across)  7.27 us
    ppermute x3, waiting for transfers between devices, shards(): lax.ppermute(sums, 'tensor', [(i, i ^ bit) for i in range(tensors)])  7.06 us
    ppermute x1, starting transfers between devices, shards(): far = lax.ppermute(near, 'replica', across)  5.93 us
    all_to_all x1, starting transfers between devices, shards(): lax.all_to_all(large, 'replica', split_axis=0, concat_axis=0, tiled=True,...  5.22 us
    ppermute x3, starting transfers between devices, shards(): lax.ppermute(sums, 'tensor', [(i, i ^ bit) for i in range(tensors)])  3.88 us
    pallas_call x1, Pallas kernels, shards(): call(first_scan_kernel, 'svvvvvvvv', [('v', shape((MOVES + 1, DS, channel...  2.95 us
    all_to_all x1, waiting for transfers between devices, shards(): lax.all_to_all(small, 'replica', split_axis=0, concat_axis=0, tiled=True,...  2.81 us
  transfers between devices with their start and end apart: 8, of which 6 were waited for; matrix products, arithmetic and copies ran while one was open for 0% of the time, Pallas kernels for 19%

profile of v5, /device:TPU:8, one launch (start us, length us, event | category | flops | bytes accessed | tf_op | source)
XLA Modules:
  0.0 60.9 jit_solution(6646358210888810477)
XLA Ops:
  0.6 0.0 copy-start.5
  0.6 1.7 %shard_map.219.own._ = bf16[192,128]{1,0:T(8,128)(2,1)} custom-call(s32[2,256]{1,0:T(2,128)} %bitcast.12, f32[3,16,1024]{2,1,0:T(8,128)} %bitcast.8, bf16[2,16,1024]{2,1,0:T(8,128)(2,1)} %x.3, bf16[2,16,512]{2,1,0:T(8,128)(2,1)} %q.1, bf16[2,16,128]{2,1,0:T(8,128)(2,1)} %nk.3, bf16[2,16,128]{2,1,0:T(8,128)(2,1)} %nv.3, f32[4,1024]{1,0:T(4,128)} %cw.1, ...), custom_call_target="tpu_custom_call" | custom-call | tf_op jit(solution)/shard_map/pallas_call | solution.py:518
  2.4 0.0 copy-start.4
  2.4 0.0 copy-start.6
  2.4 0.0 copy-start.7
  2.4 0.0 copy-start.8
  2.4 0.0 copy-start.11
  2.4 0.0 copy-start.21
  2.4 7.3 %collective-permute-start = (bf16[192,128]{1,0:T(8,128)(2,1)}, bf16[192,128]{1,0:T(8,128)(2,1)S(1)}, u32[]{:S(2)}, u32[]{:S(2)}) collective-permute-start(bf16[192,128]{1,0:T(8,128)(2,1)} %shard_map.219.own._), channel_id=1, source_target_pairs={{0,32},{8,40},{16,48},{24,56},{32,0},{40,8},{48,16},{56,24},{64,96... | collective-permute-start | bytes 147464 | tf_op jit(solution)/shard_map/ppermute | solution.py:536
  9.7 2.7 %shard_map.225.own = bf16[8,144,128]{2,1,0:T(8,128)(2,1)} custom-call(s32[2,256]{1,0:T(2,128)} %bitcast.13, f32[16,16,1024]{2,1,0:T(8,128)} %ssm.3, f32[3,16,1024]{2,1,0:T(8,128)} %bitcast.9, bf16[2,16,1024]{2,1,0:T(8,128)(2,1)} %x.3, bf16[192,128]{1,0:T(8,128)(2,1)} %shard_map.219.own._), custom_call_target="tpu_custom_call" | custom-call | tf_op jit(solution)/shard_map/pallas_call | solution.py:538
  12.4 0.1 collective-permute-start.5
  12.5 0.0 collective-permute-done.other
  12.5 0.0 copy-done.5
  12.5 0.0 copy-done.4
  12.5 1.4 %shard_map.220 = bf16[32,24,128]{2,1,0:T(8,128)(2,1)} custom-call(s32[2,256]{1,0:T(2,128)S(1)} %bitcast.14, bf16[192,128]{1,0:T(8,128)(2,1)S(1)} %copy-done.4, bf16[192,128]{1,0:T(8,128)(2,1)S(1)} %collective-permute-done.other), custom_call_target="tpu_custom_call" | custom-call | tf_op jit(solution)/shard_map/pallas_call | solution.py:554
  14.0 7.4 %all-to-all-start = ((bf16[32,24,128]{2,1,0:T(8,128)(2,1)}), bf16[32,24,128]{2,1,0:T(8,128)(2,1)S(1)}, u32[]{:S(2)}, u32[]{:S(2)}) async-start(bf16[32,24,128]{2,1,0:T(8,128)(2,1)} %shard_map.220), calls=%async_computation | async-start | bytes 393216 | tf_op jit(solution)/shard_map/all_to_all | solution.py:560
  21.3 0.0 copy-done.6
  21.4 0.0 copy-done.7
  21.4 0.0 copy-done.8
  21.4 0.0 copy-done.11
  21.4 0.0 copy-done.21
  21.4 0.0 copy-start.12
  21.4 1.2 %copy-done.12 = bf16[32,128,128]{2,1,0:T(8,128)(2,1)S(1)} copy-done((bf16[32,128,128]{2,1,0:T(8,128)(2,1)S(1)}, bf16[32,128,128]{2,1,0:T(8,128)(2,1)}, u32[]{:S(2)}) %copy-start.12) | copy-done | bytes 1048600
  22.6 1.2 %copy-done.13 = bf16[32,128,128]{2,1,0:T(8,128)(2,1)S(1)} copy-done((bf16[32,128,128]{2,1,0:T(8,128)(2,1)S(1)}, bf16[32,128,128]{2,1,0:T(8,128)(2,1)}, u32[]{:S(2)}) %copy-start.13) | copy-done | bytes 1048600
  23.8 1.4 %shard_map.223 = (f32[128,128]{1,0:T(8,128)S(1)}, bf16[8,2,256,128]{3,2,1,0:T(8,128)(2,1)S(1)}) custom-call(s32[2,256]{1,0:T(2,128)S(1)} %bitcast.15, s32[512]{0:T(512)S(1)} %copy-done.11, s32[2,16]{1,0:T(2,128)S(1)} %bitcast.27, bf16[32,128,128]{2,1,0:T(8,128)(2,1)S(1)} %copy-done.12, bf16[32,128,128]{2,1,0:T(8,128)(2,1)S(1)} %copy-done.13, ...), custom_call_target="tpu_custom_call" | custom-call | flops 4000000000 | tf_op jit(solution)/shard_map/pallas_call | solution.py:564
  25.3 2.8 %all-to-all-done.recv = bf16[32,24,128]{2,1,0:T(8,128)(2,1)S(1)} async-done(((bf16[32,24,128]{2,1,0:T(8,128)(2,1)}), bf16[32,24,128]{2,1,0:T(8,128)(2,1)S(1)}, u32[]{:S(2)}, u32[]{:S(2)}) %all-to-all-start) | async-done | bytes 196640 | tf_op jit(solution)/shard_map/all_to_all | solution.py:560
  28.1 1.1 %shard_map.224._.near = bf16[64,128]{1,0:T(8,128)(2,1)S(1)} custom-call(s32[2,256]{1,0:T(2,128)S(1)} %bitcast.16, s32[512]{0:T(512)S(1)} %copy-done.11, bf16[32,24,128]{2,1,0:T(8,128)(2,1)S(1)} %all-to-all-done.recv, bf16[8,2,256,128]{3,2,1,0:T(8,128)(2,1)S(1)} %get-tuple-element.29.kept, bf16[2,16,128]{2,1,0:T(8,128)(2,1)S(1)} %copy-done.6, ...), custom_call_target="tpu_custom_call" | custom-call | tf_op jit(solution)/shard_map/pallas_call | solution.py:574
  29.2 5.9 %collective-permute-start.4 = (bf16[64,128]{1,0:T(8,128)(2,1)S(1)}, bf16[64,128]{1,0:T(8,128)(2,1)S(1)}, u32[]{:S(2)}, u32[]{:S(2)}) collective-permute-start(bf16[64,128]{1,0:T(8,128)(2,1)S(1)} %shard_map.224._.near), channel_id=1, source_target_pairs={{0,32},{8,40},{16,48},{24,56},{32,0},{40,8},{48,16},{56,24},{64,96... | collective-permute-start | bytes 49160 | tf_op jit(solution)/shard_map/ppermute | solution.py:587
  35.1 0.0 collective-permute-done.5.other
  35.1 0.0 copy-done.1
  35.1 1.4 %shard_map.226._ = bf16[32,152,128]{2,1,0:T(8,128)(2,1)} custom-call(s32[2,256]{1,0:T(2,128)S(1)} %bitcast.17, bf16[8,144,128]{2,1,0:T(8,128)(2,1)S(1)} %copy-done.1, bf16[8,144,128]{2,1,0:T(8,128)(2,1)S(1)} %collective-permute-done.5.other, bf16[64,128]{1,0:T(8,128)(2,1)S(1)} %shard_map.224._.near), custom_call_target="tpu_custom_call" | custom-call | tf_op jit(solution)/shard_map/pallas_call | solution.py:596
  36.5 0.4 collective-permute-done.4.far
  36.9 1.3 %shard_map.227 = bf16[32,152,128]{2,1,0:T(8,128)(2,1)} custom-call(s32[2,256]{1,0:T(2,128)S(1)} %bitcast.18, bf16[64,128]{1,0:T(8,128)(2,1)S(1)} %shard_map.224._.near, bf16[64,128]{1,0:T(8,128)(2,1)S(1)} %collective-permute-done.4.far, bf16[32,152,128]{2,1,0:T(8,128)(2,1)} %shard_map.226._), custom_call_target="tpu_custom_call", output_to_operand_aliasing={{}: (3, {})} | custom-call | tf_op jit(solution)/shard_map/pallas_call | solution.py:602
  38.2 0.0 copy-start
  38.2 0.0 copy-start.3
  38.3 0.0 copy-start.9
  38.3 0.0 copy-start.10
  38.3 0.0 copy-start.14
  38.3 0.0 copy-start.16
  38.3 5.2 %all-to-all-start.1 = ((bf16[32,152,128]{2,1,0:T(8,128)(2,1)}), bf16[32,152,128]{2,1,0:T(8,128)(2,1)S(1)}, u32[]{:S(2)}, u32[]{:S(2)}) async-start(bf16[32,152,128]{2,1,0:T(8,128)(2,1)} %shard_map.227), calls=%async_computation.1 | async-start | bytes 2490368 | tf_op jit(solution)/shard_map/all_to_all | solution.py:609
  43.5 0.0 copy-done
  43.5 0.0 copy-done.3
  43.5 0.0 copy-done.9
  43.5 0.0 copy-done.10
  43.6 0.0 copy-done.14
  43.6 0.0 copy-done.16
  43.6 0.0 copy-start.2
  43.6 0.0 copy-start.15
  43.6 0.0 copy-start.17
  43.6 0.0 copy-start.18
  43.6 0.0 copy-start.19
  43.6 0.0 copy-start.20
  43.6 0.9 %shard_map.221 = (f32[64,256]{1,0:T(8,128)S(1)}, f32[48,1024]{1,0:T(8,128)S(1)}) custom-call(s32[2,256]{1,0:T(2,128)S(1)} %bitcast.19, bf16[32,24,128]{2,1,0:T(8,128)(2,1)S(1)} %all-to-all-done.recv, f32[3,16,1024]{2,1,0:T(8,128)S(1)} %bitcast.10, bf16[2,16,1024]{2,1,0:T(8,128)(2,1)S(1)} %copy-done.3, f32[4,1024]{1,0:T(4,128)S(1)} %copy-done.9, ...), custom_call_target="tpu_custom_call" | custom-call | flops 2000000000 | tf_op jit(solution)/shard_map/pallas_call | solution.py:589
  44.6 0.1 collective-permute-start.1
  44.7 1.2 %collective-permute-done.1 = f32[64,256]{1,0:T(8,128)S(1)} collective-permute-done((f32[64,256]{1,0:T(8,128)S(1)}, f32[64,256]{1,0:T(8,128)S(1)}, u32[]{:S(2)}, u32[]{:S(2)}) %collective-permute-start.1) | collective-permute-done | bytes 65568 | tf_op jit(solution)/shard_map/ppermute | solution.py:615
  45.9 1.6 %collective-permute-start.2 = (f32[64,256]{1,0:T(8,128)S(1)}, f32[64,256]{1,0:T(8,128)S(1)}, u32[]{:S(2)}, u32[]{:S(2)}) collective-permute-start(f32[64,256]{1,0:T(8,128)S(1)} %add.9), channel_id=1, source_target_pairs={{0,2},{1,3},{2,0},{3,1},{4,6},{5,7},{6,4},{7,5},{8,10},{9,11},{10,... | collective-permute-start | bytes 196616 | tf_op jit(solution)/shard_map/ppermute | solution.py:615
  47.5 2.8 %collective-permute-done.2 = f32[64,256]{1,0:T(8,128)S(1)} collective-permute-done((f32[64,256]{1,0:T(8,128)S(1)}, f32[64,256]{1,0:T(8,128)S(1)}, u32[]{:S(2)}, u32[]{:S(2)}) %collective-permute-start.2) | collective-permute-done | bytes 65568 | tf_op jit(solution)/shard_map/ppermute | solution.py:615
  50.3 2.2 %collective-permute-start.3 = (f32[64,256]{1,0:T(8,128)S(1)}, f32[64,256]{1,0:T(8,128)S(1)}, u32[]{:S(2)}, u32[]{:S(2)}) collective-permute-start(f32[64,256]{1,0:T(8,128)S(1)} %add.10), channel_id=1, source_target_pairs={{0,4},{1,5},{2,6},{3,7},{4,0},{5,1},{6,2},{7,3},{8,12},{9,13},{10,... | collective-permute-start | bytes 196616 | tf_op jit(solution)/shard_map/ppermute | solution.py:615
  52.5 3.1 %collective-permute-done.3 = f32[64,256]{1,0:T(8,128)S(1)} collective-permute-done((f32[64,256]{1,0:T(8,128)S(1)}, f32[64,256]{1,0:T(8,128)S(1)}, u32[]{:S(2)}, u32[]{:S(2)}) %collective-permute-start.3) | collective-permute-done | bytes 65568 | tf_op jit(solution)/shard_map/ppermute | solution.py:615
  55.5 0.0 copy-done.2
  55.6 0.0 copy-done.15
  55.6 3.0 %shard_map.222 = (f32[9,16,1024]{2,1,0:T(8,128)S(1)}, f32[9,16,1024]{2,1,0:T(8,128)S(1)}, f32[9,16,128]{2,1,0:T(8,128)S(1)}, bf16[16,1024]{1,0:T(8,128)(2,1)S(1)...) custom-call(s32[2,256]{1,0:T(2,128)S(1)} %bitcast.20, ...), custom_call_target="tpu_custom_call" | custom-call | flops 3000000000 | tf_op jit(solution)/shard_map/pallas_call | solution.py:618
  58.6 0.8 %all-to-all-done.1.recv = bf16[32,152,128]{2,1,0:T(8,128)(2,1)S(1)} async-done(((bf16[32,152,128]{2,1,0:T(8,128)(2,1)}), bf16[32,152,128]{2,1,0:T(8,128)(2,1)S(1)}, u32[]{:S(2)}, u32[]{:S(2)}) %all-to-all-start.1) | async-done | bytes 1245216 | tf_op jit(solution)/shard_map/all_to_all | solution.py:609
  59.3 1.6 %shard_map.228 = (f32[16,16,1024]{2,1,0:T(8,128)}, bf16[2,16,1024]{2,1,0:T(8,128)(2,1)}, f32[3,16,1024]{2,1,0:T(8,128)}, bf16[2,16,512]{2,1,0:T(8,128)(2,1)}) custom-call(s32[2,256]{1,0:T(2,128)S(1)} %bitcast.21, f32[9,16,1024]{2,1,0:T(8,128)S(1)} %get-tuple-element.22.factor, ...), custom_call_target="tpu_custom_call", output_to_operand_aliasing={{0}: (12, {})} | custom-call | tf_op jit(solution)/shard_map/pallas_call | solution.py:641
  (9 shorter events, 0.0 us)
Async XLA Ops:
  0.6 11.9 %copy-start.5 = (s32[256,2]{0,1:T(2,128)S(1)}, s32[256,2]{0,1:T(2,128)}, u32[]{:S(2)}) copy-start(s32[256,2]{0,1:T(2,128)} %param.39) | copy-start | bytes 6148
  2.4 10.2 %copy-start.4 = (bf16[192,128]{1,0:T(8,128)(2,1)S(1)}, bf16[192,128]{1,0:T(8,128)(2,1)}, u32[]{:S(2)}) copy-start(bf16[192,128]{1,0:T(8,128)(2,1)} %shard_map.219.own._) | copy-start | bytes 147460
  2.4 19.0 %copy-start.6 = (bf16[2,16,128]{2,1,0:T(8,128)(2,1)S(1)}, bf16[2,16,128]{2,1,0:T(8,128)(2,1)}, u32[]{:S(2)}) copy-start(bf16[2,16,128]{2,1,0:T(8,128)(2,1)} %nk.3) | copy-start | bytes 24580
  2.4 19.0 %copy-start.7 = (bf16[2,16,128]{2,1,0:T(8,128)(2,1)S(1)}, bf16[2,16,128]{2,1,0:T(8,128)(2,1)}, u32[]{:S(2)}) copy-start(bf16[2,16,128]{2,1,0:T(8,128)(2,1)} %nv.3) | copy-start | bytes 24580
  2.4 19.0 %copy-start.8 = (bf16[2,16,512]{2,1,0:T(8,128)(2,1)S(1)}, bf16[2,16,512]{2,1,0:T(8,128)(2,1)}, u32[]{:S(2)}) copy-start(bf16[2,16,512]{2,1,0:T(8,128)(2,1)} %q.1) | copy-start | bytes 98308
  2.4 19.0 %copy-start.11 = (s32[512]{0:T(512)S(1)}, s32[512]{0:T(512)}, u32[]{:S(2)}) copy-start(s32[512]{0:T(512)} %lens.3) | copy-start | bytes 6148
  2.4 18.9 %copy-start.21 = (s32[16,2]{0,1:T(2,128)S(1)}, s32[16,2]{0,1:T(2,128)}, u32[]{:S(2)}) copy-start(s32[16,2]{0,1:T(2,128)} %param.21) | copy-start | bytes 388
  2.4 10.1 %collective-permute-start = (bf16[192,128]{1,0:T(8,128)(2,1)}, bf16[192,128]{1,0:T(8,128)(2,1)S(1)}, u32[]{:S(2)}, u32[]{:S(2)}) collective-permute-start(bf16[192,128]{1,0:T(8,128)(2,1)} %shard_map.219.own._), channel_id=1, source_target_pairs={{0,32},{8,40},{16,48},{24,56},{32,0},{40,8},{48,16},{56,24},{64,96... | collective-permute-start | bytes 147464 | tf_op jit(solution)/shard_map/ppermute | solution.py:536
  12.4 22.7 %collective-permute-start.5 = (bf16[8,144,128]{2,1,0:T(8,128)(2,1)}, bf16[8,144,128]{2,1,0:T(8,128)(2,1)S(1)}, u32[]{:S(2)}, u32[]{:S(2)}) collective-permute-start(bf16[8,144,128]{2,1,0:T(8,128)(2,1)} %shard_map.225.own), channel_id=1, source_target_pairs={{0,32},{8,40},{16,48},{24,56},{32,0},{40,8},{48,16},{56,24},{64,96... | collective-permute-start | bytes 884744 | tf_op jit(solution)/shard_map/ppermute | solution.py:552
  14.0 14.1 %all-to-all-start = ((bf16[32,24,128]{2,1,0:T(8,128)(2,1)}), bf16[32,24,128]{2,1,0:T(8,128)(2,1)S(1)}, u32[]{:S(2)}, u32[]{:S(2)}) async-start(bf16[32,24,128]{2,1,0:T(8,128)(2,1)} %shard_map.220), calls=%async_computation | async-start | bytes 393216 | tf_op jit(solution)/shard_map/all_to_all | solution.py:560
  21.4 1.2 %copy-start.12 = (bf16[32,128,128]{2,1,0:T(8,128)(2,1)S(1)}, bf16[32,128,128]{2,1,0:T(8,128)(2,1)}, u32[]{:S(2)}) copy-start(bf16[32,128,128]{2,1,0:T(8,128)(2,1)} %keys.1) | copy-start | bytes 3145732
  22.6 1.2 %copy-start.13 = (bf16[32,128,128]{2,1,0:T(8,128)(2,1)S(1)}, bf16[32,128,128]{2,1,0:T(8,128)(2,1)}, u32[]{:S(2)}) copy-start(bf16[32,128,128]{2,1,0:T(8,128)(2,1)} %values.1) | copy-start | bytes 3145732
  25.2 9.9 %copy-start.1 = (bf16[8,144,128]{2,1,0:T(8,128)(2,1)S(1)}, bf16[8,144,128]{2,1,0:T(8,128)(2,1)}, u32[]{:S(2)}) copy-start(bf16[8,144,128]{2,1,0:T(8,128)(2,1)} %shard_map.225.own) | copy-start | bytes 884740
  29.2 7.7 %collective-permute-start.4 = (bf16[64,128]{1,0:T(8,128)(2,1)S(1)}, bf16[64,128]{1,0:T(8,128)(2,1)S(1)}, u32[]{:S(2)}, u32[]{:S(2)}) collective-permute-start(bf16[64,128]{1,0:T(8,128)(2,1)S(1)} %shard_map.224._.near), channel_id=1, source_target_pairs={{0,32},{8,40},{16,48},{24,56},{32,0},{40,8},{48,16},{56,24},{64,96... | collective-permute-start | bytes 49160 | tf_op jit(solution)/shard_map/ppermute | solution.py:587
  38.2 5.3 %copy-start = (f32[16,3,1024]{2,0,1:T(8,128)S(1)}, f32[16,3,1024]{2,0,1:T(8,128)}, u32[]{:S(2)}) copy-start(f32[16,3,1024]{2,0,1:T(8,128)} %param.27) | copy-start | bytes 589828
  38.2 5.3 %copy-start.3 = (bf16[2,16,1024]{2,1,0:T(8,128)(2,1)S(1)}, bf16[2,16,1024]{2,1,0:T(8,128)(2,1)}, u32[]{:S(2)}) copy-start(bf16[2,16,1024]{2,1,0:T(8,128)(2,1)} %x.3) | copy-start | bytes 196612
  38.3 5.3 %copy-start.9 = (f32[4,1024]{1,0:T(4,128)S(1)}, f32[4,1024]{1,0:T(4,128)}, u32[]{:S(2)}) copy-start(f32[4,1024]{1,0:T(4,128)} %cw.1) | copy-start | bytes 49156
  38.3 5.3 %copy-start.10 = (f32[1024]{0:T(1024)S(1)}, f32[1024]{0:T(1024)}, u32[]{:S(2)}) copy-start(f32[1024]{0:T(1024)} %param.32) | copy-start | bytes 12292
  38.3 5.3 %copy-start.14 = (bf16[1024,256]{1,0:T(8,128)(2,1)S(1)}, bf16[1024,256]{1,0:T(8,128)(2,1)}, u32[]{:S(2)}) copy-start(bf16[1024,256]{1,0:T(8,128)(2,1)} %down.1) | copy-start | bytes 1572868
  38.3 5.3 %copy-start.16 = (bf16[1024,32]{0,1:T(8,128)(2,1)S(1)}, bf16[1024,32]{0,1:T(8,128)(2,1)}, u32[]{:S(2)}) copy-start(bf16[1024,32]{0,1:T(8,128)(2,1)} %param.34) | copy-start | bytes 196612
  38.3 21.0 %all-to-all-start.1 = ((bf16[32,152,128]{2,1,0:T(8,128)(2,1)}), bf16[32,152,128]{2,1,0:T(8,128)(2,1)S(1)}, u32[]{:S(2)}, u32[]{:S(2)}) async-start(bf16[32,152,128]{2,1,0:T(8,128)(2,1)} %shard_map.227), calls=%async_computation.1 | async-start | bytes 2490368 | tf_op jit(solution)/shard_map/all_to_all | solution.py:609
  43.6 12.0 %copy-start.2 = (f32[16,16,1024]{2,1,0:T(8,128)S(1)}, f32[16,16,1024]{2,1,0:T(8,128)}, u32[]{:S(2)}) copy-start(f32[16,16,1024]{2,1,0:T(8,128)} %ssm.3) | copy-start | bytes 3145732
  43.6 12.0 %copy-start.15 = (bf16[256,1024]{1,0:T(8,128)(2,1)S(1)}, bf16[256,1024]{1,0:T(8,128)(2,1)}, u32[]{:S(2)}) copy-start(bf16[256,1024]{1,0:T(8,128)(2,1)} %up.1) | copy-start | bytes 1572868
  43.6 12.0 %copy-start.17 = (bf16[2,16,1024]{2,1,0:T(8,128)(2,1)S(1)}, bf16[2,16,1024]{2,1,0:T(8,128)(2,1)}, u32[]{:S(2)}) copy-start(bf16[2,16,1024]{2,1,0:T(8,128)(2,1)} %z.1) | copy-start | bytes 196612
  43.6 12.0 %copy-start.18 = (f32[16,1024]{1,0:T(8,128)S(1)}, f32[16,1024]{1,0:T(8,128)}, u32[]{:S(2)}) copy-start(f32[16,1024]{1,0:T(8,128)} %alog.1) | copy-start | bytes 196612
  43.6 12.0 %copy-start.19 = (f32[1024]{0:T(1024)S(1)}, f32[1024]{0:T(1024)}, u32[]{:S(2)}) copy-start(f32[1024]{0:T(1024)} %param.36) | copy-start | bytes 12292
  43.6 12.0 %copy-start.20 = (f32[1024]{0:T(1024)S(1)}, f32[1024]{0:T(1024)}, u32[]{:S(2)}) copy-start(f32[1024]{0:T(1024)} %param.38) | copy-start | bytes 12292
  44.6 1.3 %collective-permute-start.1 = (f32[64,256]{1,0:T(8,128)S(1)}, f32[64,256]{1,0:T(8,128)S(1)}, u32[]{:S(2)}, u32[]{:S(2)}) collective-permute-start(f32[64,256]{1,0:T(8,128)S(1)} %get-tuple-element.20), channel_id=1, source_target_pairs={{0,1},{1,0},{2,3},{3,2},{4,5},{5,4},{6,7},{7,6},{8,9},{9,8},{10,11... | collective-permute-start | bytes 196616 | tf_op jit(solution)/shard_map/ppermute | solution.py:615
  45.9 4.4 %collective-permute-start.2 = (f32[64,256]{1,0:T(8,128)S(1)}, f32[64,256]{1,0:T(8,128)S(1)}, u32[]{:S(2)}, u32[]{:S(2)}) collective-permute-start(f32[64,256]{1,0:T(8,128)S(1)} %add.9), channel_id=1, source_target_pairs={{0,2},{1,3},{2,0},{3,1},{4,6},{5,7},{6,4},{7,5},{8,10},{9,11},{10,... | collective-permute-start | bytes 196616 | tf_op jit(solution)/shard_map/ppermute | solution.py:615
  50.3 5.3 %collective-permute-start.3 = (f32[64,256]{1,0:T(8,128)S(1)}, f32[64,256]{1,0:T(8,128)S(1)}, u32[]{:S(2)}, u32[]{:S(2)}) collective-permute-start(f32[64,256]{1,0:T(8,128)S(1)} %add.10), channel_id=1, source_target_pairs={{0,4},{1,5},{2,6},{3,7},{4,0},{5,1},{6,2},{7,3},{8,12},{9,13},{10,... | collective-permute-start | bytes 196616 | tf_op jit(solution)/shard_map/ppermute | solution.py:615

commit v6 on v5

--- a/solution.py
+++ b/solution.py
@@ -169,7 +169,8 @@
         score[i * 8 : i * 8 + 8, :] = lax.dot_general(
             wide[i * 8 : i * 8 + 8, :].astype(BF), keys(), NT, preferred_element_type=F32
         )
-        limit[i * 8 : i * 8 + 8, :] = jnp.full((8, HD), length, jnp.int32)
+        if length is not None:
+            limit[i * 8 : i * 8 + 8, :] = jnp.full((8, HD), length, jnp.int32)
     position = lax.broadcasted_iota(jnp.int32, (count * 8, HD), 1)
     ends = limit[...]
     score0 = jnp.where(position < ends, score[:, :HD] * SCALE, -1e30)
@@ -199,7 +200,7 @@
 
 
 def attend_home_kernel(
-    moves, lens, pages, keys, values, q, nk, nv, result, kept, qs, fk, fv, gk, gv, score, limit
+    moves, lens, pages, keys, values, q, nk, nv, result, kept, rows_out, ends_out, qs, fk, fv, gk, gv, score, limit
 ):
     me = lax.axis_index("replica")
     for step in range(2):
@@ -228,36 +229,34 @@
         slot, _ = out_move(me, moves, j)
         kept[j, 0] = both_pages(keys, slot)
         kept[j, 1] = both_pages(values, slot)
-
-
-def attend_away_kernel(
-    moves, lens, recv, kept, nk, nv, send, qs, fk, fv, score, limit, result
-):
-    me = lax.axis_index("replica")
-    spread(fk, nk[0].astype(F32))
-    spread(fv, nv[0].astype(F32))
+        start = pl.multiple_of(slot * 8, 8)
+        lines = slice(j * 8, j * 8 + 8)
+        rows_out[0, lines, :] = fk[pl.ds(start, 8), :]
+        rows_out[1, lines, :] = fv[pl.ds(start, 8), :]
+        ends_out[lines, :] = jnp.full((8, HD), lens[me * SLOTS + slot], jnp.int32)
+
+
+def attend_away_kernel(moves, recv, kept, first, ends, send, qs, score, result):
+    me = lax.axis_index("replica")
     slots = []
-    first_k, first_v, next_k, next_v = [], [], [], []
-    for j in range(MOVES):
-        slot, target = out_move(me, moves, j)
+    next_k, next_v = [], []
+    for j in range(MOVES):
+        _, target = out_move(me, moves, j)
         flip = crosses(me, target)
         got = recv[place(target) * 2 + flip, PAIR_ROWS:, :].astype(F32)
         qs[j * 8 : j * 8 + 8, :] = got
-        start = pl.multiple_of(slot * 8, 8)
-        first_k.append(fk[pl.ds(start, 8), :])
-        first_v.append(fv[pl.ds(start, 8), :])
         next_k.append(jnp.broadcast_to(got[0:1, :], (8, HD)))
         next_v.append(jnp.broadcast_to(got[1:2, :], (8, HD)))
         slots.append(
             (
-                lens[me * SLOTS + slot],
+                None,
                 functools.partial(lambda i: kept[i, 0], j),
                 functools.partial(lambda i: kept[i, 1], j),
             )
         )
     join = functools.partial(jnp.concatenate, axis=0)
     attend_slots(
-        slots, qs, join(first_k), join(first_v), join(next_k), join(next_v), False, score, limit, result
+        slots, qs, first[0], first[1], join(next_k), join(next_v), False, score, ends, result
     )
     send[...] = result[...].astype(BF)
 
@@ -348,6 +347,7 @@
     read_out,
     final,
     step,
+    rates,
     held,
     yrows,
     position,
@@ -361,31 +361,35 @@
         position[slot] = j
     dt = jnp.dot(sums[0:48, :].astype(BF), up[...], preferred_element_type=F32) + db[...]
     step[...] = jnp.maximum(dt, 0.0) + jnp.log1p(jnp.exp(-jnp.abs(dt)))
-    rate = -jnp.exp(alog[...])
-
-    def terms(row):
-        dts = step[row : row + 1, :]
-        added = sums[48:64, row : row + 1] * (dts * mixed[row : row + 1, :])
-        return jnp.exp(dts * rate), added
-
+    rates[...] = -jnp.exp(alog[...])
     copies = []
     for s in range(SLOTS):
-        decay, added = terms(s)
-        state = decay * ssm[s] + added
-        read = sums[48:64, 128 + s : 129 + s] * state
-        yrows[s : s + 1, :] = jnp.sum(read, axis=0, keepdims=True)
-        decay, added = terms(16 + s)
-        later, more = terms(32 + s)
         at = position[s]
-        factor[at] = decay * later
-        offset[at] = later * added + more
-        column = sums[48:64, 160 + s : 161 + s]
-        maps[at] = jnp.broadcast_to(column, (DS, HD))
-        state = later * state + more
-        held[s] = state
+        columns = [sums[48:64, row : row + 1] for row in (s, 16 + s, 32 + s, 128 + s, 160 + s)]
+        columns = [jnp.broadcast_to(column, (DS, HD)) for column in columns]
+        maps[at] = columns[4]
+        for c in range(PIECES):
+            lanes = slice(c * HD, (c + 1) * HD)
+            rate = rates[:, lanes]
+
+            def terms(row, column):
+                dts = step[row : row + 1, lanes]
+                return jnp.exp(dts * rate), column * (dts * mixed[row : row + 1, lanes])
+
+            decay, added = terms(s, columns[0])
+            state = decay * ssm[s, :, lanes] + added
+            yrows[s : s + 1, lanes] = jnp.sum(columns[3] * state, axis=0, keepdims=True)
+            decay, added = terms(16 + s, columns[1])
+            later, more = terms(32 + s, columns[2])
+            factor[at, :, lanes] = decay * later
+            offset[at, :, lanes] = later * added + more
+            state = later * state + more
+            held[s, :, lanes] = state
+            read_out[s * 8 + c : s * 8 + c + 1, :] = jnp.sum(
+                columns[4] * state, axis=0, keepdims=True
+            )
         copies.append(pltpu.make_async_copy(held.at[s], final.at[s], left.at[s]))
         copies[s].start()
-        read_out[s * 8 : s * 8 + 8, :] = lay(jnp.sum(column * state, axis=0, keepdims=True))
     first[...] = ((yrows[...] + skip[...] * mixed[0:16]) * silu(z[0].astype(F32))).astype(BF)
     base[...] = skip[...] * mixed[32:48]
     gate[...] = silu(z[1].astype(F32))
@@ -561,29 +565,31 @@
         small, "replica", split_axis=0, concat_axis=0, tiled=True, axis_index_groups=planes
     )
 
-    home, kept = call(
+    away = MOVES * 8
+    home, kept, kept_rows, kept_ends = call(
         attend_home_kernel,
         "sssvvddd",
-        [("v", shape((rows, HD), F32)), ("v", shape((MOVES, 2, 2 * HD, HD), BF))],
+        [
+            ("v", shape((rows, HD), F32)),
+            ("v", shape((MOVES, 2, 2 * HD, HD), BF)),
+            ("v", shape((2, away, HD), F32)),
+            ("v", shape((away, HD), jnp.int32)),
+        ],
         [pltpu.VMEM((rows, HD), F32)] * 5
         + [pltpu.VMEM((rows, 2 * HD), F32), pltpu.VMEM((rows, HD), jnp.int32)],
         flops=4_000_000_000,
     )(moves, lengths, pages, key_pool, value_pool, queries, new_keys, new_values)
 
-    away = MOVES * 8
     near = call(
         attend_away_kernel,
-        "ssvvdd",
+        "svvvv",
         [("v", shape((away, HD), BF))],
         [
             pltpu.VMEM((away, HD), F32),
-            pltpu.VMEM((rows, HD), F32),
-            pltpu.VMEM((rows, HD), F32),
             pltpu.VMEM((away, 2 * HD), F32),
-            pltpu.VMEM((away, HD), jnp.int32),
             pltpu.VMEM((away, HD), F32),
         ],
-    )(moves, lengths, small, kept, new_keys, new_values)
+    )(moves, small, kept, kept_rows, kept_ends)
     far = lax.ppermute(near, "replica", across)
 
     sums, mixed = call(
@@ -630,6 +636,7 @@
         ],
         [
             pltpu.VMEM((48, channels), F32),
+            pltpu.VMEM((DS, channels), F32),
             pltpu.VMEM((SLOTS, DS, channels), F32),
             pltpu.VMEM((SLOTS, channels), F32),
             pltpu.SMEM((SLOTS,), jnp.int32),

time: 62.1 us -> 62 us (level)
  no operation moved by 1% of the time
where the time goes in v6:
time: 62 us; the launch traced here: 60.9 us
  starting transfers between devices  29.8 us (48%)
  Pallas kernels  16.3 us (26%)
  waiting for transfers between devices  11.2 us (18%)
  local copies, waits for them, and re-layouts  2.57 us (4%)
  between operations  1.01 us (2%)
    all_to_all x1, starting transfers between devices, shards(): lax.all_to_all(small, 'replica', split_axis=0, concat_axis=0, tiled=True,...  7.39 us
    ppermute x1, starting transfers between devices, shards(): far_small = lax.ppermute(near_small, 'replica', across)  7.27 us
    ppermute x3, waiting for transfers between devices, shards(): lax.ppermute(sums, 'tensor', [(i, i ^ bit) for i in range(tensors)])  7.07 us
    ppermute x1, starting transfers between devices, shards(): far = lax.ppermute(near, 'replica', across)  5.93 us
    all_to_all x1, starting transfers between devices, shards(): lax.all_to_all(large, 'replica', split_axis=0, concat_axis=0, tiled=True,...  5.22 us
    ppermute x3, starting transfers between devices, shards(): lax.ppermute(sums, 'tensor', [(i, i ^ bit) for i in range(tensors)])  3.87 us
    all_to_all x1, waiting for transfers between devices, shards(): lax.all_to_all(small, 'replica', split_axis=0, concat_axis=0, tiled=True,...  2.81 us
    pallas_call x1, Pallas kernels, shards(): call(first_scan_kernel, 'svvvvvvvv', [('v', shape((MOVES + 1, DS, channel...  2.77 us
  transfers between devices with their start and end apart: 8, of which 6 were waited for; matrix products, arithmetic and copies ran while one was open for 0% of the time, Pallas kernels for 19%

profile of v6, /device:TPU:8, one launch (start us, length us, event | category | flops | bytes accessed | tf_op | source)
XLA Modules:
  0.0 60.9 jit_solution(4881767970563729361)
XLA Ops:
  0.6 0.0 copy-start.5
  0.6 1.7 %shard_map.219.own._ = bf16[192,128]{1,0:T(8,128)(2,1)} custom-call(s32[2,256]{1,0:T(2,128)} %bitcast.12, f32[3,16,1024]{2,1,0:T(8,128)} %bitcast.8, bf16[2,16,1024]{2,1,0:T(8,128)(2,1)} %x.3, bf16[2,16,512]{2,1,0:T(8,128)(2,1)} %q.1, bf16[2,16,128]{2,1,0:T(8,128)(2,1)} %nk.1, bf16[2,16,128]{2,1,0:T(8,128)(2,1)} %nv.1, f32[4,1024]{1,0:T(4,128)} %cw.1, ...), custom_call_target="tpu_custom_call" | custom-call | tf_op jit(solution)/shard_map/pallas_call | solution.py:522
  2.4 0.0 copy-start.4
  2.4 0.0 copy-start.6
  2.4 0.0 copy-start.8
  2.4 0.0 copy-start.9
  2.4 0.0 copy-start.20
  2.4 0.0 copy-start.21
  2.4 7.3 %collective-permute-start = (bf16[192,128]{1,0:T(8,128)(2,1)}, bf16[192,128]{1,0:T(8,128)(2,1)S(1)}, u32[]{:S(2)}, u32[]{:S(2)}) collective-permute-start(bf16[192,128]{1,0:T(8,128)(2,1)} %shard_map.219.own._), channel_id=1, source_target_pairs={{0,32},{8,40},{16,48},{24,56},{32,0},{40,8},{48,16},{56,24},{64,96... | collective-permute-start | bytes 147464 | tf_op jit(solution)/shard_map/ppermute | solution.py:540
  9.7 2.7 %shard_map.225.own = bf16[8,144,128]{2,1,0:T(8,128)(2,1)} custom-call(s32[2,256]{1,0:T(2,128)} %bitcast.13, f32[16,16,1024]{2,1,0:T(8,128)} %ssm.3, f32[3,16,1024]{2,1,0:T(8,128)} %bitcast.9, bf16[2,16,1024]{2,1,0:T(8,128)(2,1)} %x.3, bf16[192,128]{1,0:T(8,128)(2,1)} %shard_map.219.own._), custom_call_target="tpu_custom_call" | custom-call | tf_op jit(solution)/shard_map/pallas_call | solution.py:542
  12.4 0.1 collective-permute-start.5
  12.5 0.0 collective-permute-done.other
  12.5 0.0 copy-done.5
  12.5 0.0 copy-done.4
  12.5 1.4 %shard_map.220 = bf16[32,24,128]{2,1,0:T(8,128)(2,1)} custom-call(s32[2,256]{1,0:T(2,128)S(1)} %bitcast.14, bf16[192,128]{1,0:T(8,128)(2,1)S(1)} %copy-done.4, bf16[192,128]{1,0:T(8,128)(2,1)S(1)} %collective-permute-done.other), custom_call_target="tpu_custom_call" | custom-call | tf_op jit(solution)/shard_map/pallas_call | solution.py:558
  14.0 7.4 %all-to-all-start = ((bf16[32,24,128]{2,1,0:T(8,128)(2,1)}), bf16[32,24,128]{2,1,0:T(8,128)(2,1)S(1)}, u32[]{:S(2)}, u32[]{:S(2)}) async-start(bf16[32,24,128]{2,1,0:T(8,128)(2,1)} %shard_map.220), calls=%async_computation | async-start | bytes 393216 | tf_op jit(solution)/shard_map/all_to_all | solution.py:564
  21.3 0.0 copy-done.6
  21.4 0.0 copy-done.8
  21.4 0.0 copy-done.9
  21.4 0.0 copy-done.20
  21.4 0.0 copy-done.21
  21.4 0.0 copy-start.11
  21.4 1.2 %copy-done.11 = bf16[32,128,128]{2,1,0:T(8,128)(2,1)S(1)} copy-done((bf16[32,128,128]{2,1,0:T(8,128)(2,1)S(1)}, bf16[32,128,128]{2,1,0:T(8,128)(2,1)}, u32[]{:S(2)}) %copy-start.11) | copy-done | bytes 1048600
  22.6 1.2 %copy-done.12 = bf16[32,128,128]{2,1,0:T(8,128)(2,1)S(1)} copy-done((bf16[32,128,128]{2,1,0:T(8,128)(2,1)S(1)}, bf16[32,128,128]{2,1,0:T(8,128)(2,1)}, u32[]{:S(2)}) %copy-start.12) | copy-done | bytes 1048600
  23.8 1.4 %shard_map.223 = (f32[128,128]{1,0:T(8,128)S(1)}, bf16[8,2,256,128]{3,2,1,0:T(8,128)(2,1)S(1)}, f32[2,64,128]{2,1,0:T(8,128)S(1)}, s32[64,128]{1,0:T(8,128)S(1)}) custom-call(s32[2,256]{1,0:T(2,128)S(1)} %bitcast.15, s32[512]{0:T(512)S(1)} %copy-done.20, s32[2,16]{1,0:T(2,128)S(1)} %bitcast.27, bf16[32,128,128]{2,1,0:T(8,128)(2,1)S(1)} %copy-done.11, ...), custom_call_target="tpu_custom_call" | custom-call | flops 4000000000 | tf_op jit(solution)/shard_map/pallas_call | solution.py:569
  25.2 2.8 %all-to-all-done.recv = bf16[32,24,128]{2,1,0:T(8,128)(2,1)S(1)} async-done(((bf16[32,24,128]{2,1,0:T(8,128)(2,1)}), bf16[32,24,128]{2,1,0:T(8,128)(2,1)S(1)}, u32[]{:S(2)}, u32[]{:S(2)}) %all-to-all-start) | async-done | bytes 196640 | tf_op jit(solution)/shard_map/all_to_all | solution.py:564
  28.1 1.1 %shard_map.224._.near = bf16[64,128]{1,0:T(8,128)(2,1)S(1)} custom-call(s32[2,256]{1,0:T(2,128)S(1)} %bitcast.16, bf16[32,24,128]{2,1,0:T(8,128)(2,1)S(1)} %all-to-all-done.recv, bf16[8,2,256,128]{3,2,1,0:T(8,128)(2,1)S(1)} %get-tuple-element.31.kept, f32[2,64,128]{2,1,0:T(8,128)S(1)} %get-tuple-element.32.first, s32[64,128]{1,0:T(8,128)S(1)} %get-tuple-element.33.ends), custom_call_target="tpu_custom_call" | custom-call | tf_op jit(solution)/shard_map/pallas_call | solution.py:583
  29.2 5.9 %collective-permute-start.4 = (bf16[64,128]{1,0:T(8,128)(2,1)S(1)}, bf16[64,128]{1,0:T(8,128)(2,1)S(1)}, u32[]{:S(2)}, u32[]{:S(2)}) collective-permute-start(bf16[64,128]{1,0:T(8,128)(2,1)S(1)} %shard_map.224._.near), channel_id=1, source_target_pairs={{0,32},{8,40},{16,48},{24,56},{32,0},{40,8},{48,16},{56,24},{64,96... | collective-permute-start | bytes 49160 | tf_op jit(solution)/shard_map/ppermute | solution.py:593
  35.1 0.0 collective-permute-done.5.other
  35.1 0.0 copy-done.1
  35.1 1.4 %shard_map.226._ = bf16[32,152,128]{2,1,0:T(8,128)(2,1)} custom-call(s32[2,256]{1,0:T(2,128)S(1)} %bitcast.17, bf16[8,144,128]{2,1,0:T(8,128)(2,1)S(1)} %copy-done.1, bf16[8,144,128]{2,1,0:T(8,128)(2,1)S(1)} %collective-permute-done.5.other, bf16[64,128]{1,0:T(8,128)(2,1)S(1)} %shard_map.224._.near), custom_call_target="tpu_custom_call" | custom-call | tf_op jit(solution)/shard_map/pallas_call | solution.py:602
  36.5 0.4 collective-permute-done.4.far
  36.9 1.3 %shard_map.227 = bf16[32,152,128]{2,1,0:T(8,128)(2,1)} custom-call(s32[2,256]{1,0:T(2,128)S(1)} %bitcast.18, bf16[64,128]{1,0:T(8,128)(2,1)S(1)} %shard_map.224._.near, bf16[64,128]{1,0:T(8,128)(2,1)S(1)} %collective-permute-done.4.far, bf16[32,152,128]{2,1,0:T(8,128)(2,1)} %shard_map.226._), custom_call_target="tpu_custom_call", output_to_operand_aliasing={{}: (3, {})} | custom-call | tf_op jit(solution)/shard_map/pallas_call | solution.py:608
  38.2 0.0 copy-start
  38.2 0.0 copy-start.3
  38.2 0.0 copy-start.7
  38.2 0.0 copy-start.10
  38.3 0.0 copy-start.13
  38.3 0.0 copy-start.15
  38.3 5.2 %all-to-all-start.1 = ((bf16[32,152,128]{2,1,0:T(8,128)(2,1)}), bf16[32,152,128]{2,1,0:T(8,128)(2,1)S(1)}, u32[]{:S(2)}, u32[]{:S(2)}) async-start(bf16[32,152,128]{2,1,0:T(8,128)(2,1)} %shard_map.227), calls=%async_computation.1 | async-start | bytes 2490368 | tf_op jit(solution)/shard_map/all_to_all | solution.py:615
  43.5 0.0 copy-done
  43.5 0.0 copy-done.3
  43.5 0.0 copy-done.7
  43.5 0.0 copy-done.10
  43.5 0.0 copy-done.13
  43.5 0.0 copy-done.15
  43.5 0.0 copy-start.2
  43.6 0.0 copy-start.14
  43.6 0.0 copy-start.16
  43.6 0.0 copy-start.17
  43.6 0.0 copy-start.18
  43.6 0.0 copy-start.19
  43.6 0.9 %shard_map.221 = (f32[64,256]{1,0:T(8,128)S(1)}, f32[48,1024]{1,0:T(8,128)S(1)}) custom-call(s32[2,256]{1,0:T(2,128)S(1)} %bitcast.19, bf16[32,24,128]{2,1,0:T(8,128)(2,1)S(1)} %all-to-all-done.recv, f32[3,16,1024]{2,1,0:T(8,128)S(1)} %bitcast.10, bf16[2,16,1024]{2,1,0:T(8,128)(2,1)S(1)} %copy-done.3, f32[4,1024]{1,0:T(4,128)S(1)} %copy-done.7, ...), custom_call_target="tpu_custom_call" | custom-call | flops 2000000000 | tf_op jit(solution)/shard_map/pallas_call | solution.py:595
  44.5 0.1 collective-permute-start.1
  44.6 1.2 %collective-permute-done.1 = f32[64,256]{1,0:T(8,128)S(1)} collective-permute-done((f32[64,256]{1,0:T(8,128)S(1)}, f32[64,256]{1,0:T(8,128)S(1)}, u32[]{:S(2)}, u32[]{:S(2)}) %collective-permute-start.1) | collective-permute-done | bytes 65568 | tf_op jit(solution)/shard_map/ppermute | solution.py:621
  45.9 1.6 %collective-permute-start.2 = (f32[64,256]{1,0:T(8,128)S(1)}, f32[64,256]{1,0:T(8,128)S(1)}, u32[]{:S(2)}, u32[]{:S(2)}) collective-permute-start(f32[64,256]{1,0:T(8,128)S(1)} %add.9), channel_id=1, source_target_pairs={{0,2},{1,3},{2,0},{3,1},{4,6},{5,7},{6,4},{7,5},{8,10},{9,11},{10,... | collective-permute-start | bytes 196616 | tf_op jit(solution)/shard_map/ppermute | solution.py:621
  47.5 2.8 %collective-permute-done.2 = f32[64,256]{1,0:T(8,128)S(1)} collective-permute-done((f32[64,256]{1,0:T(8,128)S(1)}, f32[64,256]{1,0:T(8,128)S(1)}, u32[]{:S(2)}, u32[]{:S(2)}) %collective-permute-start.2) | collective-permute-done | bytes 65568 | tf_op jit(solution)/shard_map/ppermute | solution.py:621
  50.3 2.2 %collective-permute-start.3 = (f32[64,256]{1,0:T(8,128)S(1)}, f32[64,256]{1,0:T(8,128)S(1)}, u32[]{:S(2)}, u32[]{:S(2)}) collective-permute-start(f32[64,256]{1,0:T(8,128)S(1)} %add.10), channel_id=1, source_target_pairs={{0,4},{1,5},{2,6},{3,7},{4,0},{5,1},{6,2},{7,3},{8,12},{9,13},{10,... | collective-permute-start | bytes 196616 | tf_op jit(solution)/shard_map/ppermute | solution.py:621
  52.4 3.1 %collective-permute-done.3 = f32[64,256]{1,0:T(8,128)S(1)} collective-permute-done((f32[64,256]{1,0:T(8,128)S(1)}, f32[64,256]{1,0:T(8,128)S(1)}, u32[]{:S(2)}, u32[]{:S(2)}) %collective-permute-start.3) | collective-permute-done | bytes 65568 | tf_op jit(solution)/shard_map/ppermute | solution.py:621
  55.5 0.0 copy-done.2
  55.5 0.0 copy-done.14
  55.6 2.8 %shard_map.222 = (f32[9,16,1024]{2,1,0:T(8,128)S(1)}, f32[9,16,1024]{2,1,0:T(8,128)S(1)}, f32[9,16,128]{2,1,0:T(8,128)S(1)}, bf16[16,1024]{1,0:T(8,128)(2,1)S(1)...) custom-call(s32[2,256]{1,0:T(2,128)S(1)} %bitcast.20, ...), custom_call_target="tpu_custom_call" | custom-call | flops 3000000000 | tf_op jit(solution)/shard_map/pallas_call | solution.py:624
  58.4 0.9 %all-to-all-done.1.recv = bf16[32,152,128]{2,1,0:T(8,128)(2,1)S(1)} async-done(((bf16[32,152,128]{2,1,0:T(8,128)(2,1)}), bf16[32,152,128]{2,1,0:T(8,128)(2,1)S(1)}, u32[]{:S(2)}, u32[]{:S(2)}) %all-to-all-start.1) | async-done | bytes 1245216 | tf_op jit(solution)/shard_map/all_to_all | solution.py:615
  59.3 1.6 %shard_map.228 = (f32[16,16,1024]{2,1,0:T(8,128)}, bf16[2,16,1024]{2,1,0:T(8,128)(2,1)}, f32[3,16,1024]{2,1,0:T(8,128)}, bf16[2,16,512]{2,1,0:T(8,128)(2,1)}) custom-call(s32[2,256]{1,0:T(2,128)S(1)} %bitcast.21, f32[9,16,1024]{2,1,0:T(8,128)S(1)} %get-tuple-element.24.factor, ...), custom_call_target="tpu_custom_call", output_to_operand_aliasing={{0}: (12, {})} | custom-call | tf_op jit(solution)/shard_map/pallas_call | solution.py:648
  (9 shorter events, 0.0 us)
Async XLA Ops:
  0.6 11.9 %copy-start.5 = (s32[256,2]{0,1:T(2,128)S(1)}, s32[256,2]{0,1:T(2,128)}, u32[]{:S(2)}) copy-start(s32[256,2]{0,1:T(2,128)} %param.39) | copy-start | bytes 6148
  2.4 10.2 %copy-start.4 = (bf16[192,128]{1,0:T(8,128)(2,1)S(1)}, bf16[192,128]{1,0:T(8,128)(2,1)}, u32[]{:S(2)}) copy-start(bf16[192,128]{1,0:T(8,128)(2,1)} %shard_map.219.own._) | copy-start | bytes 147460
  2.4 19.0 %copy-start.6 = (bf16[2,16,512]{2,1,0:T(8,128)(2,1)S(1)}, bf16[2,16,512]{2,1,0:T(8,128)(2,1)}, u32[]{:S(2)}) copy-start(bf16[2,16,512]{2,1,0:T(8,128)(2,1)} %q.1) | copy-start | bytes 98308
  2.4 19.0 %copy-start.8 = (bf16[2,16,128]{2,1,0:T(8,128)(2,1)S(1)}, bf16[2,16,128]{2,1,0:T(8,128)(2,1)}, u32[]{:S(2)}) copy-start(bf16[2,16,128]{2,1,0:T(8,128)(2,1)} %nk.1) | copy-start | bytes 24580
  2.4 19.0 %copy-start.9 = (bf16[2,16,128]{2,1,0:T(8,128)(2,1)S(1)}, bf16[2,16,128]{2,1,0:T(8,128)(2,1)}, u32[]{:S(2)}) copy-start(bf16[2,16,128]{2,1,0:T(8,128)(2,1)} %nv.1) | copy-start | bytes 24580
  2.4 18.9 %copy-start.20 = (s32[512]{0:T(512)S(1)}, s32[512]{0:T(512)}, u32[]{:S(2)}) copy-start(s32[512]{0:T(512)} %lens.1) | copy-start | bytes 6148
  2.4 18.9 %copy-start.21 = (s32[16,2]{0,1:T(2,128)S(1)}, s32[16,2]{0,1:T(2,128)}, u32[]{:S(2)}) copy-start(s32[16,2]{0,1:T(2,128)} %param.21) | copy-start | bytes 388
  2.4 10.1 %collective-permute-start = (bf16[192,128]{1,0:T(8,128)(2,1)}, bf16[192,128]{1,0:T(8,128)(2,1)S(1)}, u32[]{:S(2)}, u32[]{:S(2)}) collective-permute-start(bf16[192,128]{1,0:T(8,128)(2,1)} %shard_map.219.own._), channel_id=1, source_target_pairs={{0,32},{8,40},{16,48},{24,56},{32,0},{40,8},{48,16},{56,24},{64,96... | collective-permute-start | bytes 147464 | tf_op jit(solution)/shard_map/ppermute | solution.py:540
  12.4 22.7 %collective-permute-start.5 = (bf16[8,144,128]{2,1,0:T(8,128)(2,1)}, bf16[8,144,128]{2,1,0:T(8,128)(2,1)S(1)}, u32[]{:S(2)}, u32[]{:S(2)}) collective-permute-start(bf16[8,144,128]{2,1,0:T(8,128)(2,1)} %shard_map.225.own), channel_id=1, source_target_pairs={{0,32},{8,40},{16,48},{24,56},{32,0},{40,8},{48,16},{56,24},{64,96... | collective-permute-start | bytes 884744 | tf_op jit(solution)/shard_map/ppermute | solution.py:556
  14.0 14.1 %all-to-all-start = ((bf16[32,24,128]{2,1,0:T(8,128)(2,1)}), bf16[32,24,128]{2,1,0:T(8,128)(2,1)S(1)}, u32[]{:S(2)}, u32[]{:S(2)}) async-start(bf16[32,24,128]{2,1,0:T(8,128)(2,1)} %shard_map.220), calls=%async_computation | async-start | bytes 393216 | tf_op jit(solution)/shard_map/all_to_all | solution.py:564
  21.4 1.2 %copy-start.11 = (bf16[32,128,128]{2,1,0:T(8,128)(2,1)S(1)}, bf16[32,128,128]{2,1,0:T(8,128)(2,1)}, u32[]{:S(2)}) copy-start(bf16[32,128,128]{2,1,0:T(8,128)(2,1)} %keys.1) | copy-start | bytes 3145732
  22.6 1.2 %copy-start.12 = (bf16[32,128,128]{2,1,0:T(8,128)(2,1)S(1)}, bf16[32,128,128]{2,1,0:T(8,128)(2,1)}, u32[]{:S(2)}) copy-start(bf16[32,128,128]{2,1,0:T(8,128)(2,1)} %values.1) | copy-start | bytes 3145732
  25.2 9.8 %copy-start.1 = (bf16[8,144,128]{2,1,0:T(8,128)(2,1)S(1)}, bf16[8,144,128]{2,1,0:T(8,128)(2,1)}, u32[]{:S(2)}) copy-start(bf16[8,144,128]{2,1,0:T(8,128)(2,1)} %shard_map.225.own) | copy-start | bytes 884740
  29.2 7.7 %collective-permute-start.4 = (bf16[64,128]{1,0:T(8,128)(2,1)S(1)}, bf16[64,128]{1,0:T(8,128)(2,1)S(1)}, u32[]{:S(2)}, u32[]{:S(2)}) collective-permute-start(bf16[64,128]{1,0:T(8,128)(2,1)S(1)} %shard_map.224._.near), channel_id=1, source_target_pairs={{0,32},{8,40},{16,48},{24,56},{32,0},{40,8},{48,16},{56,24},{64,96... | collective-permute-start | bytes 49160 | tf_op jit(solution)/shard_map/ppermute | solution.py:593
  38.2 5.3 %copy-start = (f32[16,3,1024]{2,0,1:T(8,128)S(1)}, f32[16,3,1024]{2,0,1:T(8,128)}, u32[]{:S(2)}) copy-start(f32[16,3,1024]{2,0,1:T(8,128)} %param.27) | copy-start | bytes 589828
  38.2 5.3 %copy-start.3 = (bf16[2,16,1024]{2,1,0:T(8,128)(2,1)S(1)}, bf16[2,16,1024]{2,1,0:T(8,128)(2,1)}, u32[]{:S(2)}) copy-start(bf16[2,16,1024]{2,1,0:T(8,128)(2,1)} %x.3) | copy-start | bytes 196612
  38.2 5.3 %copy-start.7 = (f32[4,1024]{1,0:T(4,128)S(1)}, f32[4,1024]{1,0:T(4,128)}, u32[]{:S(2)}) copy-start(f32[4,1024]{1,0:T(4,128)} %cw.1) | copy-start | bytes 49156
  38.2 5.3 %copy-start.10 = (f32[1024]{0:T(1024)S(1)}, f32[1024]{0:T(1024)}, u32[]{:S(2)}) copy-start(f32[1024]{0:T(1024)} %param.32) | copy-start | bytes 12292
  38.3 5.3 %copy-start.13 = (bf16[1024,256]{1,0:T(8,128)(2,1)S(1)}, bf16[1024,256]{1,0:T(8,128)(2,1)}, u32[]{:S(2)}) copy-start(bf16[1024,256]{1,0:T(8,128)(2,1)} %down.1) | copy-start | bytes 1572868
  38.3 5.3 %copy-start.15 = (bf16[1024,32]{0,1:T(8,128)(2,1)S(1)}, bf16[1024,32]{0,1:T(8,128)(2,1)}, u32[]{:S(2)}) copy-start(bf16[1024,32]{0,1:T(8,128)(2,1)} %param.34) | copy-start | bytes 196612
  38.3 21.0 %all-to-all-start.1 = ((bf16[32,152,128]{2,1,0:T(8,128)(2,1)}), bf16[32,152,128]{2,1,0:T(8,128)(2,1)S(1)}, u32[]{:S(2)}, u32[]{:S(2)}) async-start(bf16[32,152,128]{2,1,0:T(8,128)(2,1)} %shard_map.227), calls=%async_computation.1 | async-start | bytes 2490368 | tf_op jit(solution)/shard_map/all_to_all | solution.py:615
  43.5 12.0 %copy-start.2 = (f32[16,16,1024]{2,1,0:T(8,128)S(1)}, f32[16,16,1024]{2,1,0:T(8,128)}, u32[]{:S(2)}) copy-start(f32[16,16,1024]{2,1,0:T(8,128)} %ssm.3) | copy-start | bytes 3145732
  43.6 12.0 %copy-start.14 = (bf16[256,1024]{1,0:T(8,128)(2,1)S(1)}, bf16[256,1024]{1,0:T(8,128)(2,1)}, u32[]{:S(2)}) copy-start(bf16[256,1024]{1,0:T(8,128)(2,1)} %up.1) | copy-start | bytes 1572868
  43.6 12.0 %copy-start.16 = (bf16[2,16,1024]{2,1,0:T(8,128)(2,1)S(1)}, bf16[2,16,1024]{2,1,0:T(8,128)(2,1)}, u32[]{:S(2)}) copy-start(bf16[2,16,1024]{2,1,0:T(8,128)(2,1)} %z.1) | copy-start | bytes 196612
  43.6 12.0 %copy-start.17 = (f32[16,1024]{1,0:T(8,128)S(1)}, f32[16,1024]{1,0:T(8,128)}, u32[]{:S(2)}) copy-start(f32[16,1024]{1,0:T(8,128)} %alog.1) | copy-start | bytes 196612
  43.6 12.0 %copy-start.18 = (f32[1024]{0:T(1024)S(1)}, f32[1024]{0:T(1024)}, u32[]{:S(2)}) copy-start(f32[1024]{0:T(1024)} %param.36) | copy-start | bytes 12292
  43.6 12.0 %copy-start.19 = (f32[1024]{0:T(1024)S(1)}, f32[1024]{0:T(1024)}, u32[]{:S(2)}) copy-start(f32[1024]{0:T(1024)} %param.38) | copy-start | bytes 12292
  44.5 1.3 %collective-permute-start.1 = (f32[64,256]{1,0:T(8,128)S(1)}, f32[64,256]{1,0:T(8,128)S(1)}, u32[]{:S(2)}, u32[]{:S(2)}) collective-permute-start(f32[64,256]{1,0:T(8,128)S(1)} %get-tuple-element.22), channel_id=1, source_target_pairs={{0,1},{1,0},{2,3},{3,2},{4,5},{5,4},{6,7},{7,6},{8,9},{9,8},{10,11... | collective-permute-start | bytes 196616 | tf_op jit(solution)/shard_map/ppermute | solution.py:621
  45.9 4.4 %collective-permute-start.2 = (f32[64,256]{1,0:T(8,128)S(1)}, f32[64,256]{1,0:T(8,128)S(1)}, u32[]{:S(2)}, u32[]{:S(2)}) collective-permute-start(f32[64,256]{1,0:T(8,128)S(1)} %add.9), channel_id=1, source_target_pairs={{0,2},{1,3},{2,0},{3,1},{4,6},{5,7},{6,4},{7,5},{8,10},{9,11},{10,... | collective-permute-start | bytes 196616 | tf_op jit(solution)/shard_map/ppermute | solution.py:621
  50.3 5.3 %collective-permute-start.3 = (f32[64,256]{1,0:T(8,128)S(1)}, f32[64,256]{1,0:T(8,128)S(1)}, u32[]{:S(2)}, u32[]{:S(2)}) collective-permute-start(f32[64,256]{1,0:T(8,128)S(1)} %add.10), channel_id=1, source_target_pairs={{0,4},{1,5},{2,6},{3,7},{4,0},{5,1},{6,2},{7,3},{8,12},{9,13},{10,... | collective-permute-start | bytes 196616 | tf_op jit(solution)/shard_map/ppermute | solution.py:621
